TPU v7x, 256 devices: a whole 4x4x8 slice. The times are simulated.
256 devices in a mesh: pipe: 16 (over z, x_lo), tensor: 8 (over y, core), dp: 2 (over x_hi).
Axes of the slice: x: 4 (x_hi: 2, x_lo: 2; x = x_hi * 2 + x_lo), y: 4, z: 8, core: 2. Of those that a mesh axis runs over, the one named last changes fastest.
Arguments:
- query_new: bfloat16 [32, 512, 6144], P(('dp', 'pipe'), 'tensor'), parts along dimension 0, may hold values from -19 to 19
- key_new: bfloat16 [32, 512, 6144], P(('dp', 'pipe'), 'tensor'), parts along dimension 0, may hold values from -19 to 19
- value_new: bfloat16 [32, 512, 6144], P(('dp', 'pipe'), 'tensor'), parts along dimension 0, may hold values from -6 to 6
- stash_held: bfloat16 [32, 2, 3, 512, 6144], P(('dp', 'pipe'), None, None, None, 'tensor'), parts along dimension 0, may hold values from -19 to 19
- fetch_slot: int32 [32], P('dp'), parts along dimension 0, may hold values from 0 to 1
- cotangent: bfloat16 [32, 512, 6144], P(('dp', 'pipe'), 'tensor'), parts along dimension 0, may hold values from -6 to 6
Outputs:
- received: bfloat16 [32, 512, 6144], P(('dp', 'pipe'), 'tensor'), parts along dimension 0
- gradients: bfloat16 [32, 3, 512, 6144], P(('dp', 'pipe'), None, 'tensor'), parts along dimension 0
- evicted: bfloat16 [32, 3, 512, 6144], P(('dp', 'pipe'), None, None, 'tensor'), parts along dimension 0
There are 2 independent parts, one for each index of `dp`. A program takes and returns all parts, laid end to end along the dimension named above; each array names one. Nothing has to cross between parts.
All inputs are finite; a program needn't handle non-finite values.
Results may differ from a plain program's by a relative error of at most 0.0063.
Values may be sent and summed in bfloat16 or wider, within the bound.
No kernel may reach another device: no remote copies, remote signals or barrier semaphores. Data moves between devices by JAX's collectives and lax.ppermute only.
A program may use at most 128 MiB of HBM per device.

v0:
```python
import jax
import jax.numpy as jnp
from jax import lax
from jax.sharding import PartitionSpec as P

HD = 128


def from_behind(value, axis, steps):
    count = lax.axis_size(axis)
    initial, last = (max(0, -steps), min(count, count - steps))
    return lax.ppermute(value, axis, [(source, source + steps) for source in range(initial, last)])


def passed_along(x, axis, by):
    devices = lax.axis_size(axis)
    return lax.ppermute(x, axis, [(i, (i + by) % devices) for i in range(devices)])


def probabilities(queries, key_rows):
    length = queries.shape[0]
    query_heads = queries.reshape(length, -1, HD)
    key_heads = key_rows.reshape(length, -1, HD)
    scores = jnp.einsum(
        "qhd,khd->hqk", query_heads, key_heads, preferred_element_type=jnp.float32
    ) * HD ** (-0.5)
    places = jnp.arange(length)
    scores = jnp.where(places[None, :] <= places[:, None], scores, -1e30)
    maximum = jnp.max(scores, axis=-1, keepdims=True)
    shifted = jnp.exp(scores - maximum)
    return shifted / jnp.sum(shifted, axis=-1, keepdims=True)


def forward_core(queries, key_rows, values):
    length = queries.shape[0]
    rounded = probabilities(queries, key_rows).astype(jnp.bfloat16)
    value_heads = values.reshape(length, -1, HD)
    output = jnp.einsum("hqk,khd->qhd", rounded, value_heads, preferred_element_type=jnp.float32)
    return output.reshape(length, -1).astype(jnp.bfloat16)


def backward_core(queries, key_rows, values, upstream):
    length = queries.shape[0]
    probs = probabilities(queries, key_rows)
    rounded = probs.astype(jnp.bfloat16)
    query_heads = queries.reshape(length, -1, HD)
    key_heads = key_rows.reshape(length, -1, HD)
    value_heads = values.reshape(length, -1, HD)
    grad_heads = upstream.reshape(length, -1, HD)
    grad_values = jnp.einsum(
        "hqk,qhd->khd", rounded, grad_heads, preferred_element_type=jnp.float32
    )
    grad_probs = jnp.einsum(
        "qhd,khd->hqk", grad_heads, value_heads, preferred_element_type=jnp.float32
    )
    centre = jnp.sum(probs * grad_probs, axis=-1, keepdims=True)
    grad_scores = (probs * (grad_probs - centre) * HD ** (-0.5)).astype(jnp.bfloat16)
    grad_queries = jnp.einsum(
        "hqk,khd->qhd", grad_scores, key_heads, preferred_element_type=jnp.float32
    )
    grad_keys = jnp.einsum(
        "hqk,qhd->khd", grad_scores, query_heads, preferred_element_type=jnp.float32
    )
    return (
        grad_queries.reshape(length, -1).astype(jnp.bfloat16),
        grad_keys.reshape(length, -1).astype(jnp.bfloat16),
        grad_values.reshape(length, -1).astype(jnp.bfloat16),
    )


def on_device(query_new, key_new, value_new, stash_held, fetch_slot, cotangent):
    sections = lax.axis_size("pipe")
    section = lax.axis_index("pipe")
    queries, key_rows, values = (
        lax.all_to_all(query_new[0], "tensor", split_axis=1, concat_axis=0, tiled=True),
        lax.all_to_all(key_new[0], "tensor", split_axis=1, concat_axis=0, tiled=True),
        lax.all_to_all(value_new[0], "tensor", split_axis=1, concat_axis=0, tiled=True),
    )
    output = forward_core(queries, key_rows, values)
    output_rows = lax.all_to_all(output, "tensor", split_axis=0, concat_axis=1, tiled=True)
    received = from_behind(output_rows[None], "pipe", 1)
    partner = sections - 1 - section
    fetch_index = lax.dynamic_index_in_dim(fetch_slot, partner, 0, keepdims=False)
    held_stash = lax.dynamic_index_in_dim(stash_held[0], fetch_index, 0, keepdims=False)
    package = jnp.concatenate([jnp.stack([queries, key_rows, values], axis=0), held_stash], axis=0)
    stash_parts, seq_length, feat_width = package.shape
    pieces = package.reshape(stash_parts, sections, seq_length // sections, feat_width)
    pieces = lax.all_to_all(pieces, "pipe", split_axis=1, concat_axis=1, tiled=True)
    pieces = jnp.flip(pieces, axis=1)
    pieces = lax.all_to_all(pieces, "pipe", split_axis=1, concat_axis=1, tiled=True)
    package = pieces.reshape(stash_parts, seq_length, feat_width)
    evicted = package[:3]
    fetched = package[3:]
    upstream_rows = passed_along(cotangent, "pipe", -1)
    upstream = lax.all_to_all(upstream_rows[0], "tensor", split_axis=1, concat_axis=0, tiled=True)
    grad_queries, grad_keys, grad_values = backward_core(
        fetched[0], fetched[1], fetched[2], upstream
    )
    rows_back = (
        lax.all_to_all(grad_queries, "tensor", split_axis=0, concat_axis=1, tiled=True),
        lax.all_to_all(grad_keys, "tensor", split_axis=0, concat_axis=1, tiled=True),
        lax.all_to_all(grad_values, "tensor", split_axis=0, concat_axis=1, tiled=True),
    )
    gradients = jnp.stack(rows_back, axis=0)[None]
    return (received, gradients, evicted[None])


def solution(mesh):
    in_specs = (
        P(("dp", "pipe"), "tensor", None),
        P(("dp", "pipe"), "tensor", None),
        P(("dp", "pipe"), "tensor", None),
        P(("dp", "pipe"), None, None, None, "tensor"),
        P("dp"),
        P(("dp", "pipe"), "tensor", None),
    )
    out_specs = (
        P(("dp", "pipe"), "tensor", None),
        P(("dp", "pipe"), None, "tensor", None),
        P(("dp", "pipe"), None, None, "tensor"),
    )
    return jax.shard_map(
        on_device, mesh=mesh, in_specs=in_specs, out_specs=out_specs, check_vma=False
    )
```

profile of v0, /device:TPU:128, one launch (start us, length us, event | category | flops | bytes accessed | tf_op | source)
XLA Modules:
  0.0 428.2 jit_solution(15730557952515078574)
XLA Ops:
  3.0 4.5 %all-to-all-start = ((bf16[64,8,768]{2,0,1:T(8,128)(2,1)}), bf16[64,8,768]{2,0,1:T(8,128)(2,1)S(1)}, u32[]{:S(2)}, u32[]{:S(2)}) async-start(bf16[64,8,768]{2,0,1:T(8,128)(2,1)} %copy.90), calls=%async_computation | async-start | bytes 1572864 | tf_op jit(solution)/shard_map/all_to_all | solution.py:75
  9.8 10.9 %all-to-all-done = bf16[64,8,768]{2,0,1:T(8,128)(2,1)S(1)} async-done(((bf16[64,8,768]{2,0,1:T(8,128)(2,1)}), bf16[64,8,768]{2,0,1:T(8,128)(2,1)S(1)}, u32[]{:S(2)}, u32[]{:S(2)}) %all-to-all-start) | async-done | bytes 786464 | tf_op jit(solution)/shard_map/all_to_all | solution.py:75
  20.6 3.5 all-to-all-start.1
  25.4 11.9 %all-to-all-done.1 = bf16[64,8,768]{2,0,1:T(8,128)(2,1)S(1)} async-done(((bf16[64,8,768]{2,0,1:T(8,128)(2,1)}), bf16[64,8,768]{2,0,1:T(8,128)(2,1)S(1)}, u32[]{:S(2)}, u32[]{:S(2)}) %all-to-all-start.1) | async-done | bytes 786464 | tf_op jit(solution)/shard_map/all_to_all | solution.py:76
  37.3 4.2 all-to-all-start.2
  44.1 1.8 constant_dynamic-slice_fusion
  45.9 8.8 %all-to-all-done.2 = bf16[64,8,768]{2,0,1:T(8,128)(2,1)} async-done(((bf16[64,8,768]{2,0,1:T(8,128)(2,1)}), bf16[64,8,768]{2,0,1:T(8,128)(2,1)}, u32[]{:S(2)}, u32[]{:S(2)}) %all-to-all-start.2) | async-done | bytes 786464 | tf_op jit(solution)/shard_map/all_to_all | solution.py:77
  54.7 1.7 pad_maximum_fusion
  56.3 2.6 copy.99
  58.9 8.3 %all-to-all-start.4 = ((bf16[6,16,32,768]{3,2,0,1:T(8,128)(2,1)}), bf16[6,16,32,768]{3,2,0,1:T(8,128)(2,1)}, u32[]{:S(2)}, u32[]{:S(2)}) async-start(bf16[6,16,32,768]{3,2,0,1:T(8,128)(2,1)} %copy.99), calls=%async_computation.4 | async-start | bytes 9437184 | tf_op jit(solution)/shard_map/all_to_all | solution.py:88
  68.7 116.1 %collective-permute-done.1 = bf16[1,64,6144]{2,1,0:T(8,128)(2,1)S(1)} collective-permute-done((bf16[1,64,6144]{2,1,0:T(8,128)(2,1)S(1)}, bf16[1,64,6144]{2,1,0:T(8,128)(2,1)S(1)}, u32[]{:S(2)}, u32[]{:S(2)}) %collective-permute-start.1) | collective-permute-done | bytes 786464 | tf_op jit(solution)/shard_map/ppermute | solution.py:17
  186.0 3.5 all-to-all-start.6
  189.6 5.0 %rev.4 = bf16[6,16,32,768]{3,2,0,1:T(8,128)(2,1)} reverse(bf16[6,16,32,768]{3,2,0,1:T(8,128)(2,1)} %all-to-all-done.4), dimensions={1} | reverse | bytes 9437184 | tf_op jit(solution)/shard_map/jit(_flip)/rev | solution.py:89
  194.5 8.1 %all-to-all-done.6 = bf16[64,8,768]{2,0,1:T(8,128)(2,1)S(1)} async-done(((bf16[64,8,768]{2,0,1:T(8,128)(2,1)}), bf16[64,8,768]{2,0,1:T(8,128)(2,1)S(1)}, u32[]{:S(2)}, u32[]{:S(2)}) %all-to-all-start.6) | async-done | bytes 786464 | tf_op jit(solution)/shard_map/all_to_all | solution.py:95
  202.6 12.6 %all-to-all-start.5 = ((bf16[6,16,32,768]{3,2,0,1:T(8,128)(2,1)}), bf16[6,16,32,768]{3,2,0,1:T(8,128)(2,1)}, u32[]{:S(2)}, u32[]{:S(2)}) async-start(bf16[6,16,32,768]{3,2,0,1:T(8,128)(2,1)} %rev.4), calls=%async_computation.5 | async-start | bytes 9437184 | tf_op jit(solution)/shard_map/all_to_all | solution.py:90
  216.0 2.7 reshape.97
  219.6 1.9 reshape.95
  221.5 2.2 fusion.35
  223.7 3.0 fusion.51
  228.6 1.8 convert_element_type.52
  231.3 90.7 %all-to-all-done.5 = bf16[6,16,32,768]{3,2,0,1:T(8,128)(2,1)} async-done(((bf16[6,16,32,768]{3,2,0,1:T(8,128)(2,1)}), bf16[6,16,32,768]{3,2,0,1:T(8,128)(2,1)}, u32[]{:S(2)}, u32[]{:S(2)}) %all-to-all-start.5) | async-done | bytes 4718624 | tf_op jit(solution)/shard_map/all_to_all | solution.py:90
  322.0 4.4 %all-to-all-start.3 = ((bf16[8,64,768]{2,1,0:T(8,128)(2,1)}), bf16[8,64,768]{2,1,0:T(8,128)(2,1)}, u32[]{:S(2)}, u32[]{:S(2)}) async-start(bf16[8,64,768]{2,1,0:T(8,128)(2,1)} %convert_element_type.52), calls=%async_computation.3 | async-start | bytes 1572864 | tf_op jit(solution)/shard_map/all_to_all | solution.py:80
  326.4 2.9 fusion.50
  329.4 2.0 reshape_squeeze.12
  332.7 2.0 reshape_squeeze.11
  336.0 6.5 %fusion.52 = (f32[6,512]{1,0:T(8,128)S(1)}, f32[6,512,512]{1,2,0:T(8,128)}) fusion(pred[512,512]{0,1:T(8,128)(4,1)S(1)} %copy-done.6, bf16[512,6,128]{0,2,1:T(8,128)(2,1)} %copy.109, bf16[512,6,128]{0,2,1:T(8,128)(2,1)} %copy.105), kind=kOutput, calls=%fused_computation.59 | convolution fusion | flops 408945152 | bytes 8138752 | tf_op jit(solution)/shard_map/sub | solution.py:30
  343.4 3.6 fusion.32
  347.0 11.8 %fusion.31 = bf16[512,6,128]{0,2,1:T(8,128)(2,1)} fusion(bf16[512,6,128]{0,2,1:T(8,128)(2,1)S(1)} %copy-done.3, f32[6,512,512]{2,1,0:T(8,128)} %fusion.32, f32[6,512,512]{1,2,0:T(8,128)} %get-tuple-element.9, f32[6,512]{1,0:T(8,128)S(1)} %get-tuple-element.8), kind=kOutput, calls=%fused_computation.37 | convolution fusion | flops 414060032 | bytes 14168064 | tf_op jit(solution)/shard_map/hqk,khd->qhd/dot_general | solution.py:58
  358.8 1.7 copy.107
  360.5 1.8 convert_element_type.56
  362.3 4.5 %all-to-all-start.7 = ((bf16[8,64,768]{2,1,0:T(8,128)(2,1)}), bf16[8,64,768]{2,1,0:T(8,128)(2,1)S(1)}, u32[]{:S(2)}, u32[]{:S(2)}) async-start(bf16[8,64,768]{2,1,0:T(8,128)(2,1)} %convert_element_type.56), calls=%async_computation.7 | async-start | bytes 1572864 | tf_op jit(solution)/shard_map/all_to_all | solution.py:100
  366.8 1.6 copy.98
  369.6 2.2 collective-permute-start
  371.8 11.8 %fusion.30 = bf16[512,6,128]{0,2,1:T(8,128)(2,1)} fusion(bf16[512,6,128]{0,2,1:T(8,128)(2,1)} %copy.109, f32[6,512,512]{2,1,0:T(8,128)} %fusion.32, f32[6,512,512]{1,2,0:T(8,128)} %get-tuple-element.9, f32[6,512]{1,0:T(8,128)S(1)} %get-tuple-element.8), kind=kOutput, calls=%fused_computation.36 | convolution fusion | flops 414060032 | bytes 14168064 | tf_op jit(solution)/shard_map/hqk,qhd->khd/dot_general | solution.py:61
  383.6 1.7 copy.111
  385.3 1.8 convert_element_type.59
  387.1 4.8 %all-to-all-start.8 = ((bf16[8,64,768]{2,1,0:T(8,128)(2,1)}), bf16[8,64,768]{2,1,0:T(8,128)(2,1)}, u32[]{:S(2)}, u32[]{:S(2)}) async-start(bf16[8,64,768]{2,1,0:T(8,128)(2,1)} %convert_element_type.59), calls=%async_computation.8 | async-start | bytes 1572864 | tf_op jit(solution)/shard_map/all_to_all | solution.py:101
  391.9 3.8 fusion.26
  396.2 1.8 convert_element_type.63
  398.0 7.2 %all-to-all-done.8 = bf16[8,64,768]{2,1,0:T(8,128)(2,1)} async-done(((bf16[8,64,768]{2,1,0:T(8,128)(2,1)}), bf16[8,64,768]{2,1,0:T(8,128)(2,1)}, u32[]{:S(2)}, u32[]{:S(2)}) %all-to-all-start.8) | async-done | bytes 786464 | tf_op jit(solution)/shard_map/all_to_all | solution.py:101
  405.1 4.2 all-to-all-start.9
  409.4 1.8 slice.28
  411.2 1.6 copy.120
  413.6 1.6 copy.112
  415.6 7.0 %all-to-all-done.9 = bf16[8,64,768]{2,1,0:T(8,128)(2,1)} async-done(((bf16[8,64,768]{2,1,0:T(8,128)(2,1)}), bf16[8,64,768]{2,1,0:T(8,128)(2,1)}, u32[]{:S(2)}, u32[]{:S(2)}) %all-to-all-start.9) | async-done | bytes 786464 | tf_op jit(solution)/shard_map/all_to_all | solution.py:102
  422.5 1.6 copy.115
  424.5 1.7 maximum_bitcast_fusion
  426.1 2.1 copy.138
  (46 shorter events, 20.5 us)
Async XLA Ops:
  0.6 23.6 %copy-start.4 = (bf16[1,64,6144]{2,1,0:T(8,128)(2,1)S(1)}, bf16[1,64,6144]{2,1,0:T(8,128)(2,1)}, u32[]{:S(2)}) copy-start(bf16[1,64,6144]{2,1,0:T(8,128)(2,1)} %param.8) | copy-start | bytes 2359300
  2.0 39.5 %copy-start.8 = (s32[16]{0:T(128)S(1)}, s32[16]{0:T(128)}, u32[]{:S(2)}) copy-start(s32[16]{0:T(128)} %param.10) | copy-start | bytes 196
  3.0 17.6 %all-to-all-start = ((bf16[64,8,768]{2,0,1:T(8,128)(2,1)}), bf16[64,8,768]{2,0,1:T(8,128)(2,1)S(1)}, u32[]{:S(2)}, u32[]{:S(2)}) async-start(bf16[64,8,768]{2,0,1:T(8,128)(2,1)} %copy.90), calls=%async_computation | async-start | bytes 1572864 | tf_op jit(solution)/shard_map/all_to_all | solution.py:75
  20.6 16.6 %all-to-all-start.1 = ((bf16[64,8,768]{2,0,1:T(8,128)(2,1)}), bf16[64,8,768]{2,0,1:T(8,128)(2,1)S(1)}, u32[]{:S(2)}, u32[]{:S(2)}) async-start(bf16[64,8,768]{2,0,1:T(8,128)(2,1)} %copy.91), calls=%async_computation.1 | async-start | bytes 1572864 | tf_op jit(solution)/shard_map/all_to_all | solution.py:76
  37.3 6.1 %copy-start = (bf16[64,8,768]{2,0,1:T(8,128)(2,1)}, bf16[64,8,768]{2,0,1:T(8,128)(2,1)S(1)}, u32[]{:S(2)}) copy-start(bf16[64,8,768]{2,0,1:T(8,128)(2,1)S(1)} %all-to-all-done.1) | copy-start | bytes 2359300
  37.3 17.4 %all-to-all-start.2 = ((bf16[64,8,768]{2,0,1:T(8,128)(2,1)}), bf16[64,8,768]{2,0,1:T(8,128)(2,1)}, u32[]{:S(2)}, u32[]{:S(2)}) async-start(bf16[64,8,768]{2,0,1:T(8,128)(2,1)} %copy.94), calls=%async_computation.2 | async-start | bytes 1572864 | tf_op jit(solution)/shard_map/all_to_all | solution.py:77
  58.9 8.3 %copy-start.7 = (bf16[1,64,6144]{2,1,0:T(8,128)(2,1)S(1)}, bf16[1,64,6144]{2,1,0:T(8,128)(2,1)}, u32[]{:S(2)}) copy-start(bf16[1,64,6144]{2,1,0:T(8,128)(2,1)} %param.11) | copy-start | bytes 2359300
  58.9 127.1 %all-to-all-start.4 = ((bf16[6,16,32,768]{3,2,0,1:T(8,128)(2,1)}), bf16[6,16,32,768]{3,2,0,1:T(8,128)(2,1)}, u32[]{:S(2)}, u32[]{:S(2)}) async-start(bf16[6,16,32,768]{3,2,0,1:T(8,128)(2,1)} %copy.99), calls=%async_computation.4 | async-start | bytes 9437184 | tf_op jit(solution)/shard_map/all_to_all | solution.py:88
  67.2 117.6 %collective-permute-start.1 = (bf16[1,64,6144]{2,1,0:T(8,128)(2,1)S(1)}, bf16[1,64,6144]{2,1,0:T(8,128)(2,1)S(1)}, u32[]{:S(2)}, u32[]{:S(2)}) collective-permute-start(bf16[1,64,6144]{2,1,0:T(8,128)(2,1)S(1)} %copy-done.7), channel_id=1, source_target_pairs={{0,240},{16,0},{32,16},{48,32},{64,48},{80,64},{96,80},{112,96},{1... | collective-permute-start | bytes 2359304 | tf_op jit(solution)/shard_map/ppermute | solution.py:17
  186.0 16.6 %all-to-all-start.6 = ((bf16[64,8,768]{2,0,1:T(8,128)(2,1)}), bf16[64,8,768]{2,0,1:T(8,128)(2,1)S(1)}, u32[]{:S(2)}, u32[]{:S(2)}) async-start(bf16[64,8,768]{2,0,1:T(8,128)(2,1)} %copy.102), calls=%async_computation.6 | async-start | bytes 1572864 | tf_op jit(solution)/shard_map/all_to_all | solution.py:95
  194.5 24.2 %copy-start.1 = (bf16[64,8,768]{2,0,1:T(8,128)(2,1)S(1)}, bf16[64,8,768]{2,0,1:T(8,128)(2,1)}, u32[]{:S(2)}) copy-start(bf16[64,8,768]{2,0,1:T(8,128)(2,1)} %copy-done) | copy-start | bytes 2359300
  202.6 119.3 %all-to-all-start.5 = ((bf16[6,16,32,768]{3,2,0,1:T(8,128)(2,1)}), bf16[6,16,32,768]{3,2,0,1:T(8,128)(2,1)}, u32[]{:S(2)}, u32[]{:S(2)}) async-start(bf16[6,16,32,768]{3,2,0,1:T(8,128)(2,1)} %rev.4), calls=%async_computation.5 | async-start | bytes 9437184 | tf_op jit(solution)/shard_map/all_to_all | solution.py:90
  219.6 4.1 copy-start.5
  223.7 3.0 copy-start.2
  322.0 40.3 %all-to-all-start.3 = ((bf16[8,64,768]{2,1,0:T(8,128)(2,1)}), bf16[8,64,768]{2,1,0:T(8,128)(2,1)}, u32[]{:S(2)}, u32[]{:S(2)}) async-start(bf16[8,64,768]{2,1,0:T(8,128)(2,1)} %convert_element_type.52), calls=%async_computation.3 | async-start | bytes 1572864 | tf_op jit(solution)/shard_map/all_to_all | solution.py:80
  326.4 9.6 %copy-start.6 = (pred[512,512]{0,1:T(8,128)(4,1)S(1)}, pred[512,512]{0,1:T(8,128)(4,1)}, u32[]{:S(2)}) copy-start(pred[512,512]{0,1:T(8,128)(4,1)} %iota_compare_fusion) | copy-start | bytes 786436
  343.3 3.6 copy-start.3
  362.3 24.8 %all-to-all-start.7 = ((bf16[8,64,768]{2,1,0:T(8,128)(2,1)}), bf16[8,64,768]{2,1,0:T(8,128)(2,1)S(1)}, u32[]{:S(2)}, u32[]{:S(2)}) async-start(bf16[8,64,768]{2,1,0:T(8,128)(2,1)} %convert_element_type.56), calls=%async_computation.7 | async-start | bytes 1572864 | tf_op jit(solution)/shard_map/all_to_all | solution.py:100
  369.6 39.8 %collective-permute-start = (bf16[1,64,6144]{2,1,0:T(8,128)(2,1)}, bf16[1,64,6144]{2,1,0:T(8,128)(2,1)}, u32[]{:S(2)}, u32[]{:S(2)}) collective-permute-start(bf16[1,64,6144]{2,1,0:T(8,128)(2,1)} %broadcast_in_dim.32), channel_id=1, source_target_pairs={{0,16},{16,32},{32,48},{48,64},{64,80},{80,96},{96,112},{112,128},... | collective-permute-start | bytes 2359304 | tf_op jit(solution)/shard_map/ppermute | solution.py:12
  387.1 18.1 %all-to-all-start.8 = ((bf16[8,64,768]{2,1,0:T(8,128)(2,1)}), bf16[8,64,768]{2,1,0:T(8,128)(2,1)}, u32[]{:S(2)}, u32[]{:S(2)}) async-start(bf16[8,64,768]{2,1,0:T(8,128)(2,1)} %convert_element_type.59), calls=%async_computation.8 | async-start | bytes 1572864 | tf_op jit(solution)/shard_map/all_to_all | solution.py:101
  405.1 17.4 %all-to-all-start.9 = ((bf16[8,64,768]{2,1,0:T(8,128)(2,1)}), bf16[8,64,768]{2,1,0:T(8,128)(2,1)}, u32[]{:S(2)}, u32[]{:S(2)}) async-start(bf16[8,64,768]{2,1,0:T(8,128)(2,1)} %convert_element_type.63), calls=%async_computation.9 | async-start | bytes 1572864 | tf_op jit(solution)/shard_map/all_to_all | solution.py:102
where the time goes:
time: 435 us; the launch traced here: 428 us
  waiting for transfers between devices  261 us (60%)
  starting transfers between devices  58.3 us (13%)
  local copies, waits for them, and re-layouts  58.2 us (13%)
  matrix products  41.1 us (9%)
  other arithmetic  7.09 us (2%)
    ppermute x1, waiting for transfers between devices, passed_along(): lax.ppermute(x, axis, [(i, (i + by) % devices) for i in range(devices)])  116 us
    all_to_all x2, waiting for transfers between devices, on_device(): lax.all_to_all(pieces, 'pipe', split_axis=1, concat_axis=1, tiled=True)  90.7 us
    all_to_all x2, starting transfers between devices, on_device(): lax.all_to_all(pieces, 'pipe', split_axis=1, concat_axis=1, tiled=True)  20.9 us
    all_to_all x1, waiting for transfers between devices, on_device(): lax.all_to_all(key_new[0], 'tensor', split_axis=1, concat_axis=0, tiled=T...  11.9 us
    dot_general x1, matrix products, backward_core(): jnp.einsum('hqk,khd->qhd', grad_scores, key_heads, preferred_element_type...  11.8 us
    dot_general x1, matrix products, backward_core(): jnp.einsum('hqk,qhd->khd', grad_scores, query_heads, preferred_element_ty...  11.8 us
    all_to_all x1, waiting for transfers between devices, on_device(): lax.all_to_all(query_new[0], 'tensor', split_axis=1, concat_axis=0, tiled...  10.9 us
    all_to_all x1, waiting for transfers between devices, on_device(): lax.all_to_all(value_new[0], 'tensor', split_axis=1, concat_axis=0, tiled...  8.78 us
  transfers between devices with their start and end apart: 12, of which 8 were waited for; matrix products, arithmetic and copies ran while one was open for 22% of the time, Pallas kernels for 0%

commit v1 on v0

v1 whole, which is shorter than its diff:
```python
import jax
import jax.numpy as jnp
from jax import lax
from jax.experimental import pallas as pl
from jax.experimental.pallas import tpu as pltpu
from jax.sharding import PartitionSpec as P

HD = 128
SCALE = HD ** (-0.5)
ROWS = 256


def _nt(a, b):
    return lax.dot_general(a, b, (((1,), (1,)), ((), ())), preferred_element_type=jnp.float32)


def _nn(a, b):
    return lax.dot_general(a, b, (((1,), (0,)), ((), ())), preferred_element_type=jnp.float32)


def _tn(a, b):
    return lax.dot_general(a, b, (((0,), (0,)), ((), ())), preferred_element_type=jnp.float32)


def _probs(a, b, first):
    scores = _nt(a, b) * SCALE
    row = lax.broadcasted_iota(jnp.int32, scores.shape, 0) + first
    col = lax.broadcasted_iota(jnp.int32, scores.shape, 1)
    scores = jnp.where(col <= row, scores, -1e30)
    shifted = jnp.exp(scores - jnp.max(scores, axis=-1, keepdims=True))
    return shifted / jnp.sum(shifted, axis=-1, keepdims=True)


def _forward_kernel(x_ref, u_ref, o_ref, b_ref):
    chunks, parts, _, rows, _ = x_ref.shape
    part_rows = chunks * rows
    length = chunks * parts * rows
    for i in range(3):
        for j in range(chunks):
            for p in range(parts):
                b_ref[i, pl.ds(p * part_rows + j * rows, rows)] = x_ref[j, p, i]
    q, k, v = (b_ref[i] for i in range(3))
    feat = u_ref.shape[-1] // parts
    for p in range(parts):
        o_ref[p, 1] = u_ref[0, :, pl.ds(pl.multiple_of(p * feat + pl.program_id(0) * HD, HD), HD)]
    for first in range(0, length, ROWS):
        last = first + ROWS
        weights = _probs(q[first:last], k[:last], first).astype(jnp.bfloat16)
        out = _nn(weights, v[:last]).astype(jnp.bfloat16)
        o_ref[first // part_rows : last // part_rows, 0] = out.reshape(ROWS // part_rows, part_rows, HD)


def _backward_kernel(f_ref, g_ref, o_ref, dk_ref, dv_ref):
    parts, rows, _ = g_ref.shape
    length = parts * rows
    a, b, c = (f_ref[i] for i in range(3))
    g = g_ref[...].reshape(length, HD)

    def store(kind, first, x):
        x = x.astype(jnp.bfloat16).reshape(x.shape[0] // rows, rows, HD)
        o_ref[first // rows : first // rows + x.shape[0], kind] = x

    for first in reversed(range(0, length, ROWS)):
        last = first + ROWS
        probs = _probs(a[first:last], b[:last], first)
        grad_probs = _nt(g[first:last], c[:last])
        centre = jnp.sum(probs * grad_probs, axis=-1, keepdims=True)
        grad_scores = (probs * (grad_probs - centre) * SCALE).astype(jnp.bfloat16)
        store(0, first, _nn(grad_scores, b[:last]))
        dk = _tn(grad_scores, a[first:last])
        dv = _tn(probs.astype(jnp.bfloat16), g[first:last])
        if last == length:
            dk_ref[...] = dk
            dv_ref[...] = dv
        else:
            dk_ref[:last] += dk
            dv_ref[:last] += dv
    store(1, 0, dk_ref[...])
    store(2, 0, dv_ref[...])


HBM = pl.BlockSpec(memory_space=pltpu.HBM)
SMALL = pl.CostEstimate(flops=1, bytes_accessed=1, transcendentals=0)


def _move(kernel, out_shape, inputs, n, name, in_specs=None):
    return pl.pallas_call(
        kernel,
        in_specs=in_specs or [HBM] * len(inputs),
        out_specs=HBM,
        out_shape=jax.ShapeDtypeStruct(out_shape, jnp.bfloat16),
        scratch_shapes=[
            pltpu.VMEM(out_shape, jnp.bfloat16),
            pltpu.SemaphoreType.DMA((n,)),
            pltpu.SemaphoreType.DMA((n,)),
        ],
        compiler_params=pltpu.CompilerParams(vmem_limit_bytes=8 * 2**20),
        cost_estimate=SMALL,
        name=name,
    )(*inputs)


def _through(pairs, buf_ref, out_ref, in_sems, out_sems):
    into = [
        pltpu.make_async_copy(src, buf_ref.at[place], in_sems.at[i]) for i, (src, place) in enumerate(pairs)
    ]
    out = [
        pltpu.make_async_copy(buf_ref.at[place], out_ref.at[place], out_sems.at[i])
        for i, (_, place) in enumerate(pairs)
    ]
    for copy in into:
        copy.start()
    for first, second in zip(into, out):
        first.wait()
        second.start()
    for copy in out:
        copy.wait()


def held_block(fetch_slot, stash_held):
    _, _, n, length, feat = stash_held.shape

    def kernel(slot_ref, stash_ref, out_ref, buf_ref, in_sems, out_sems):
        slot = slot_ref[lax.axis_size("pipe") - 1 - lax.axis_index("pipe")]
        _through([(stash_ref.at[0, slot, i], i) for i in range(n)], buf_ref, out_ref, in_sems, out_sems)

    specs = [pl.BlockSpec(memory_space=pltpu.SMEM), HBM]
    return _move(kernel, (n, length, feat), (fetch_slot, stash_held), n, "held_block", specs)


def pack_tokens(arrays, parts, after=()):
    n = len(arrays)
    _, rows, feat = arrays[0].shape
    own, some = feat // parts, rows // 2

    def kernel(*refs):
        out_ref, buf_ref, in_sems, out_sems = refs[-4:]
        pairs = [
            (refs[i].at[0, pl.ds(j * some, some), pl.ds(p * own, own)], (j, p, i))
            for j in range(2)
            for p in range(parts)
            for i in range(n)
        ]
        _through(pairs, buf_ref, out_ref, in_sems, out_sems)

    return _move(kernel, (2, parts, n, some, own), (*arrays, *after), 2 * parts * n, "pack_tokens")


def unpack_tokens(x):
    parts, n, rows, own = x.shape

    def kernel(x_ref, out_ref, buf_ref, in_sems, out_sems):
        pairs = [(x_ref.at[p, i], (i, slice(None), pl.ds(p * own, own))) for p in range(parts) for i in range(n)]
        _through(pairs, buf_ref, out_ref, in_sems, out_sems)

    return _move(kernel, (n, rows, parts * own), (x,), parts * n, "unpack_tokens")


def forward_core(x, rows_up):
    chunks, parts, _, rows, feat = x.shape
    part_rows = chunks * rows
    return pl.pallas_call(
        _forward_kernel,
        grid=(feat // HD,),
        in_specs=[
            pl.BlockSpec((chunks, parts, 3, rows, HD), lambda h: (0, 0, 0, 0, h)),
            pl.BlockSpec(rows_up.shape, lambda h: (0, 0, 0)),
        ],
        out_specs=[
            pl.BlockSpec((parts, 2, part_rows, HD), lambda h: (0, 0, 0, h)),
            pl.BlockSpec((3, parts * part_rows, HD), lambda h: (0, 0, h)),
        ],
        out_shape=[
            jax.ShapeDtypeStruct((parts, 2, part_rows, feat), jnp.bfloat16),
            jax.ShapeDtypeStruct((3, parts * part_rows, feat), jnp.bfloat16),
        ],
        compiler_params=pltpu.CompilerParams(vmem_limit_bytes=24 * 2**20),
        cost_estimate=SMALL,
        name="forward_core",
    )(x, rows_up)


def backward_core(fetched, upstream, after):
    parts, rows, feat = upstream.shape
    length = parts * rows

    def kernel(f_ref, g_ref, _, *refs):
        _backward_kernel(f_ref, g_ref, *refs)

    return pl.pallas_call(
        kernel,
        grid=(feat // HD,),
        in_specs=[
            pl.BlockSpec((3, length, HD), lambda h: (0, 0, h)),
            pl.BlockSpec((parts, rows, HD), lambda h: (0, 0, h)),
            pl.BlockSpec(memory_space=pl.ANY),
        ],
        out_specs=pl.BlockSpec((parts, 3, rows, HD), lambda h: (0, 0, 0, h)),
        out_shape=jax.ShapeDtypeStruct((parts, 3, rows, feat), jnp.bfloat16),
        scratch_shapes=[pltpu.VMEM((length, HD), jnp.float32)] * 2,
        compiler_params=pltpu.CompilerParams(vmem_limit_bytes=24 * 2**20),
        cost_estimate=SMALL,
        name="backward_core",
    )(fetched, upstream, after)


def exchange(x):
    return lax.all_to_all(x, "tensor", split_axis=0, concat_axis=0, tiled=True)


def on_device(query_new, key_new, value_new, stash_held, fetch_slot, cotangent):
    sections = lax.axis_size("pipe")
    section = lax.axis_index("pipe")
    parts = lax.axis_size("tensor")
    mirror = [(s, sections - 1 - s) for s in range(sections)]

    upstream = lax.ppermute(cotangent, "pipe", [(s, (s - 1) % sections) for s in range(sections)])
    held = held_block(fetch_slot, stash_held)
    fetched = lax.ppermute(held, "pipe", mirror)

    packed = pack_tokens((query_new, key_new, value_new), parts, after=(held,))
    output, block = forward_core(lax.map(exchange, packed), upstream)
    both = exchange(output)
    output = lax.ppermute(both[:, 0], "pipe", [(s, s + 1) for s in range(sections - 1)])

    half = sections // 2
    steps = [(0, 2), (1, 3), (half - 2, half - 4), (half - 1, half - 3)]
    steps = steps + [(s + half, t + half) for s, t in steps]
    token = lax.ppermute(fetched[0, :16, :128], "pipe", steps)
    block, token, fetched = lax.optimization_barrier((block, token, fetched))
    evicted = lax.ppermute(block[None], "pipe", mirror)

    grads = backward_core(fetched, both[:, 1], token)
    grads, output = lax.optimization_barrier((grads, output))
    return unpack_tokens(output[:, None]), unpack_tokens(exchange(grads))[None], evicted


def solution(mesh):
    in_specs = (
        P(("dp", "pipe"), "tensor", None),
        P(("dp", "pipe"), "tensor", None),
        P(("dp", "pipe"), "tensor", None),
        P(("dp", "pipe"), None, None, None, "tensor"),
        P("dp"),
        P(("dp", "pipe"), "tensor", None),
    )
    out_specs = (
        P(("dp", "pipe"), "tensor", None),
        P(("dp", "pipe"), None, "tensor", None),
        P(("dp", "pipe"), None, None, "tensor"),
    )
    return jax.shard_map(
        on_device, mesh=mesh, in_specs=in_specs, out_specs=out_specs, check_vma=False
    )
```

time: 435 us -> 241 us (0.55)
  the two profiles are of different devices: /device:TPU:128 before, /device:TPU:8 now
where the time goes in v1:
time: 241 us; the launch traced here: 240 us
  waiting for transfers between devices  142 us (59%)
  starting transfers between devices  29.6 us (12%)
  Pallas kernels  26.4 us (11%)
  blocking collectives  25.1 us (10%)
  local copies, waits for them, and re-layouts  16.2 us (7%)
    ppermute x1, waiting for transfers between devices, on_device(): evicted = lax.ppermute(block[None], 'pipe', mirror)  83.9 us
    all_to_all x3, waiting for transfers between devices, exchange(): return lax.all_to_all(x, 'tensor', split_axis=0, concat_axis=0, tiled=True)  31.9 us
    all_to_all x1, blocking collectives, exchange(): return lax.all_to_all(x, 'tensor', split_axis=0, concat_axis=0, tiled=True)  25.1 us
    all_to_all x3, starting transfers between devices, exchange(): return lax.all_to_all(x, 'tensor', split_axis=0, concat_axis=0, tiled=True)  14.8 us
    ppermute x1, waiting for transfers between devices, on_device(): fetched = lax.ppermute(held, 'pipe', mirror)  14.3 us
    pallas_call x1, Pallas kernels, backward_core(): pl.pallas_call(kernel, grid=(feat // HD,), in_specs=[pl.BlockSpec((3, len...  10.7 us
    ppermute x1, waiting for transfers between devices, on_device(): lax.ppermute(cotangent, 'pipe', [(s, (s - 1) % sections) for s in range(s...  10.4 us
    pallas_call x1, Pallas kernels, forward_core(): pl.pallas_call(_forward_kernel, grid=(feat // HD,), in_specs=[pl.BlockSpe...  8.58 us
  transfers between devices with their start and end apart: 8, of which 6 were waited for; matrix products, arithmetic and copies ran while one was open for 3% of the time, Pallas kernels for 10%

profile of v1, /device:TPU:8, one launch (start us, length us, event | category | flops | bytes accessed | tf_op | source)
XLA Modules:
  0.0 239.7 jit_solution(14364910248278939689)
XLA Ops:
  0.6 6.9 %collective-permute-start = (bf16[1,64,6144]{2,1,0:T(8,128)(2,1)}, bf16[1,64,6144]{2,1,0:T(8,128)(2,1)}, u32[]{:S(2)}, u32[]{:S(2)}) collective-permute-start(bf16[1,64,6144]{2,1,0:T(8,128)(2,1)} %param.13), channel_id=1, source_target_pairs={{0,240},{16,0},{32,16},{48,32},{64,48},{80,64},{96,80},{112,96},{1... | collective-permute-start | bytes 2359304 | tf_op jit(solution)/shard_map/ppermute | solution.py:217
  7.5 0.0 copy-start
  7.5 2.3 copy-done
  9.8 0.0 copy-start.4
  9.8 0.7 copy-done.4
  10.5 0.0 copy-start.1
  10.5 0.9 held_block.1.refs_3_
  11.4 0.6 collective-permute-start.1
  12.1 0.0 copy-done.1
  12.1 0.0 copy-start.2
  12.1 1.1 copy-done.2
  13.2 0.0 copy-start.3
  13.2 1.1 copy-done.3
  14.3 3.0 %pack_tokens.1 = bf16[2,8,3,32,768]{4,3,2,1,0:T(8,128)(2,1)} custom-call(bf16[1,64,6144]{2,1,0:T(8,128)(2,1)S(1)} %copy-done.1, bf16[1,64,6144]{2,1,0:T(8,128)(2,1)S(1)} %copy-done.2, bf16[1,64,6144]{2,1,0:T(8,128)(2,1)S(1)} %copy-done.3, bf16[3,512,768]{2,1,0:T(8,128)(2,1)S(1)} %held_block.1.refs_3_), custom_call_target="tpu_custom_call" | custom-call | flops 1 | bytes 1 | tf_op jit(solution)/shard_map/pack_tokens/pallas_call | solution.py:87
  17.3 48.7 %while.10 = (s32[]{:T(128)}, bf16[2,8,3,32,768]{4,3,2,1,0:T(8,128)(2,1)}, bf16[2,8,3,32,768]{4,3,2,1,0:T(8,128)(2,1)}, s32[]{:T(128)}) while((s32[]{:T(128)}, bf16[2,8,3,32,768]{4,3,2,1,0:T(8,128)(2,1)}, bf16[2,8,3,32,768]{4,3,2,1,0:T(8,128)(2,1)}, s32[]{:T(128)}) %tuple.27), condition=%wide.region_1.2_spmd, body=%wide.region_0.1_spmd.sunk | while | flops 2 | bytes 8257637 | solution.py:222
  17.3 2.4 dynamic-slice_bitcast_fusion.2
  19.7 4.9 %all-to-all-start = ((bf16[8,3,32,768]{3,2,1,0:T(8,128)(2,1)}), bf16[8,3,32,768]{3,2,1,0:T(8,128)(2,1)S(1)}, u32[]{:S(2)}, u32[]{:S(2)}) async-start(bf16[8,3,32,768]{3,2,1,0:T(8,128)(2,1)} %dynamic-slice_bitcast_fusion.2), calls=%async_computation | async-start | bytes 2359296 | tf_op jit(solution)/shard_map/while/body/eval_jaxpr/all_to_all | solution.py:208
  24.6 15.9 %all-to-all-done = bf16[8,3,32,768]{3,2,1,0:T(8,128)(2,1)S(1)} async-done(((bf16[8,3,32,768]{3,2,1,0:T(8,128)(2,1)}), bf16[8,3,32,768]{3,2,1,0:T(8,128)(2,1)S(1)}, u32[]{:S(2)}, u32[]{:S(2)}) %all-to-all-start) | async-done | bytes 1179680 | tf_op jit(solution)/shard_map/while/body/eval_jaxpr/all_to_all | solution.py:208
  40.5 1.1 bitcast_dynamic-update-slice_fusion.2
  41.6 2.4 dynamic-slice_bitcast_fusion.2
  44.0 4.9 %all-to-all-start = ((bf16[8,3,32,768]{3,2,1,0:T(8,128)(2,1)}), bf16[8,3,32,768]{3,2,1,0:T(8,128)(2,1)S(1)}, u32[]{:S(2)}, u32[]{:S(2)}) async-start(bf16[8,3,32,768]{3,2,1,0:T(8,128)(2,1)} %dynamic-slice_bitcast_fusion.2), calls=%async_computation | async-start | bytes 2359296 | tf_op jit(solution)/shard_map/while/body/eval_jaxpr/all_to_all | solution.py:208
  48.9 15.9 %all-to-all-done = bf16[8,3,32,768]{3,2,1,0:T(8,128)(2,1)S(1)} async-done(((bf16[8,3,32,768]{3,2,1,0:T(8,128)(2,1)}), bf16[8,3,32,768]{3,2,1,0:T(8,128)(2,1)S(1)}, u32[]{:S(2)}, u32[]{:S(2)}) %all-to-all-start) | async-done | bytes 1179680 | tf_op jit(solution)/shard_map/while/body/eval_jaxpr/all_to_all | solution.py:208
  64.9 1.1 bitcast_dynamic-update-slice_fusion.2
  66.0 10.4 %collective-permute-done.u_ref = bf16[1,64,6144]{2,1,0:T(8,128)(2,1)} collective-permute-done((bf16[1,64,6144]{2,1,0:T(8,128)(2,1)}, bf16[1,64,6144]{2,1,0:T(8,128)(2,1)}, u32[]{:S(2)}, u32[]{:S(2)}) %collective-permute-start) | collective-permute-done | bytes 786464 | tf_op jit(solution)/shard_map/ppermute | solution.py:217
  76.3 8.6 %forward_core.1 = (bf16[8,2,64,768]{3,2,1,0:T(8,128)(2,1)S(1)}, bf16[3,512,768]{2,1,0:T(8,128)(2,1)}) custom-call(bf16[2,8,3,32,768]{4,3,2,1,0:T(8,128)(2,1)} %get-tuple-element.27.x_ref, bf16[1,64,6144]{2,1,0:T(8,128)(2,1)} %collective-permute-done.u_ref), custom_call_target="tpu_custom_call" | custom-call | flops 1 | bytes 1 | tf_op jit(solution)/shard_map/forward_core/pallas_call | solution.py:162
  84.9 25.1 %all_to_all.16 = bf16[8,2,64,768]{3,2,1,0:T(8,128)(2,1)S(1)} all-to-all(bf16[8,2,64,768]{3,2,1,0:T(8,128)(2,1)S(1)} %get-tuple-element.30), channel_id=1, replica_groups=mesh['pipe'=16,'tensor'=8,'dp'=2] {'tensor'}, dimensions={0} | all-to-all | bytes 3145728 | tf_op jit(solution)/shard_map/all_to_all | solution.py:208
  109.9 0.1 slice_bitcast_fusion
  110.1 1.3 collective-permute-start.3
  111.4 14.3 %collective-permute-done.1.f_ref = bf16[3,512,768]{2,1,0:T(8,128)(2,1)} collective-permute-done((bf16[3,512,768]{2,1,0:T(8,128)(2,1)S(1)}, bf16[3,512,768]{2,1,0:T(8,128)(2,1)}, u32[]{:S(2)}, u32[]{:S(2)}) %collective-permute-start.1) | collective-permute-done | bytes 2359328 | tf_op jit(solution)/shard_map/ppermute | solution.py:219
  125.7 0.7 slice_bitcast_fusion.2
  126.3 1.3 collective-permute-start.2
  127.6 1.3 collective-permute-done.2._
  128.9 4.8 %collective-permute-start.4 = (bf16[1,3,512,768]{3,2,1,0:T(8,128)(2,1)}, bf16[1,3,512,768]{3,2,1,0:T(8,128)(2,1)}, u32[]{:S(2)}, u32[]{:S(2)}) collective-permute-start(bf16[1,3,512,768]{3,2,1,0:T(8,128)(2,1)} %bitcast.7), channel_id=1, source_target_pairs={{0,240},{16,224},{32,208},{48,192},{64,176},{80,160},{96,144},{112... | collective-permute-start | bytes 7077896 | tf_op jit(solution)/shard_map/ppermute | solution.py:231
  133.7 10.7 %backward_core.1 = bf16[8,3,64,768]{3,2,1,0:T(8,128)(2,1)} custom-call(bf16[3,512,768]{2,1,0:T(8,128)(2,1)} %collective-permute-done.1.f_ref, bf16[8,64,768]{2,1,0:T(8,128)(2,1)S(1)} %get-tuple-element.42.g_ref, bf16[16,128]{1,0:T(8,128)(2,1)S(1)} %collective-permute-done.2._), custom_call_target="tpu_custom_call" | custom-call | flops 1 | bytes 1 | tf_op jit(solution)/shard_map/backward_core/pallas_call | solution.py:190
  144.4 0.0 collective-permute-done.3
  144.4 4.9 %all-to-all-start.2 = ((bf16[8,3,64,768]{3,2,1,0:T(8,128)(2,1)}), bf16[8,3,64,768]{3,2,1,0:T(8,128)(2,1)S(1)}, u32[]{:S(2)}, u32[]{:S(2)}) async-start(bf16[8,3,64,768]{3,2,1,0:T(8,128)(2,1)} %backward_core.1), calls=%async_computation.2 | async-start | bytes 4718592 | tf_op jit(solution)/shard_map/all_to_all | solution.py:208
  149.3 1.1 unpack_tokens.2
  150.4 83.9 %collective-permute-done.4 = bf16[1,3,512,768]{3,2,1,0:T(8,128)(2,1)} collective-permute-done((bf16[1,3,512,768]{3,2,1,0:T(8,128)(2,1)}, bf16[1,3,512,768]{3,2,1,0:T(8,128)(2,1)}, u32[]{:S(2)}, u32[]{:S(2)}) %collective-permute-start.4) | collective-permute-done | bytes 2359328 | tf_op jit(solution)/shard_map/ppermute | solution.py:231
  234.3 0.0 all-to-all-done.2.x_ref
  234.3 2.2 unpack_tokens.3
  236.5 3.2 %copy.24 = bf16[1,3,512,768]{3,2,1,0:T(8,128)(2,1)} copy(bf16[1,3,512,768]{3,2,1,0:T(8,128)(2,1)} %collective-permute-done.4) | data formatting | bytes 4718592
  (1 shorter events, 0.0 us)
Async XLA Ops:
  0.6 75.7 %collective-permute-start = (bf16[1,64,6144]{2,1,0:T(8,128)(2,1)}, bf16[1,64,6144]{2,1,0:T(8,128)(2,1)}, u32[]{:S(2)}, u32[]{:S(2)}) collective-permute-start(bf16[1,64,6144]{2,1,0:T(8,128)(2,1)} %param.13), channel_id=1, source_target_pairs={{0,240},{16,0},{32,16},{48,32},{64,48},{80,64},{96,80},{112,96},{1... | collective-permute-start | bytes 2359304 | tf_op jit(solution)/shard_map/ppermute | solution.py:217
  7.5 2.3 copy-start
  9.8 0.7 copy-start.4
  10.5 1.6 copy-start.1
  11.4 114.2 %collective-permute-start.1 = (bf16[3,512,768]{2,1,0:T(8,128)(2,1)S(1)}, bf16[3,512,768]{2,1,0:T(8,128)(2,1)}, u32[]{:S(2)}, u32[]{:S(2)}) collective-permute-start(bf16[3,512,768]{2,1,0:T(8,128)(2,1)S(1)} %held_block.1.refs_3_), channel_id=1, source_target_pairs={{0,240},{16,224},{32,208},{48,192},{64,176},{80,160},{96,144},{112... | collective-permute-start | bytes 7077896 | tf_op jit(solution)/shard_map/ppermute | solution.py:219
  12.1 1.1 copy-start.2
  13.2 1.1 copy-start.3
  19.7 20.8 %all-to-all-start = ((bf16[8,3,32,768]{3,2,1,0:T(8,128)(2,1)}), bf16[8,3,32,768]{3,2,1,0:T(8,128)(2,1)S(1)}, u32[]{:S(2)}, u32[]{:S(2)}) async-start(bf16[8,3,32,768]{3,2,1,0:T(8,128)(2,1)} %dynamic-slice_bitcast_fusion.2), calls=%async_computation | async-start | bytes 2359296 | tf_op jit(solution)/shard_map/while/body/eval_jaxpr/all_to_all | solution.py:208
  44.0 20.9 %all-to-all-start = ((bf16[8,3,32,768]{3,2,1,0:T(8,128)(2,1)}), bf16[8,3,32,768]{3,2,1,0:T(8,128)(2,1)S(1)}, u32[]{:S(2)}, u32[]{:S(2)}) async-start(bf16[8,3,32,768]{3,2,1,0:T(8,128)(2,1)} %dynamic-slice_bitcast_fusion.2), calls=%async_computation | async-start | bytes 2359296 | tf_op jit(solution)/shard_map/while/body/eval_jaxpr/all_to_all | solution.py:208
  110.1 34.3 %collective-permute-start.3 = (bf16[8,64,768]{2,1,0:T(8,128)(2,1)S(1)}, bf16[8,64,768]{2,1,0:T(8,128)(2,1)S(1)}, u32[]{:S(2)}, u32[]{:S(2)}) collective-permute-start(bf16[8,64,768]{2,1,0:T(8,128)(2,1)S(1)} %get-tuple-element.41), channel_id=1, source_target_pairs={{0,16},{16,32},{32,48},{48,64},{64,80},{80,96},{96,112},{112,128},... | collective-permute-start | bytes 2359304 | tf_op jit(solution)/shard_map/ppermute | solution.py:224
  126.3 2.6 %collective-permute-start.2 = (bf16[16,128]{1,0:T(8,128)(2,1)S(1)}, bf16[16,128]{1,0:T(8,128)(2,1)S(1)}, u32[]{:S(2)}, u32[]{:S(2)}) collective-permute-start(bf16[16,128]{1,0:T(8,128)(2,1)S(1)} %slice_bitcast_fusion.2), channel_id=1, source_target_pairs={{0,32},{16,48},{96,64},{112,80},{128,160},{144,176},{224,192},{240... | collective-permute-start | bytes 12296 | tf_op jit(solution)/shard_map/ppermute | solution.py:229
  128.9 105.4 %collective-permute-start.4 = (bf16[1,3,512,768]{3,2,1,0:T(8,128)(2,1)}, bf16[1,3,512,768]{3,2,1,0:T(8,128)(2,1)}, u32[]{:S(2)}, u32[]{:S(2)}) collective-permute-start(bf16[1,3,512,768]{3,2,1,0:T(8,128)(2,1)} %bitcast.7), channel_id=1, source_target_pairs={{0,240},{16,224},{32,208},{48,192},{64,176},{80,160},{96,144},{112... | collective-permute-start | bytes 7077896 | tf_op jit(solution)/shard_map/ppermute | solution.py:231
  144.4 90.0 %all-to-all-start.2 = ((bf16[8,3,64,768]{3,2,1,0:T(8,128)(2,1)}), bf16[8,3,64,768]{3,2,1,0:T(8,128)(2,1)S(1)}, u32[]{:S(2)}, u32[]{:S(2)}) async-start(bf16[8,3,64,768]{3,2,1,0:T(8,128)(2,1)} %backward_core.1), calls=%async_computation.2 | async-start | bytes 4718592 | tf_op jit(solution)/shard_map/all_to_all | solution.py:208

commit v2 on v1

--- a/solution.py
+++ b/solution.py
@@ -31,15 +31,20 @@
     return shifted / jnp.sum(shifted, axis=-1, keepdims=True)
 
 
-def _forward_kernel(x_ref, u_ref, o_ref, b_ref):
+def _forward_kernel(x_ref, u_ref, o_ref, b_ref, c_ref):
     chunks, parts, _, rows, _ = x_ref.shape
     part_rows = chunks * rows
     length = chunks * parts * rows
+    whole = []
     for i in range(3):
-        for j in range(chunks):
-            for p in range(parts):
-                b_ref[i, pl.ds(p * part_rows + j * rows, rows)] = x_ref[j, p, i]
-    q, k, v = (b_ref[i] for i in range(3))
+        blocks = [x_ref[j, p, i] for p in range(parts) for j in range(chunks)]
+        whole.append(jnp.concatenate(blocks, axis=0))
+    q, k, v = whole
+    main = b_ref.shape[0] - 2 * length
+    b_ref[:length] = q
+    b_ref[length : 2 * length] = k
+    b_ref[2 * length :] = v[:main]
+    c_ref[...] = v[main:]
     feat = u_ref.shape[-1] // parts
     for p in range(parts):
         o_ref[p, 1] = u_ref[0, :, pl.ds(pl.multiple_of(p * feat + pl.program_id(0) * HD, HD), HD)]
@@ -80,10 +85,12 @@
 
 
 HBM = pl.BlockSpec(memory_space=pltpu.HBM)
+FULL = 60 * 2**20
+PIECE = 128
 SMALL = pl.CostEstimate(flops=1, bytes_accessed=1, transcendentals=0)
 
 
-def _move(kernel, out_shape, inputs, n, name, in_specs=None):
+def _move(kernel, out_shape, inputs, n, name, in_specs=None, vmem=8 * 2**20):
     return pl.pallas_call(
         kernel,
         in_specs=in_specs or [HBM] * len(inputs),
@@ -94,7 +101,7 @@
             pltpu.SemaphoreType.DMA((n,)),
             pltpu.SemaphoreType.DMA((n,)),
         ],
-        compiler_params=pltpu.CompilerParams(vmem_limit_bytes=8 * 2**20),
+        compiler_params=pltpu.CompilerParams(vmem_limit_bytes=vmem),
         cost_estimate=SMALL,
         name=name,
     )(*inputs)
@@ -125,7 +132,7 @@
         _through([(stash_ref.at[0, slot, i], i) for i in range(n)], buf_ref, out_ref, in_sems, out_sems)
 
     specs = [pl.BlockSpec(memory_space=pltpu.SMEM), HBM]
-    return _move(kernel, (n, length, feat), (fetch_slot, stash_held), n, "held_block", specs)
+    return _move(kernel, (n, length, feat), (fetch_slot, stash_held), n, "held_block", specs, FULL)
 
 
 def pack_tokens(arrays, parts, after=()):
@@ -143,7 +150,7 @@
         ]
         _through(pairs, buf_ref, out_ref, in_sems, out_sems)
 
-    return _move(kernel, (2, parts, n, some, own), (*arrays, *after), 2 * parts * n, "pack_tokens")
+    return _move(kernel, (2, parts, n, some, own), (*arrays, *after), 2 * parts * n, "pack_tokens", vmem=FULL)
 
 
 def unpack_tokens(x):
@@ -159,6 +166,7 @@
 def forward_core(x, rows_up):
     chunks, parts, _, rows, feat = x.shape
     part_rows = chunks * rows
+    main = 3 * parts * part_rows - PIECE
     return pl.pallas_call(
         _forward_kernel,
         grid=(feat // HD,),
@@ -168,11 +176,13 @@
         ],
         out_specs=[
             pl.BlockSpec((parts, 2, part_rows, HD), lambda h: (0, 0, 0, h)),
-            pl.BlockSpec((3, parts * part_rows, HD), lambda h: (0, 0, h)),
+            pl.BlockSpec((main, HD), lambda h: (0, h)),
+            pl.BlockSpec((PIECE, HD), lambda h: (0, h)),
         ],
         out_shape=[
             jax.ShapeDtypeStruct((parts, 2, part_rows, feat), jnp.bfloat16),
-            jax.ShapeDtypeStruct((3, parts * part_rows, feat), jnp.bfloat16),
+            jax.ShapeDtypeStruct((main, feat), jnp.bfloat16),
+            jax.ShapeDtypeStruct((PIECE, feat), jnp.bfloat16),
         ],
         compiler_params=pltpu.CompilerParams(vmem_limit_bytes=24 * 2**20),
         cost_estimate=SMALL,
@@ -204,6 +214,68 @@
     )(fetched, upstream, after)
 
 
+def place(rows, shape, after):
+    length = shape[2]
+    starts = [k * PIECE for k in range(rows.shape[0] // PIECE)]
+
+    def kernel(x_ref, *refs):
+        out_ref, buf_ref, in_sems, out_sems = refs[-4:]
+        into = [make_copy(x_ref, buf_ref, k, k, in_sems.at[i]) for i, k in enumerate(starts)]
+        out = [
+            pltpu.make_async_copy(
+                buf_ref.at[pl.ds(k, PIECE)], out_ref.at[0, k // length, pl.ds(k % length, PIECE)], out_sems.at[i]
+            )
+            for i, k in enumerate(starts)
+        ]
+        for copy in into:
+            copy.start()
+        for first, second in zip(into, out):
+            first.wait()
+            second.start()
+        for copy in out:
+            copy.wait()
+
+    def make_copy(src, dst, k, t, sem):
+        return pltpu.make_async_copy(src.at[pl.ds(k, PIECE)], dst.at[pl.ds(t, PIECE)], sem)
+
+    return pl.pallas_call(
+        kernel,
+        in_specs=[HBM] * (1 + len(after)),
+        out_specs=HBM,
+        out_shape=jax.ShapeDtypeStruct(shape, jnp.bfloat16),
+        scratch_shapes=[
+            pltpu.VMEM(rows.shape, jnp.bfloat16),
+            pltpu.SemaphoreType.DMA((len(starts),)),
+            pltpu.SemaphoreType.DMA((len(starts),)),
+        ],
+        compiler_params=pltpu.CompilerParams(vmem_limit_bytes=FULL),
+        cost_estimate=SMALL,
+        name="place",
+    )(rows, *after)
+
+
+def place_last(rows, out):
+    n, length = out.shape[1:3]
+    first = length - rows.shape[0]
+
+    def kernel(x_ref, _, out_ref, sem):
+        copy = pltpu.make_async_copy(x_ref, out_ref.at[0, n - 1, pl.ds(first, rows.shape[0])], sem)
+        copy.start()
+        copy.wait()
+
+    return pl.pallas_call(
+        kernel,
+        in_specs=[pl.BlockSpec(memory_space=pltpu.VMEM), HBM],
+        out_specs=HBM,
+        out_shape=jax.ShapeDtypeStruct(out.shape, out.dtype),
+        scratch_shapes=[pltpu.SemaphoreType.DMA],
+        input_output_aliases={1: 0},
+        compiler_params=pltpu.CompilerParams(vmem_limit_bytes=8 * 2**20),
+        cost_estimate=SMALL,
+        name="place_last",
+    )(rows, out)
+
+
 def exchange(x):
     return lax.all_to_all(x, "tensor", split_axis=0, concat_axis=0, tiled=True)
 
@@ -219,20 +291,28 @@
     fetched = lax.ppermute(held, "pipe", mirror)
 
     packed = pack_tokens((query_new, key_new, value_new), parts, after=(held,))
-    output, block = forward_core(lax.map(exchange, packed), upstream)
+    output, block, last = forward_core(lax.map(exchange, packed), upstream)
     both = exchange(output)
-    output = lax.ppermute(both[:, 0], "pipe", [(s, s + 1) for s in range(sections - 1)])
-
     half = sections // 2
+    crossing = lax.ppermute(both[:, 0], "pipe", [(half - 1, half)])
+
     steps = [(0, 2), (1, 3), (half - 2, half - 4), (half - 1, half - 3)]
     steps = steps + [(s + half, t + half) for s, t in steps]
-    token = lax.ppermute(fetched[0, :16, :128], "pipe", steps)
+    token, fetched = lax.optimization_barrier((cotangent[0, :16, :128], fetched))
+    token = lax.ppermute(token, "pipe", steps)
     block, token, fetched = lax.optimization_barrier((block, token, fetched))
-    evicted = lax.ppermute(block[None], "pipe", mirror)
+    moved = lax.ppermute(block, "pipe", mirror)
+    last = lax.ppermute(last, "pipe", mirror)
 
     grads = backward_core(fetched, both[:, 1], token)
-    grads, output = lax.optimization_barrier((grads, output))
-    return unpack_tokens(output[:, None]), unpack_tokens(exchange(grads))[None], evicted
+    grads, crossing = lax.optimization_barrier((grads, crossing))
+    output, _ = lax.optimization_barrier((both[:, 0], token))
+    output = lax.ppermute(output, "pipe", [(s, s + 1) for s in range(sections - 1) if s + 1 != half])
+    output = jnp.where(lax.axis_index("pipe") == half, crossing, output)
+    received = unpack_tokens(output[:, None])
+    gradients = unpack_tokens(exchange(grads))[None]
+    evicted = place(moved, (1, *held.shape), (received, gradients))
+    return received, gradients, place_last(last, evicted)
 
 
 def solution(mesh):

time: 241 us -> 236 us (0.979)
  waiting for transfers between devices: 142 us -> 134 us
  local copies, waits for them, and re-layouts: 16.2 us -> 10.3 us
  Pallas kernels: 26.4 us -> 31.4 us
    ppermute x3 -> x5, waiting for transfers between devices: 85.2 us -> 71 us  [the longest x1 52.8 us: on_device(): moved = lax.ppermute(block, 'pipe', mirror)]
    unnamed x11 -> x2, local copies, waits for them, and re-layouts: 8.48 us -> 0.01 us
    all_to_all x3, waiting for transfers between devices: 31.9 us -> 39.2 us  [exchange(): return lax.all_to_all(x, 'tensor', split_axis=0, concat_axis=0, tiled=True)]
    pallas_call x0 -> x2, Pallas kernels: none -> 3.23 us  [the longest x1 2.54 us: place(): pl.pallas_call(kernel, in_specs=[HBM] * (1 + len(after)), out_specs=HBM,...]
    pallas_call x4, Pallas kernels: 7.21 us -> 9.76 us  [_move(): pl.pallas_call(kernel, in_specs=in_specs or [HBM] * len(inputs), out_spec...]
    dynamic_update_slice x2, local copies, waits for them, and re-layouts: 2.19 us -> 4.72 us  [on_device(): output, block, last = forward_core(lax.map(exchange, packed), upstream)]
    ppermute x3 -> x5, starting transfers between devices: 7.38 us -> 8.65 us  [the longest x1 4.49 us: on_device(): moved = lax.ppermute(block, 'pipe', mirror)]
  transfers between devices with their start and end apart: 8 -> 10, of which waited for: 6 -> 8; matrix products, arithmetic and copies ran while one was open for 3% -> 5% of each run, Pallas kernels for 10% -> 13%
where the time goes in v2:
time: 236 us; the launch traced here: 235 us
  waiting for transfers between devices  134 us (57%)
  starting transfers between devices  31.5 us (13%)
  Pallas kernels  31.4 us (13%)
  blocking collectives  25 us (11%)
  local copies, waits for them, and re-layouts  10.3 us (4%)
    ppermute x1, waiting for transfers between devices, on_device(): moved = lax.ppermute(block, 'pipe', mirror)  52.8 us
    all_to_all x3, waiting for transfers between devices, exchange(): return lax.all_to_all(x, 'tensor', split_axis=0, concat_axis=0, tiled=True)  39.2 us
    all_to_all x1, blocking collectives, exchange(): return lax.all_to_all(x, 'tensor', split_axis=0, concat_axis=0, tiled=True)  25 us
    ppermute x1, waiting for transfers between devices, on_device(): lax.ppermute(output, 'pipe', [(s, s + 1) for s in range(sections - 1) if...  16.9 us
    all_to_all x3, starting transfers between devices, exchange(): return lax.all_to_all(x, 'tensor', split_axis=0, concat_axis=0, tiled=True)  15.4 us
    ppermute x1, waiting for transfers between devices, on_device(): fetched = lax.ppermute(held, 'pipe', mirror)  14.6 us
    pallas_call x1, Pallas kernels, backward_core(): pl.pallas_call(kernel, grid=(feat // HD,), in_specs=[pl.BlockSpec((3, len...  10.1 us
    pallas_call x4, Pallas kernels, _move(): pl.pallas_call(kernel, in_specs=in_specs or [HBM] * len(inputs), out_spec...  9.76 us
  transfers between devices with their start and end apart: 10, of which 8 were waited for; matrix products, arithmetic and copies ran while one was open for 5% of the time, Pallas kernels for 13%

profile of v2, /device:TPU:8, one launch (start us, length us, event | category | flops | bytes accessed | tf_op | source)
XLA Modules:
  0.0 234.6 jit_solution(7706031326467664306)
XLA Ops:
  0.6 6.9 %collective-permute-start = (bf16[1,64,6144]{2,1,0:T(8,128)(2,1)}, bf16[1,64,6144]{2,1,0:T(8,128)(2,1)S(1)}, u32[]{:S(2)}, u32[]{:S(2)}) collective-permute-start(bf16[1,64,6144]{2,1,0:T(8,128)(2,1)} %param.13), channel_id=1, source_target_pairs={{0,240},{16,0},{32,16},{48,32},{64,48},{80,64},{96,80},{112,96},{1... | collective-permute-start | bytes 2359304 | tf_op jit(solution)/shard_map/ppermute | solution.py:289
  7.5 3.3 %held_block.1.refs_3_ = bf16[3,512,768]{2,1,0:T(8,128)(2,1)} custom-call(s32[16]{0:T(128)} %slot_ref.1, bf16[1,2,3,512,768]{4,3,2,1,0:T(8,128)(2,1)} %stash_ref.1), custom_call_target="tpu_custom_call" | custom-call | flops 1 | bytes 1 | tf_op jit(solution)/shard_map/held_block/pallas_call | solution.py:94
  10.8 0.6 collective-permute-start.1
  11.4 3.2 %pack_tokens.1 = bf16[2,8,3,32,768]{4,3,2,1,0:T(8,128)(2,1)} custom-call(bf16[1,64,6144]{2,1,0:T(8,128)(2,1)} %refs_0_.1, bf16[1,64,6144]{2,1,0:T(8,128)(2,1)} %refs_1_.1, bf16[1,64,6144]{2,1,0:T(8,128)(2,1)} %refs_2_.1, bf16[3,512,768]{2,1,0:T(8,128)(2,1)} %held_block.1.refs_3_), custom_call_target="tpu_custom_call" | custom-call | flops 1 | bytes 1 | tf_op jit(solution)/shard_map/pack_tokens/pallas_call | solution.py:94
  14.6 52.1 %while.10 = (s32[]{:T(128)}, bf16[2,8,3,32,768]{4,3,2,1,0:T(8,128)(2,1)}, bf16[2,8,3,32,768]{4,3,2,1,0:T(8,128)(2,1)}, s32[]{:T(128)}) while((s32[]{:T(128)}, bf16[2,8,3,32,768]{4,3,2,1,0:T(8,128)(2,1)}, bf16[2,8,3,32,768]{4,3,2,1,0:T(8,128)(2,1)}, s32[]{:T(128)}) %tuple.31), condition=%wide.region_1.2_spmd, body=%wide.region_0.1_spmd.sunk | while | flops 2 | bytes 8257637 | solution.py:294
  14.6 2.4 %dynamic-slice_bitcast_fusion.2 = bf16[8,3,32,768]{3,2,1,0:T(8,128)(2,1)} fusion(bf16[2,8,3,32,768]{4,3,2,1,0:T(8,128)(2,1)} %get-tuple-element.80, s32[]{:T(128)S(6)} %copy.18), kind=kLoop, calls=%fused_computation.1.clone.1 | loop fusion | bytes 2359300 | tf_op jit(solution)/shard_map/while/body/jit(dynamic_index_in_dim)/squeeze | solution.py:294
  17.0 4.9 %all-to-all-start = ((bf16[8,3,32,768]{3,2,1,0:T(8,128)(2,1)}), bf16[8,3,32,768]{3,2,1,0:T(8,128)(2,1)}, u32[]{:S(2)}, u32[]{:S(2)}) async-start(bf16[8,3,32,768]{3,2,1,0:T(8,128)(2,1)} %dynamic-slice_bitcast_fusion.2), calls=%async_computation | async-start | bytes 2359296 | tf_op jit(solution)/shard_map/while/body/eval_jaxpr/all_to_all | solution.py:280
  21.9 16.0 %all-to-all-done = bf16[8,3,32,768]{3,2,1,0:T(8,128)(2,1)} async-done(((bf16[8,3,32,768]{3,2,1,0:T(8,128)(2,1)}), bf16[8,3,32,768]{3,2,1,0:T(8,128)(2,1)}, u32[]{:S(2)}, u32[]{:S(2)}) %all-to-all-start) | async-done | bytes 1179680 | tf_op jit(solution)/shard_map/while/body/eval_jaxpr/all_to_all | solution.py:280
  37.9 2.4 %bitcast_dynamic-update-slice_fusion.2 = bf16[2,8,3,32,768]{4,3,2,1,0:T(8,128)(2,1)} fusion(bf16[2,8,3,32,768]{4,3,2,1,0:T(8,128)(2,1)} %get-tuple-element.75, s32[]{:T(128)S(6)} %copy.18, bf16[8,3,32,768]{3,2,1,0:T(8,128)(2,1)} %all-to-all-done), kind=kLoop, calls=%fused_computation.clone.1 | loop fusion | bytes 2359300 | tf_op jit(solution)/shard_map/while/body/jit(dynamic_update_index_in_dim)/dynamic_update_slice | solution.py:294
  40.3 2.4 %dynamic-slice_bitcast_fusion.2 = bf16[8,3,32,768]{3,2,1,0:T(8,128)(2,1)} fusion(bf16[2,8,3,32,768]{4,3,2,1,0:T(8,128)(2,1)} %get-tuple-element.80, s32[]{:T(128)S(6)} %copy.18), kind=kLoop, calls=%fused_computation.1.clone.1 | loop fusion | bytes 2359300 | tf_op jit(solution)/shard_map/while/body/jit(dynamic_index_in_dim)/squeeze | solution.py:294
  42.7 5.6 %all-to-all-start = ((bf16[8,3,32,768]{3,2,1,0:T(8,128)(2,1)}), bf16[8,3,32,768]{3,2,1,0:T(8,128)(2,1)}, u32[]{:S(2)}, u32[]{:S(2)}) async-start(bf16[8,3,32,768]{3,2,1,0:T(8,128)(2,1)} %dynamic-slice_bitcast_fusion.2), calls=%async_computation | async-start | bytes 2359296 | tf_op jit(solution)/shard_map/while/body/eval_jaxpr/all_to_all | solution.py:280
  48.2 16.0 %all-to-all-done = bf16[8,3,32,768]{3,2,1,0:T(8,128)(2,1)} async-done(((bf16[8,3,32,768]{3,2,1,0:T(8,128)(2,1)}), bf16[8,3,32,768]{3,2,1,0:T(8,128)(2,1)}, u32[]{:S(2)}, u32[]{:S(2)}) %all-to-all-start) | async-done | bytes 1179680 | tf_op jit(solution)/shard_map/while/body/eval_jaxpr/all_to_all | solution.py:280
  64.3 2.4 %bitcast_dynamic-update-slice_fusion.2 = bf16[2,8,3,32,768]{4,3,2,1,0:T(8,128)(2,1)} fusion(bf16[2,8,3,32,768]{4,3,2,1,0:T(8,128)(2,1)} %get-tuple-element.75, s32[]{:T(128)S(6)} %copy.18, bf16[8,3,32,768]{3,2,1,0:T(8,128)(2,1)} %all-to-all-done), kind=kLoop, calls=%fused_computation.clone.1 | loop fusion | bytes 2359300 | tf_op jit(solution)/shard_map/while/body/jit(dynamic_update_index_in_dim)/dynamic_update_slice | solution.py:294
  66.6 9.7 %collective-permute-done.u_ref = bf16[1,64,6144]{2,1,0:T(8,128)(2,1)S(1)} collective-permute-done((bf16[1,64,6144]{2,1,0:T(8,128)(2,1)}, bf16[1,64,6144]{2,1,0:T(8,128)(2,1)S(1)}, u32[]{:S(2)}, u32[]{:S(2)}) %collective-permute-start) | collective-permute-done | bytes 786464 | tf_op jit(solution)/shard_map/ppermute | solution.py:289
  76.3 8.3 %forward_core.1 = (bf16[8,2,64,768]{3,2,1,0:T(8,128)(2,1)S(1)}, bf16[1408,768]{1,0:T(8,128)(2,1)}, bf16[128,768]{1,0:T(8,128)(2,1)S(1)}) custom-call(bf16[2,8,3,32,768]{4,3,2,1,0:T(8,128)(2,1)} %get-tuple-element.31.x_ref, bf16[1,64,6144]{2,1,0:T(8,128)(2,1)S(1)} %collective-permute-done.u_ref), custom_call_target="tpu_custom_call" | custom-call | flops 1 | bytes 1 | tf_op jit(solution)/shard_map/forward_core/pallas_call | solution.py:170
  84.6 25.0 %all_to_all.16 = bf16[8,2,64,768]{3,2,1,0:T(8,128)(2,1)S(1)} all-to-all(bf16[8,2,64,768]{3,2,1,0:T(8,128)(2,1)S(1)} %get-tuple-element.36), channel_id=1, replica_groups=mesh['pipe'=16,'tensor'=8,'dp'=2] {'tensor'}, dimensions={0} | all-to-all | bytes 3145728 | tf_op jit(solution)/shard_map/all_to_all | solution.py:280
  109.6 0.1 slice_bitcast_fusion
  109.7 0.0 copy-start
  109.7 0.7 collective-permute-start.3
  110.5 0.7 slice_bitcast_fusion.2
  111.1 14.6 %collective-permute-done.1.f_ref = bf16[3,512,768]{2,1,0:T(8,128)(2,1)S(1)} collective-permute-done((bf16[3,512,768]{2,1,0:T(8,128)(2,1)}, bf16[3,512,768]{2,1,0:T(8,128)(2,1)S(1)}, u32[]{:S(2)}, u32[]{:S(2)}) %collective-permute-start.1) | collective-permute-done | bytes 2359328 | tf_op jit(solution)/shard_map/ppermute | solution.py:291
  125.7 1.3 collective-permute-start.2
  127.0 1.3 collective-permute-done.2._
  128.3 4.5 %collective-permute-start.6 = (bf16[1408,768]{1,0:T(8,128)(2,1)}, bf16[1408,768]{1,0:T(8,128)(2,1)}, u32[]{:S(2)}, u32[]{:S(2)}) collective-permute-start(bf16[1408,768]{1,0:T(8,128)(2,1)} %get-tuple-element.42), channel_id=1, source_target_pairs={{0,240},{16,224},{32,208},{48,192},{64,176},{80,160},{96,144},{112... | collective-permute-start | bytes 6488072 | tf_op jit(solution)/shard_map/ppermute | solution.py:304
  132.8 10.1 %backward_core.1 = bf16[8,3,64,768]{3,2,1,0:T(8,128)(2,1)} custom-call(bf16[3,512,768]{2,1,0:T(8,128)(2,1)S(1)} %collective-permute-done.1.f_ref, bf16[8,64,768]{2,1,0:T(8,128)(2,1)S(1)} %get-tuple-element.50.g_ref, bf16[16,128]{1,0:T(8,128)(2,1)S(1)} %collective-permute-done.2._), custom_call_target="tpu_custom_call" | custom-call | flops 1 | bytes 1 | tf_op jit(solution)/shard_map/backward_core/pallas_call | solution.py:200
  142.9 0.0 copy-done
  142.9 0.0 collective-permute-done.3
  142.9 4.9 %all-to-all-start.2 = ((bf16[8,3,64,768]{3,2,1,0:T(8,128)(2,1)}), bf16[8,3,64,768]{3,2,1,0:T(8,128)(2,1)S(1)}, u32[]{:S(2)}, u32[]{:S(2)}) async-start(bf16[8,3,64,768]{3,2,1,0:T(8,128)(2,1)} %backward_core.1), calls=%async_computation.2 | async-start | bytes 4718592 | tf_op jit(solution)/shard_map/all_to_all | solution.py:280
  147.8 2.2 collective-permute-start.4
  150.0 0.0 collective-permute-start.5
  150.0 16.9 %collective-permute-done.4 = bf16[8,64,768]{2,1,0:T(8,128)(2,1)} collective-permute-done((bf16[8,64,768]{2,1,0:T(8,128)(2,1)}, bf16[8,64,768]{2,1,0:T(8,128)(2,1)}, u32[]{:S(2)}, u32[]{:S(2)}) %collective-permute-start.4) | collective-permute-done | bytes 786464 | tf_op jit(solution)/shard_map/ppermute | solution.py:310
  166.9 1.2 select_bitcast_fusion.x_ref
  168.1 1.1 unpack_tokens.2.refs_0_
  169.2 7.2 %all-to-all-done.2.x_ref = bf16[8,3,64,768]{3,2,1,0:T(8,128)(2,1)S(1)} async-done(((bf16[8,3,64,768]{3,2,1,0:T(8,128)(2,1)}), bf16[8,3,64,768]{3,2,1,0:T(8,128)(2,1)S(1)}, u32[]{:S(2)}, u32[]{:S(2)}) %all-to-all-start.2) | async-done | bytes 2359328 | tf_op jit(solution)/shard_map/all_to_all | solution.py:280
  176.4 2.2 unpack_tokens.3
  178.6 52.8 %collective-permute-done.6.x_ref = bf16[1408,768]{1,0:T(8,128)(2,1)} collective-permute-done((bf16[1408,768]{1,0:T(8,128)(2,1)}, bf16[1408,768]{1,0:T(8,128)(2,1)}, u32[]{:S(2)}, u32[]{:S(2)}) %collective-permute-start.6) | collective-permute-done | bytes 2162720 | tf_op jit(solution)/shard_map/ppermute | solution.py:304
  231.4 2.5 %place.1._ = bf16[1,3,512,768]{3,2,1,0:T(8,128)(2,1)} custom-call(bf16[1408,768]{1,0:T(8,128)(2,1)} %collective-permute-done.6.x_ref, bf16[1,64,6144]{2,1,0:T(8,128)(2,1)} %unpack_tokens.2.refs_0_, bf16[1,3,64,6144]{3,2,1,0:T(8,128)(2,1)} %bitcast.21), custom_call_target="tpu_custom_call" | custom-call | flops 1 | bytes 1 | tf_op jit(solution)/shard_map/place/pallas_call | solution.py:241
  233.9 0.0 collective-permute-done.5.x_ref
  233.9 0.7 place_last.1
  (1 shorter events, 0.0 us)
Async XLA Ops:
  0.6 75.7 %collective-permute-start = (bf16[1,64,6144]{2,1,0:T(8,128)(2,1)}, bf16[1,64,6144]{2,1,0:T(8,128)(2,1)S(1)}, u32[]{:S(2)}, u32[]{:S(2)}) collective-permute-start(bf16[1,64,6144]{2,1,0:T(8,128)(2,1)} %param.13), channel_id=1, source_target_pairs={{0,240},{16,0},{32,16},{48,32},{64,48},{80,64},{96,80},{112,96},{1... | collective-permute-start | bytes 2359304 | tf_op jit(solution)/shard_map/ppermute | solution.py:289
  10.8 115.0 %collective-permute-start.1 = (bf16[3,512,768]{2,1,0:T(8,128)(2,1)}, bf16[3,512,768]{2,1,0:T(8,128)(2,1)S(1)}, u32[]{:S(2)}, u32[]{:S(2)}) collective-permute-start(bf16[3,512,768]{2,1,0:T(8,128)(2,1)} %held_block.1.refs_3_), channel_id=1, source_target_pairs={{0,240},{16,224},{32,208},{48,192},{64,176},{80,160},{96,144},{112... | collective-permute-start | bytes 7077896 | tf_op jit(solution)/shard_map/ppermute | solution.py:291
  17.0 20.9 %all-to-all-start = ((bf16[8,3,32,768]{3,2,1,0:T(8,128)(2,1)}), bf16[8,3,32,768]{3,2,1,0:T(8,128)(2,1)}, u32[]{:S(2)}, u32[]{:S(2)}) async-start(bf16[8,3,32,768]{3,2,1,0:T(8,128)(2,1)} %dynamic-slice_bitcast_fusion.2), calls=%async_computation | async-start | bytes 2359296 | tf_op jit(solution)/shard_map/while/body/eval_jaxpr/all_to_all | solution.py:280
  42.7 21.6 %all-to-all-start = ((bf16[8,3,32,768]{3,2,1,0:T(8,128)(2,1)}), bf16[8,3,32,768]{3,2,1,0:T(8,128)(2,1)}, u32[]{:S(2)}, u32[]{:S(2)}) async-start(bf16[8,3,32,768]{3,2,1,0:T(8,128)(2,1)} %dynamic-slice_bitcast_fusion.2), calls=%async_computation | async-start | bytes 2359296 | tf_op jit(solution)/shard_map/while/body/eval_jaxpr/all_to_all | solution.py:280
  109.7 33.2 %copy-start = (bf16[8,64,768]{2,1,0:T(8,128)(2,1)}, bf16[8,64,768]{2,1,0:T(8,128)(2,1)S(1)}, u32[]{:S(2)}) copy-start(bf16[8,64,768]{2,1,0:T(8,128)(2,1)S(1)} %get-tuple-element.39) | copy-start | bytes 2359300
  109.7 33.2 %collective-permute-start.3 = (bf16[8,64,768]{2,1,0:T(8,128)(2,1)S(1)}, bf16[8,64,768]{2,1,0:T(8,128)(2,1)S(1)}, u32[]{:S(2)}, u32[]{:S(2)}) collective-permute-start(bf16[8,64,768]{2,1,0:T(8,128)(2,1)S(1)} %get-tuple-element.39), channel_id=1, source_target_pairs={{112,128},{113,129},{114,130},{115,131},{116,132},{117,133},{118,1... | collective-permute-start | bytes 2359304 | tf_op jit(solution)/shard_map/ppermute | solution.py:297
  125.7 2.6 %collective-permute-start.2 = (bf16[16,128]{1,0:T(8,128)(2,1)S(1)}, bf16[16,128]{1,0:T(8,128)(2,1)S(1)}, u32[]{:S(2)}, u32[]{:S(2)}) collective-permute-start(bf16[16,128]{1,0:T(8,128)(2,1)S(1)} %slice_bitcast_fusion.2), channel_id=1, source_target_pairs={{0,32},{16,48},{96,64},{112,80},{128,160},{144,176},{224,192},{240... | collective-permute-start | bytes 12296 | tf_op jit(solution)/shard_map/ppermute | solution.py:302
  128.3 103.1 %collective-permute-start.6 = (bf16[1408,768]{1,0:T(8,128)(2,1)}, bf16[1408,768]{1,0:T(8,128)(2,1)}, u32[]{:S(2)}, u32[]{:S(2)}) collective-permute-start(bf16[1408,768]{1,0:T(8,128)(2,1)} %get-tuple-element.42), channel_id=1, source_target_pairs={{0,240},{16,224},{32,208},{48,192},{64,176},{80,160},{96,144},{112... | collective-permute-start | bytes 6488072 | tf_op jit(solution)/shard_map/ppermute | solution.py:304
  142.9 33.5 %all-to-all-start.2 = ((bf16[8,3,64,768]{3,2,1,0:T(8,128)(2,1)}), bf16[8,3,64,768]{3,2,1,0:T(8,128)(2,1)S(1)}, u32[]{:S(2)}, u32[]{:S(2)}) async-start(bf16[8,3,64,768]{3,2,1,0:T(8,128)(2,1)} %backward_core.1), calls=%async_computation.2 | async-start | bytes 4718592 | tf_op jit(solution)/shard_map/all_to_all | solution.py:280
  147.8 19.0 %collective-permute-start.4 = (bf16[8,64,768]{2,1,0:T(8,128)(2,1)}, bf16[8,64,768]{2,1,0:T(8,128)(2,1)}, u32[]{:S(2)}, u32[]{:S(2)}) collective-permute-start(bf16[8,64,768]{2,1,0:T(8,128)(2,1)} %copy-done), channel_id=1, source_target_pairs={{0,16},{16,32},{32,48},{48,64},{64,80},{80,96},{96,112},{128,144},... | collective-permute-start | bytes 2359304 | tf_op jit(solution)/shard_map/ppermute | solution.py:310
  150.0 83.9 %collective-permute-start.5 = (bf16[128,768]{1,0:T(8,128)(2,1)S(1)}, bf16[128,768]{1,0:T(8,128)(2,1)S(1)}, u32[]{:S(2)}, u32[]{:S(2)}) collective-permute-start(bf16[128,768]{1,0:T(8,128)(2,1)S(1)} %get-tuple-element.41), channel_id=1, source_target_pairs={{0,240},{16,224},{32,208},{48,192},{64,176},{80,160},{96,144},{112... | collective-permute-start | bytes 589832 | tf_op jit(solution)/shard_map/ppermute | solution.py:305

commit v3 on v2

--- a/solution.py
+++ b/solution.py
@@ -32,14 +32,9 @@
 
 
 def _forward_kernel(x_ref, u_ref, o_ref, b_ref, c_ref):
-    chunks, parts, _, rows, _ = x_ref.shape
-    part_rows = chunks * rows
-    length = chunks * parts * rows
-    whole = []
-    for i in range(3):
-        blocks = [x_ref[j, p, i] for p in range(parts) for j in range(chunks)]
-        whole.append(jnp.concatenate(blocks, axis=0))
-    q, k, v = whole
+    parts, _, part_rows, _ = x_ref.shape
+    length = parts * part_rows
+    q, k, v = (x_ref[:, i].reshape(length, HD) for i in range(3))
     main = b_ref.shape[0] - 2 * length
     b_ref[:length] = q
     b_ref[length : 2 * length] = k
@@ -138,19 +133,14 @@
 def pack_tokens(arrays, parts, after=()):
     n = len(arrays)
     _, rows, feat = arrays[0].shape
-    own, some = feat // parts, rows // 2
+    own = feat // parts
 
     def kernel(*refs):
         out_ref, buf_ref, in_sems, out_sems = refs[-4:]
-        pairs = [
-            (refs[i].at[0, pl.ds(j * some, some), pl.ds(p * own, own)], (j, p, i))
-            for j in range(2)
-            for p in range(parts)
-            for i in range(n)
-        ]
+        pairs = [(refs[i].at[0, :, pl.ds(p * own, own)], (p, i)) for p in range(parts) for i in range(n)]
         _through(pairs, buf_ref, out_ref, in_sems, out_sems)
 
-    return _move(kernel, (2, parts, n, some, own), (*arrays, *after), 2 * parts * n, "pack_tokens", vmem=FULL)
+    return _move(kernel, (parts, n, rows, own), (*arrays, *after), parts * n, "pack_tokens", vmem=FULL)
 
 
 def unpack_tokens(x):
@@ -164,14 +154,13 @@
 
 
 def forward_core(x, rows_up):
-    chunks, parts, _, rows, feat = x.shape
-    part_rows = chunks * rows
+    parts, _, part_rows, feat = x.shape
     main = 3 * parts * part_rows - PIECE
     return pl.pallas_call(
         _forward_kernel,
         grid=(feat // HD,),
         in_specs=[
-            pl.BlockSpec((chunks, parts, 3, rows, HD), lambda h: (0, 0, 0, 0, h)),
+            pl.BlockSpec((parts, 3, part_rows, HD), lambda h: (0, 0, 0, h)),
             pl.BlockSpec(rows_up.shape, lambda h: (0, 0, 0)),
         ],
         out_specs=[
@@ -185,25 +174,21 @@
             jax.ShapeDtypeStruct((PIECE, feat), jnp.bfloat16),
         ],
         compiler_params=pltpu.CompilerParams(vmem_limit_bytes=24 * 2**20),
-        cost_estimate=SMALL,
+        cost_estimate=pl.CostEstimate(flops=23000000000, bytes_accessed=73800000, transcendentals=0),
         name="forward_core",
     )(x, rows_up)
 
 
-def backward_core(fetched, upstream, after):
+def backward_core(fetched, upstream):
     parts, rows, feat = upstream.shape
     length = parts * rows
 
-    def kernel(f_ref, g_ref, _, *refs):
-        _backward_kernel(f_ref, g_ref, *refs)
-
-    return pl.pallas_call(
-        kernel,
+    return pl.pallas_call(
+        _backward_kernel,
         grid=(feat // HD,),
         in_specs=[
             pl.BlockSpec((3, length, HD), lambda h: (0, 0, h)),
             pl.BlockSpec((parts, rows, HD), lambda h: (0, 0, h)),
-            pl.BlockSpec(memory_space=pl.ANY),
         ],
         out_specs=pl.BlockSpec((parts, 3, rows, HD), lambda h: (0, 0, 0, h)),
         out_shape=jax.ShapeDtypeStruct((parts, 3, rows, feat), jnp.bfloat16),
@@ -211,7 +196,7 @@
         compiler_params=pltpu.CompilerParams(vmem_limit_bytes=24 * 2**20),
         cost_estimate=SMALL,
         name="backward_core",
-    )(fetched, upstream, after)
+    )(fetched, upstream)
 
 
 def place(rows, shape, after):
@@ -280,35 +265,35 @@
     return lax.all_to_all(x, "tensor", split_axis=0, concat_axis=0, tiled=True)
 
 
+def apart(x, times):
+    def step(state):
+        return state[0] + 1, exchange(state[1])
+
+    return lax.while_loop(lambda state: state[0] < times, step, (0, x))[1]
+
+
 def on_device(query_new, key_new, value_new, stash_held, fetch_slot, cotangent):
     sections = lax.axis_size("pipe")
     section = lax.axis_index("pipe")
     parts = lax.axis_size("tensor")
     mirror = [(s, sections - 1 - s) for s in range(sections)]
 
+    once = jnp.minimum(jnp.max(fetch_slot) + 1, 1)
     upstream = lax.ppermute(cotangent, "pipe", [(s, (s - 1) % sections) for s in range(sections)])
     held = held_block(fetch_slot, stash_held)
     fetched = lax.ppermute(held, "pipe", mirror)
 
     packed = pack_tokens((query_new, key_new, value_new), parts, after=(held,))
-    output, block, last = forward_core(lax.map(exchange, packed), upstream)
-    both = exchange(output)
-    half = sections // 2
-    crossing = lax.ppermute(both[:, 0], "pipe", [(half - 1, half)])
-
-    steps = [(0, 2), (1, 3), (half - 2, half - 4), (half - 1, half - 3)]
-    steps = steps + [(s + half, t + half) for s, t in steps]
-    token, fetched = lax.optimization_barrier((cotangent[0, :16, :128], fetched))
-    token = lax.ppermute(token, "pipe", steps)
-    block, token, fetched = lax.optimization_barrier((block, token, fetched))
+    output, block, last = forward_core(apart(packed, once), upstream)
+    both = apart(output, once)
+    output = lax.ppermute(both[:, 0], "pipe", [(s, s + 1) for s in range(sections - 1)])
+
+    block, both = lax.optimization_barrier((block, both))
     moved = lax.ppermute(block, "pipe", mirror)
     last = lax.ppermute(last, "pipe", mirror)
 
-    grads = backward_core(fetched, both[:, 1], token)
-    grads, crossing = lax.optimization_barrier((grads, crossing))
-    output, _ = lax.optimization_barrier((both[:, 0], token))
-    output = lax.ppermute(output, "pipe", [(s, s + 1) for s in range(sections - 1) if s + 1 != half])
-    output = jnp.where(lax.axis_index("pipe") == half, crossing, output)
+    grads = backward_core(fetched, both[:, 1])
+    grads, output = lax.optimization_barrier((grads, output))
     received = unpack_tokens(output[:, None])
     gradients = unpack_tokens(exchange(grads))[None]
     evicted = place(moved, (1, *held.shape), (received, gradients))

time: 236 us -> 230 us (0.975)
  the two profiles are of different devices: /device:TPU:8 before, /device:TPU:128 now
where the time goes in v3:
time: 230 us; the launch traced here: 229 us
  waiting for transfers between devices  160 us (70%)
  Pallas kernels  30.2 us (13%)
  starting transfers between devices  25.6 us (11%)
  local copies, waits for them, and re-layouts  11.2 us (5%)
    all_to_all x3, waiting for transfers between devices, exchange(): return lax.all_to_all(x, 'tensor', split_axis=0, concat_axis=0, tiled=True)  76.1 us
    ppermute x1, waiting for transfers between devices, on_device(): fetched = lax.ppermute(held, 'pipe', mirror)  73.4 us
    all_to_all x3, starting transfers between devices, exchange(): return lax.all_to_all(x, 'tensor', split_axis=0, concat_axis=0, tiled=True)  13.2 us
    ppermute x1, waiting for transfers between devices, on_device(): moved = lax.ppermute(block, 'pipe', mirror)  10.8 us
    pallas_call x1, Pallas kernels, backward_core(): pl.pallas_call(_backward_kernel, grid=(feat // HD,), in_specs=[pl.BlockSp...  9.68 us
    pallas_call x4, Pallas kernels, _move(): pl.pallas_call(kernel, in_specs=in_specs or [HBM] * len(inputs), out_spec...  9.35 us
    pallas_call x1, Pallas kernels, forward_core(): pl.pallas_call(_forward_kernel, grid=(feat // HD,), in_specs=[pl.BlockSpe...  7.93 us
    while x2, local copies, waits for them, and re-layouts  6.03 us
  transfers between devices with their start and end apart: 8, of which 6 were waited for; matrix products, arithmetic and copies ran while one was open for 4% of the time, Pallas kernels for 13%

profile of v3, /device:TPU:128, one launch (start us, length us, event | category | flops | bytes accessed | tf_op | source)
XLA Modules:
  0.0 229.4 jit_solution(17126322647586299748)
XLA Ops:
  0.6 1.1 collective-permute-start.1
  1.7 3.3 %held_block.1.refs_3_ = bf16[3,512,768]{2,1,0:T(8,128)(2,1)} custom-call(s32[16]{0:T(128)} %slot_ref.1, bf16[1,2,3,512,768]{4,3,2,1,0:T(8,128)(2,1)} %stash_ref.1), custom_call_target="tpu_custom_call" | custom-call | flops 1 | bytes 1 | tf_op jit(solution)/shard_map/held_block/pallas_call | solution.py:89
  5.0 0.0 copy-start.2
  5.0 0.6 collective-permute-start
  5.6 2.8 %pack_tokens.1 = bf16[8,3,64,768]{3,2,1,0:T(8,128)(2,1)} custom-call(bf16[1,64,6144]{2,1,0:T(8,128)(2,1)} %refs_0_.1, bf16[1,64,6144]{2,1,0:T(8,128)(2,1)} %refs_1_.1, bf16[1,64,6144]{2,1,0:T(8,128)(2,1)} %refs_2_.1, bf16[3,512,768]{2,1,0:T(8,128)(2,1)} %held_block.1.refs_3_), custom_call_target="tpu_custom_call" | custom-call | flops 1 | bytes 1 | tf_op jit(solution)/shard_map/pack_tokens/pallas_call | solution.py:89
  8.4 0.0 copy-done.2
  8.5 0.7 reduce_max.9
  9.8 37.9 %while.20 = (s32[]{:T(128)}, bf16[8,3,64,768]{3,2,1,0:T(8,128)(2,1)}, s32[]{:T(128)}, s32[]{:T(128)}) while((s32[]{:T(128)}, bf16[8,3,64,768]{3,2,1,0:T(8,128)(2,1)}, s32[]{:T(128)}, s32[]{:T(128)}) %tuple.39), condition=%wide.region_2.0_spmd, body=%wide.region_1.0_spmd.sunk | while | flops 2 | bytes 11796565 | solution.py:272
  9.8 4.5 %all-to-all-start = ((bf16[8,3,64,768]{3,2,1,0:T(8,128)(2,1)}), bf16[8,3,64,768]{3,2,1,0:T(8,128)(2,1)}, u32[]{:S(2)}, u32[]{:S(2)}) async-start(bf16[8,3,64,768]{3,2,1,0:T(8,128)(2,1)} %get-tuple-element.112), calls=%async_computation | async-start | bytes 4718592 | tf_op jit(solution)/shard_map/while/body/all_to_all | solution.py:265
  14.3 30.1 %all-to-all-done = bf16[8,3,64,768]{3,2,1,0:T(8,128)(2,1)} async-done(((bf16[8,3,64,768]{3,2,1,0:T(8,128)(2,1)}), bf16[8,3,64,768]{3,2,1,0:T(8,128)(2,1)}, u32[]{:S(2)}, u32[]{:S(2)}) %all-to-all-start) | async-done | bytes 2359328 | tf_op jit(solution)/shard_map/while/body/all_to_all | solution.py:265
  44.4 3.3 %copy.21 = bf16[8,3,64,768]{3,2,1,0:T(8,128)(2,1)} copy(bf16[8,3,64,768]{3,2,1,0:T(8,128)(2,1)} %all-to-all-done) | data formatting | bytes 4718592 | tf_op jit(solution)/shard_map/while
  47.7 0.0 collective-permute-done.1.u_ref
  47.7 7.9 %forward_core.1 = (bf16[8,2,64,768]{3,2,1,0:T(8,128)(2,1)}, bf16[1408,768]{1,0:T(8,128)(2,1)S(1)}, bf16[128,768]{1,0:T(8,128)(2,1)S(1)}) custom-call(bf16[8,3,64,768]{3,2,1,0:T(8,128)(2,1)} %get-tuple-element.46.x_ref, bf16[1,64,6144]{2,1,0:T(8,128)(2,1)S(1)} %collective-permute-done.1.u_ref), custom_call_target="tpu_custom_call" | custom-call | flops 23000000512 | bytes 73800000 | tf_op jit(solution)/shard_map/forward_core/pallas_call | solution.py:159
  55.6 0.0 copy-start.1
  55.6 1.4 copy-done.1
  57.0 28.6 %while.21 = (s32[]{:T(128)}, bf16[8,2,64,768]{3,2,1,0:T(8,128)(2,1)}, s32[]{:T(128)}, s32[]{:T(128)}) while((s32[]{:T(128)}, bf16[8,2,64,768]{3,2,1,0:T(8,128)(2,1)}, s32[]{:T(128)}, s32[]{:T(128)}) %tuple.42), condition=%wide.region_4.0_spmd, body=%wide.region_3.0_spmd.sunk | while | flops 2 | bytes 7864405 | solution.py:272
  57.0 4.3 %all-to-all-start.1 = ((bf16[8,2,64,768]{3,2,1,0:T(8,128)(2,1)}), bf16[8,2,64,768]{3,2,1,0:T(8,128)(2,1)}, u32[]{:S(2)}, u32[]{:S(2)}) async-start(bf16[8,2,64,768]{3,2,1,0:T(8,128)(2,1)} %get-tuple-element.124), calls=%async_computation.1 | async-start | bytes 3145728 | tf_op jit(solution)/shard_map/while/body/all_to_all | solution.py:265
  61.3 21.6 %all-to-all-done.1 = bf16[8,2,64,768]{3,2,1,0:T(8,128)(2,1)} async-done(((bf16[8,2,64,768]{3,2,1,0:T(8,128)(2,1)}), bf16[8,2,64,768]{3,2,1,0:T(8,128)(2,1)}, u32[]{:S(2)}, u32[]{:S(2)}) %all-to-all-start.1) | async-done | bytes 1572896 | tf_op jit(solution)/shard_map/while/body/all_to_all | solution.py:265
  82.8 2.7 %copy.27 = bf16[8,2,64,768]{3,2,1,0:T(8,128)(2,1)} copy(bf16[8,2,64,768]{3,2,1,0:T(8,128)(2,1)} %all-to-all-done.1) | data formatting | bytes 3145728 | tf_op jit(solution)/shard_map/while
  85.6 1.2 slice_bitcast_fusion
  86.8 2.9 %collective-permute-start.2 = (bf16[8,64,768]{2,1,0:T(8,128)(2,1)S(1)}, bf16[8,64,768]{2,1,0:T(8,128)(2,1)S(1)}, u32[]{:S(2)}, u32[]{:S(2)}) collective-permute-start(bf16[8,64,768]{2,1,0:T(8,128)(2,1)S(1)} %slice_bitcast_fusion), channel_id=1, source_target_pairs={{0,16},{16,32},{32,48},{48,64},{64,80},{80,96},{96,112},{112,128},... | collective-permute-start | bytes 2359304 | tf_op jit(solution)/shard_map/ppermute | solution.py:289
  89.7 3.2 %collective-permute-start.4 = (bf16[1408,768]{1,0:T(8,128)(2,1)}, bf16[1408,768]{1,0:T(8,128)(2,1)}, u32[]{:S(2)}, u32[]{:S(2)}) collective-permute-start(bf16[1408,768]{1,0:T(8,128)(2,1)} %copy-done.1), channel_id=1, source_target_pairs={{0,240},{16,224},{32,208},{48,192},{64,176},{80,160},{96,144},{112... | collective-permute-start | bytes 6488072 | tf_op jit(solution)/shard_map/ppermute | solution.py:292
  92.9 1.2 slice_bitcast_fusion.1.g_ref
  94.1 73.4 %collective-permute-done.f_ref = bf16[3,512,768]{2,1,0:T(8,128)(2,1)S(1)} collective-permute-done((bf16[3,512,768]{2,1,0:T(8,128)(2,1)}, bf16[3,512,768]{2,1,0:T(8,128)(2,1)S(1)}, u32[]{:S(2)}, u32[]{:S(2)}) %collective-permute-start) | collective-permute-done | bytes 2359328 | tf_op jit(solution)/shard_map/ppermute | solution.py:284
  167.5 9.7 %backward_core.1 = bf16[8,3,64,768]{3,2,1,0:T(8,128)(2,1)S(1)} custom-call(bf16[3,512,768]{2,1,0:T(8,128)(2,1)S(1)} %collective-permute-done.f_ref, bf16[8,64,768]{2,1,0:T(8,128)(2,1)S(1)} %slice_bitcast_fusion.1.g_ref), custom_call_target="tpu_custom_call" | custom-call | flops 1 | bytes 1 | tf_op jit(solution)/shard_map/backward_core/pallas_call | solution.py:186
  177.2 0.0 copy-start
  177.2 1.4 copy-done
  178.6 0.0 collective-permute-done.2
  178.6 4.5 %all-to-all-start.2 = ((bf16[8,3,64,768]{3,2,1,0:T(8,128)(2,1)}), bf16[8,3,64,768]{3,2,1,0:T(8,128)(2,1)S(1)}, u32[]{:S(2)}, u32[]{:S(2)}) async-start(bf16[8,3,64,768]{3,2,1,0:T(8,128)(2,1)} %copy-done), calls=%async_computation.2 | async-start | bytes 4718592 | tf_op jit(solution)/shard_map/all_to_all | solution.py:265
  183.1 4.5 %collective-permute-start.3 = (bf16[128,768]{1,0:T(8,128)(2,1)S(1)}, bf16[128,768]{1,0:T(8,128)(2,1)S(1)}, u32[]{:S(2)}, u32[]{:S(2)}) collective-permute-start(bf16[128,768]{1,0:T(8,128)(2,1)S(1)} %get-tuple-element.53), channel_id=1, source_target_pairs={{0,240},{16,224},{32,208},{48,192},{64,176},{80,160},{96,144},{112... | collective-permute-start | bytes 589832 | tf_op jit(solution)/shard_map/ppermute | solution.py:293
  187.6 1.1 unpack_tokens.2.refs_0_
  188.7 24.4 %all-to-all-done.2.x_ref = bf16[8,3,64,768]{3,2,1,0:T(8,128)(2,1)S(1)} async-done(((bf16[8,3,64,768]{3,2,1,0:T(8,128)(2,1)}), bf16[8,3,64,768]{3,2,1,0:T(8,128)(2,1)S(1)}, u32[]{:S(2)}, u32[]{:S(2)}) %all-to-all-start.2) | async-done | bytes 2359328 | tf_op jit(solution)/shard_map/all_to_all | solution.py:265
  213.1 2.2 unpack_tokens.3
  215.3 10.8 %collective-permute-done.4.x_ref = bf16[1408,768]{1,0:T(8,128)(2,1)} collective-permute-done((bf16[1408,768]{1,0:T(8,128)(2,1)}, bf16[1408,768]{1,0:T(8,128)(2,1)}, u32[]{:S(2)}, u32[]{:S(2)}) %collective-permute-start.4) | collective-permute-done | bytes 2162720 | tf_op jit(solution)/shard_map/ppermute | solution.py:292
  226.1 2.5 %place.1._ = bf16[1,3,512,768]{3,2,1,0:T(8,128)(2,1)} custom-call(bf16[1408,768]{1,0:T(8,128)(2,1)} %collective-permute-done.4.x_ref, bf16[1,64,6144]{2,1,0:T(8,128)(2,1)} %unpack_tokens.2.refs_0_, bf16[1,3,64,6144]{3,2,1,0:T(8,128)(2,1)} %bitcast.7), custom_call_target="tpu_custom_call" | custom-call | flops 1 | bytes 1 | tf_op jit(solution)/shard_map/place/pallas_call | solution.py:226
  228.6 0.1 collective-permute-done.3.x_ref
  228.7 0.7 place_last.1
Async XLA Ops:
  0.6 47.0 %collective-permute-start.1 = (bf16[1,64,6144]{2,1,0:T(8,128)(2,1)}, bf16[1,64,6144]{2,1,0:T(8,128)(2,1)S(1)}, u32[]{:S(2)}, u32[]{:S(2)}) collective-permute-start(bf16[1,64,6144]{2,1,0:T(8,128)(2,1)} %param.15), channel_id=1, source_target_pairs={{0,240},{16,0},{32,16},{48,32},{64,48},{80,64},{96,80},{112,96},{1... | collective-permute-start | bytes 2359304 | tf_op jit(solution)/shard_map/ppermute | solution.py:282
  5.0 3.4 %copy-start.2 = (s32[16]{0:T(128)S(1)}, s32[16]{0:T(128)}, u32[]{:S(2)}) copy-start(s32[16]{0:T(128)} %slot_ref.1) | copy-start | bytes 196
  5.0 162.5 %collective-permute-start = (bf16[3,512,768]{2,1,0:T(8,128)(2,1)}, bf16[3,512,768]{2,1,0:T(8,128)(2,1)S(1)}, u32[]{:S(2)}, u32[]{:S(2)}) collective-permute-start(bf16[3,512,768]{2,1,0:T(8,128)(2,1)} %held_block.1.refs_3_), channel_id=1, source_target_pairs={{0,240},{16,224},{32,208},{48,192},{64,176},{80,160},{96,144},{112... | collective-permute-start | bytes 7077896 | tf_op jit(solution)/shard_map/ppermute | solution.py:284
  9.8 34.6 %all-to-all-start = ((bf16[8,3,64,768]{3,2,1,0:T(8,128)(2,1)}), bf16[8,3,64,768]{3,2,1,0:T(8,128)(2,1)}, u32[]{:S(2)}, u32[]{:S(2)}) async-start(bf16[8,3,64,768]{3,2,1,0:T(8,128)(2,1)} %get-tuple-element.112), calls=%async_computation | async-start | bytes 4718592 | tf_op jit(solution)/shard_map/while/body/all_to_all | solution.py:265
  55.6 1.4 copy-start.1
  57.0 25.9 %all-to-all-start.1 = ((bf16[8,2,64,768]{3,2,1,0:T(8,128)(2,1)}), bf16[8,2,64,768]{3,2,1,0:T(8,128)(2,1)}, u32[]{:S(2)}, u32[]{:S(2)}) async-start(bf16[8,2,64,768]{3,2,1,0:T(8,128)(2,1)} %get-tuple-element.124), calls=%async_computation.1 | async-start | bytes 3145728 | tf_op jit(solution)/shard_map/while/body/all_to_all | solution.py:265
  86.8 91.8 %collective-permute-start.2 = (bf16[8,64,768]{2,1,0:T(8,128)(2,1)S(1)}, bf16[8,64,768]{2,1,0:T(8,128)(2,1)S(1)}, u32[]{:S(2)}, u32[]{:S(2)}) collective-permute-start(bf16[8,64,768]{2,1,0:T(8,128)(2,1)S(1)} %slice_bitcast_fusion), channel_id=1, source_target_pairs={{0,16},{16,32},{32,48},{48,64},{64,80},{80,96},{96,112},{112,128},... | collective-permute-start | bytes 2359304 | tf_op jit(solution)/shard_map/ppermute | solution.py:289
  89.7 136.3 %collective-permute-start.4 = (bf16[1408,768]{1,0:T(8,128)(2,1)}, bf16[1408,768]{1,0:T(8,128)(2,1)}, u32[]{:S(2)}, u32[]{:S(2)}) collective-permute-start(bf16[1408,768]{1,0:T(8,128)(2,1)} %copy-done.1), channel_id=1, source_target_pairs={{0,240},{16,224},{32,208},{48,192},{64,176},{80,160},{96,144},{112... | collective-permute-start | bytes 6488072 | tf_op jit(solution)/shard_map/ppermute | solution.py:292
  177.2 1.4 copy-start
  178.6 34.5 %all-to-all-start.2 = ((bf16[8,3,64,768]{3,2,1,0:T(8,128)(2,1)}), bf16[8,3,64,768]{3,2,1,0:T(8,128)(2,1)S(1)}, u32[]{:S(2)}, u32[]{:S(2)}) async-start(bf16[8,3,64,768]{3,2,1,0:T(8,128)(2,1)} %copy-done), calls=%async_computation.2 | async-start | bytes 4718592 | tf_op jit(solution)/shard_map/all_to_all | solution.py:265
  183.1 45.6 %collective-permute-start.3 = (bf16[128,768]{1,0:T(8,128)(2,1)S(1)}, bf16[128,768]{1,0:T(8,128)(2,1)S(1)}, u32[]{:S(2)}, u32[]{:S(2)}) collective-permute-start(bf16[128,768]{1,0:T(8,128)(2,1)S(1)} %get-tuple-element.53), channel_id=1, source_target_pairs={{0,240},{16,224},{32,208},{48,192},{64,176},{80,160},{96,144},{112... | collective-permute-start | bytes 589832 | tf_op jit(solution)/shard_map/ppermute | solution.py:293

commit v4 on v3

--- a/solution.py
+++ b/solution.py
@@ -31,7 +31,7 @@
     return shifted / jnp.sum(shifted, axis=-1, keepdims=True)
 
 
-def _forward_kernel(x_ref, u_ref, o_ref, b_ref, c_ref):
+def _forward_kernel(x_ref, o_ref, b_ref, c_ref):
     parts, _, part_rows, _ = x_ref.shape
     length = parts * part_rows
     q, k, v = (x_ref[:, i].reshape(length, HD) for i in range(3))
@@ -40,9 +40,6 @@
     b_ref[length : 2 * length] = k
     b_ref[2 * length :] = v[:main]
     c_ref[...] = v[main:]
-    feat = u_ref.shape[-1] // parts
-    for p in range(parts):
-        o_ref[p, 1] = u_ref[0, :, pl.ds(pl.multiple_of(p * feat + pl.program_id(0) * HD, HD), HD)]
     for first in range(0, length, ROWS):
         last = first + ROWS
         weights = _probs(q[first:last], k[:last], first).astype(jnp.bfloat16)
@@ -53,7 +50,7 @@
 def _backward_kernel(f_ref, g_ref, o_ref, dk_ref, dv_ref):
     parts, rows, _ = g_ref.shape
     length = parts * rows
-    a, b, c = (f_ref[i] for i in range(3))
+    a, b, c = (f_ref[i * length : (i + 1) * length] for i in range(3))
     g = g_ref[...].reshape(length, HD)
 
     def store(kind, first, x):
@@ -82,6 +79,7 @@
 HBM = pl.BlockSpec(memory_space=pltpu.HBM)
 FULL = 60 * 2**20
 PIECE = 128
+AROUND = 256
 SMALL = pl.CostEstimate(flops=1, bytes_accessed=1, transcendentals=0)
 
 
@@ -122,12 +120,37 @@
 def held_block(fetch_slot, stash_held):
     _, _, n, length, feat = stash_held.shape
 
-    def kernel(slot_ref, stash_ref, out_ref, buf_ref, in_sems, out_sems):
+    def kernel(slot_ref, stash_ref, out_ref, end_ref, buf_ref, in_sems, out_sems):
         slot = slot_ref[lax.axis_size("pipe") - 1 - lax.axis_index("pipe")]
-        _through([(stash_ref.at[0, slot, i], i) for i in range(n)], buf_ref, out_ref, in_sems, out_sems)
-
-    specs = [pl.BlockSpec(memory_space=pltpu.SMEM), HBM]
-    return _move(kernel, (n, length, feat), (fetch_slot, stash_held), n, "held_block", specs, FULL)
+        into = [pltpu.make_async_copy(stash_ref.at[0, slot, i], buf_ref.at[i], in_sems.at[i]) for i in range(n)]
+        out = [pltpu.make_async_copy(buf_ref.at[i], out_ref.at[i], out_sems.at[i]) for i in range(n)]
+        last = pltpu.make_async_copy(buf_ref.at[n - 1, pl.ds(length - AROUND, AROUND)], end_ref, out_sems.at[n])
+        for copy in into:
+            copy.start()
+        for first, second in zip(into, out):
+            first.wait()
+            second.start()
+        last.start()
+        for copy in (*out, last):
+            copy.wait()
+
+    return pl.pallas_call(
+        kernel,
+        in_specs=[pl.BlockSpec(memory_space=pltpu.SMEM), HBM],
+        out_specs=[HBM, HBM],
+        out_shape=[
+            jax.ShapeDtypeStruct((n, length, feat), jnp.bfloat16),
+            jax.ShapeDtypeStruct((AROUND, feat), jnp.bfloat16),
+        ],
+        scratch_shapes=[
+            pltpu.VMEM((n, length, feat), jnp.bfloat16),
+            pltpu.SemaphoreType.DMA((n,)),
+            pltpu.SemaphoreType.DMA((n + 1,)),
+        ],
+        compiler_params=pltpu.CompilerParams(vmem_limit_bytes=FULL),
+        cost_estimate=SMALL,
+        name="held_block",
+    )(fetch_slot, stash_held)
 
 
 def pack_tokens(arrays, parts, after=()):
@@ -153,7 +176,31 @@
     return _move(kernel, (n, rows, parts * own), (x,), parts * n, "unpack_tokens")
 
 
-def forward_core(x, rows_up):
+def pack_beside(x, rows_up):
+    parts, _, rows, own = x.shape
+
+    def kernel(_, up_ref, out_ref, buf_ref, in_sems, out_sems):
+        pairs = [(up_ref.at[0, :, pl.ds(p * own, own)], p) for p in range(parts)]
+        _through(pairs, buf_ref, out_ref.at[:, 1], in_sems, out_sems)
+
+    return pl.pallas_call(
+        kernel,
+        in_specs=[HBM] * 2,
+        out_specs=HBM,
+        out_shape=jax.ShapeDtypeStruct(x.shape, x.dtype),
+        scratch_shapes=[
+            pltpu.VMEM((parts, rows, own), jnp.bfloat16),
+            pltpu.SemaphoreType.DMA((parts,)),
+            pltpu.SemaphoreType.DMA((parts,)),
+        ],
+        input_output_aliases={0: 0},
+        compiler_params=pltpu.CompilerParams(vmem_limit_bytes=FULL),
+        cost_estimate=pl.CostEstimate(flops=23000000000, bytes_accessed=73800000, transcendentals=0),
+        name="pack_beside",
+    )(x, rows_up)
+
+
+def forward_core(x):
     parts, _, part_rows, feat = x.shape
     main = 3 * parts * part_rows - PIECE
     return pl.pallas_call(
@@ -161,10 +208,9 @@
         grid=(feat // HD,),
         in_specs=[
             pl.BlockSpec((parts, 3, part_rows, HD), lambda h: (0, 0, 0, h)),
-            pl.BlockSpec(rows_up.shape, lambda h: (0, 0, 0)),
         ],
         out_specs=[
-            pl.BlockSpec((parts, 2, part_rows, HD), lambda h: (0, 0, 0, h)),
+            pl.BlockSpec((parts, 1, part_rows, HD), lambda h: (0, 0, 0, h)),
             pl.BlockSpec((main, HD), lambda h: (0, h)),
             pl.BlockSpec((PIECE, HD), lambda h: (0, h)),
         ],
@@ -174,29 +220,49 @@
             jax.ShapeDtypeStruct((PIECE, feat), jnp.bfloat16),
         ],
         compiler_params=pltpu.CompilerParams(vmem_limit_bytes=24 * 2**20),
-        cost_estimate=pl.CostEstimate(flops=23000000000, bytes_accessed=73800000, transcendentals=0),
+        cost_estimate=SMALL,
         name="forward_core",
-    )(x, rows_up)
-
-
-def backward_core(fetched, upstream):
+    )(x)
+
+
+def one_of(index, members):
+    found = index == members[0]
+    for m in members[1:]:
+        found = found | (index == m)
+    return found
+
+
+def backward_core(whole, main, end, upstream, in_two):
     parts, rows, feat = upstream.shape
     length = parts * rows
 
-    return pl.pallas_call(
-        _backward_kernel,
+    def kernel(w_ref, m_ref, e_ref, g_ref, o_ref, f_ref, dk_ref, dv_ref):
+        here = one_of(lax.axis_index("pipe"), in_two)
+        first = m_ref.shape[0]
+
+        @pl.when(here)
+        def _():
+            f_ref[:first] = m_ref[...]
+            f_ref[first:] = e_ref[...]
+
+        @pl.when(jnp.logical_not(here))
+        def _():
+            f_ref[...] = w_ref[...]
+
+        _backward_kernel(f_ref, g_ref, o_ref, dk_ref, dv_ref)
+
+    return pl.pallas_call(
+        kernel,
         grid=(feat // HD,),
-        in_specs=[
-            pl.BlockSpec((3, length, HD), lambda h: (0, 0, h)),
-            pl.BlockSpec((parts, rows, HD), lambda h: (0, 0, h)),
-        ],
+        in_specs=[pl.BlockSpec((x.shape[0], HD), lambda h: (0, h)) for x in (whole, main, end)]
+        + [pl.BlockSpec((parts, rows, HD), lambda h: (0, 0, h))],
         out_specs=pl.BlockSpec((parts, 3, rows, HD), lambda h: (0, 0, 0, h)),
         out_shape=jax.ShapeDtypeStruct((parts, 3, rows, feat), jnp.bfloat16),
-        scratch_shapes=[pltpu.VMEM((length, HD), jnp.float32)] * 2,
+        scratch_shapes=[pltpu.VMEM((3 * length, HD), jnp.bfloat16)] + [pltpu.VMEM((length, HD), jnp.float32)] * 2,
         compiler_params=pltpu.CompilerParams(vmem_limit_bytes=24 * 2**20),
         cost_estimate=SMALL,
         name="backward_core",
-    )(fetched, upstream)
+    )(whole, main, end, upstream)
 
 
 def place(rows, shape, after):
@@ -280,19 +346,26 @@
 
     once = jnp.minimum(jnp.max(fetch_slot) + 1, 1)
     upstream = lax.ppermute(cotangent, "pipe", [(s, (s - 1) % sections) for s in range(sections)])
-    held = held_block(fetch_slot, stash_held)
-    fetched = lax.ppermute(held, "pipe", mirror)
+    held, end = held_block(fetch_slot, stash_held)
+    half = sections // 2
+    shared = [half - 3, half + 2, 2]
+    beside = [(s, s ^ 1) for s in shared]
+    end = lax.ppermute(end, "pipe", beside)
+    end = lax.ppermute(end, "pipe", [(t, sections - 1 - s) for s, t in beside])
+    rows_held = held.reshape(-1, held.shape[2])
+    whole = lax.ppermute(rows_held, "pipe", [(s, t) for s, t in mirror if s not in shared])
+    main = lax.ppermute(rows_held[:-AROUND], "pipe", [(s, t) for s, t in mirror if s in shared])
 
     packed = pack_tokens((query_new, key_new, value_new), parts, after=(held,))
-    output, block, last = forward_core(apart(packed, once), upstream)
-    both = apart(output, once)
+    output, block, last = forward_core(apart(packed, once))
+    both = apart(pack_beside(output, upstream), once)
     output = lax.ppermute(both[:, 0], "pipe", [(s, s + 1) for s in range(sections - 1)])
 
     block, both = lax.optimization_barrier((block, both))
     moved = lax.ppermute(block, "pipe", mirror)
     last = lax.ppermute(last, "pipe", mirror)
 
-    grads = backward_core(fetched, both[:, 1])
+    grads = backward_core(whole, main, end, both[:, 1], [sections - 1 - s for s in shared])
     grads, output = lax.optimization_barrier((grads, output))
     received = unpack_tokens(output[:, None])
     gradients = unpack_tokens(exchange(grads))[None]

time: 230 us -> 227 us (0.987); the launches traced: 229 us -> 223 us
  waiting for transfers between devices: 160 us -> 142 us
  starting transfers between devices: 25.6 us -> 31.6 us
  Pallas kernels: 30.2 us -> 33.5 us
  local copies, waits for them, and re-layouts: 11.2 us -> 14 us
    ppermute x1 -> x4, waiting for transfers between devices: 73.4 us -> 53.8 us  [the longest x1 53.8 us: on_device(): lax.ppermute(rows_held, 'pipe', [(s, t) for s, t in mirror if s not in sh...]
    pallas_call x1 -> x3, Pallas kernels: 9.68 us -> 16.2 us  [the longest x1 10.8 us: backward_core(): pl.pallas_call(kernel, grid=(feat // HD,), in_specs=[pl.BlockSpec((x.shap...]
    ppermute x1 -> x4, starting transfers between devices: 0.62 us -> 6.61 us  [the longest x1 2.44 us: on_device(): lax.ppermute(rows_held, 'pipe', [(s, t) for s, t in mirror if s not in sh...]
    pallas_call x4 -> x3, Pallas kernels: 9.35 us -> 6.09 us  [_move(): pl.pallas_call(kernel, in_specs=in_specs or [HBM] * len(inputs), out_spec...]
    slice x0 -> x1, local copies, waits for them, and re-layouts: none -> 3 us  [on_device(): rows_held[:-AROUND]]
  transfers between devices with their start and end apart: 8 -> 11, of which waited for: 6 -> 6; matrix products, arithmetic and copies ran while one was open for 4% -> 5% of each run, Pallas kernels for 13% -> 15%
where the time goes in v4:
time: 227 us; the launch traced here: 223 us
  waiting for transfers between devices  142 us (63%)
  Pallas kernels  33.5 us (15%)
  starting transfers between devices  31.6 us (14%)
  local copies, waits for them, and re-layouts  14 us (6%)
    all_to_all x3, waiting for transfers between devices, exchange(): return lax.all_to_all(x, 'tensor', split_axis=0, concat_axis=0, tiled=True)  76.1 us
    ppermute x1, waiting for transfers between devices, on_device(): lax.ppermute(rows_held, 'pipe', [(s, t) for s, t in mirror if s not in sh...  53.8 us
    all_to_all x3, starting transfers between devices, exchange(): return lax.all_to_all(x, 'tensor', split_axis=0, concat_axis=0, tiled=True)  13.3 us
    ppermute x1, waiting for transfers between devices, on_device(): moved = lax.ppermute(block, 'pipe', mirror)  11.9 us
    pallas_call x1, Pallas kernels, backward_core(): pl.pallas_call(kernel, grid=(feat // HD,), in_specs=[pl.BlockSpec((x.shap...  10.8 us
    pallas_call x1, Pallas kernels, forward_core(): pl.pallas_call(_forward_kernel, grid=(feat // HD,), in_specs=[pl.BlockSpe...  7.97 us
    pallas_call x3, Pallas kernels, _move(): pl.pallas_call(kernel, in_specs=in_specs or [HBM] * len(inputs), out_spec...  6.09 us
    while x2, local copies, waits for them, and re-layouts  6.03 us
  transfers between devices with their start and end apart: 11, of which 6 were waited for; matrix products, arithmetic and copies ran while one was open for 5% of the time, Pallas kernels for 15%

profile of v4, /device:TPU:128, one launch (start us, length us, event | category | flops | bytes accessed | tf_op | source)
XLA Modules:
  0.0 223.3 jit_solution(17230952250225228467)
XLA Ops:
  0.6 1.1 collective-permute-start.4
  1.7 3.4 %held_block.1 = (bf16[3,512,768]{2,1,0:T(8,128)(2,1)}, bf16[256,768]{1,0:T(8,128)(2,1)}) custom-call(s32[16]{0:T(128)} %slot_ref.1, bf16[1,2,3,512,768]{4,3,2,1,0:T(8,128)(2,1)} %stash_ref.1), custom_call_target="tpu_custom_call" | custom-call | flops 1 | bytes 1 | tf_op jit(solution)/shard_map/held_block/pallas_call | solution.py:137
  5.1 2.4 %collective-permute-start = (bf16[1536,768]{1,0:T(8,128)(2,1)}, bf16[1536,768]{1,0:T(8,128)(2,1)S(1)}, u32[]{:S(2)}, u32[]{:S(2)}) collective-permute-start(bf16[1536,768]{1,0:T(8,128)(2,1)} %bitcast.10), channel_id=1, source_target_pairs={{0,240},{16,224},{48,192},{64,176},{96,144},{112,128},{128,112},{1... | collective-permute-start | bytes 7077896 | tf_op jit(solution)/shard_map/ppermute | solution.py:356
  7.6 3.0 %slice.12 = bf16[1280,768]{1,0:T(8,128)(2,1)} slice(bf16[1536,768]{1,0:T(8,128)(2,1)} %bitcast.11), slice={[0:1280], [0:768]} | slice | bytes 3932160 | tf_op jit(solution)/shard_map/slice | solution.py:357
  10.6 2.0 collective-permute-start.1
  12.5 0.0 copy-start.3
  12.5 1.5 collective-permute-start.2
  14.1 2.8 %pack_tokens.1 = bf16[8,3,64,768]{3,2,1,0:T(8,128)(2,1)} custom-call(bf16[1,64,6144]{2,1,0:T(8,128)(2,1)} %refs_0_.1, bf16[1,64,6144]{2,1,0:T(8,128)(2,1)} %refs_1_.1, bf16[1,64,6144]{2,1,0:T(8,128)(2,1)} %refs_2_.1, bf16[3,512,768]{2,1,0:T(8,128)(2,1)} %get-tuple-element.48.refs_3_), custom_call_target="tpu_custom_call" | custom-call | flops 1 | bytes 1 | tf_op jit(solution)/shard_map/pack_tokens/pallas_call | solution.py:87
  16.9 0.0 copy-done.3
  16.9 0.7 reduce_max.9
  18.3 37.9 %while.20 = (s32[]{:T(128)}, bf16[8,3,64,768]{3,2,1,0:T(8,128)(2,1)}, s32[]{:T(128)}, s32[]{:T(128)}) while((s32[]{:T(128)}, bf16[8,3,64,768]{3,2,1,0:T(8,128)(2,1)}, s32[]{:T(128)}, s32[]{:T(128)}) %tuple.39), condition=%wide.region_2.0_spmd, body=%wide.region_1.0_spmd.sunk | while | flops 2 | bytes 11796565 | solution.py:338
  18.3 4.5 %all-to-all-start = ((bf16[8,3,64,768]{3,2,1,0:T(8,128)(2,1)}), bf16[8,3,64,768]{3,2,1,0:T(8,128)(2,1)}, u32[]{:S(2)}, u32[]{:S(2)}) async-start(bf16[8,3,64,768]{3,2,1,0:T(8,128)(2,1)} %get-tuple-element.116), calls=%async_computation | async-start | bytes 4718592 | tf_op jit(solution)/shard_map/while/body/all_to_all | solution.py:331
  22.8 30.1 %all-to-all-done = bf16[8,3,64,768]{3,2,1,0:T(8,128)(2,1)} async-done(((bf16[8,3,64,768]{3,2,1,0:T(8,128)(2,1)}), bf16[8,3,64,768]{3,2,1,0:T(8,128)(2,1)}, u32[]{:S(2)}, u32[]{:S(2)}) %all-to-all-start) | async-done | bytes 2359328 | tf_op jit(solution)/shard_map/while/body/all_to_all | solution.py:331
  52.9 3.3 %copy.22 = bf16[8,3,64,768]{3,2,1,0:T(8,128)(2,1)} copy(bf16[8,3,64,768]{3,2,1,0:T(8,128)(2,1)} %all-to-all-done) | data formatting | bytes 4718592 | tf_op jit(solution)/shard_map/while
  56.2 8.0 %forward_core.1 = (bf16[8,2,64,768]{3,2,1,0:T(8,128)(2,1)}, bf16[1408,768]{1,0:T(8,128)(2,1)S(1)}, bf16[128,768]{1,0:T(8,128)(2,1)S(1)}) custom-call(bf16[8,3,64,768]{3,2,1,0:T(8,128)(2,1)} %get-tuple-element.50.x_ref), custom_call_target="tpu_custom_call" | custom-call | flops 1 | bytes 1 | tf_op jit(solution)/shard_map/forward_core/pallas_call | solution.py:206
  64.2 0.0 copy-start.1
  64.2 1.4 copy-done.1
  65.5 0.0 collective-permute-done.4.up_ref
  65.5 0.0 copy-start.4
  65.5 0.9 copy-done.4
  66.4 2.0 pack_beside.1
  68.4 28.6 %while.21 = (s32[]{:T(128)}, bf16[8,2,64,768]{3,2,1,0:T(8,128)(2,1)}, s32[]{:T(128)}, s32[]{:T(128)}) while((s32[]{:T(128)}, bf16[8,2,64,768]{3,2,1,0:T(8,128)(2,1)}, s32[]{:T(128)}, s32[]{:T(128)}) %tuple.42), condition=%wide.region_4.0_spmd, body=%wide.region_3.0_spmd.sunk | while | flops 2 | bytes 7864405 | solution.py:338
  68.5 4.3 %all-to-all-start.1 = ((bf16[8,2,64,768]{3,2,1,0:T(8,128)(2,1)}), bf16[8,2,64,768]{3,2,1,0:T(8,128)(2,1)}, u32[]{:S(2)}, u32[]{:S(2)}) async-start(bf16[8,2,64,768]{3,2,1,0:T(8,128)(2,1)} %get-tuple-element.128), calls=%async_computation.1 | async-start | bytes 3145728 | tf_op jit(solution)/shard_map/while/body/all_to_all | solution.py:331
  72.8 21.6 %all-to-all-done.1 = bf16[8,2,64,768]{3,2,1,0:T(8,128)(2,1)} async-done(((bf16[8,2,64,768]{3,2,1,0:T(8,128)(2,1)}), bf16[8,2,64,768]{3,2,1,0:T(8,128)(2,1)}, u32[]{:S(2)}, u32[]{:S(2)}) %all-to-all-start.1) | async-done | bytes 1572896 | tf_op jit(solution)/shard_map/while/body/all_to_all | solution.py:331
  94.3 2.7 %copy.29 = bf16[8,2,64,768]{3,2,1,0:T(8,128)(2,1)} copy(bf16[8,2,64,768]{3,2,1,0:T(8,128)(2,1)} %all-to-all-done.1) | data formatting | bytes 3145728 | tf_op jit(solution)/shard_map/while
  97.1 1.3 slice_bitcast_fusion
  98.4 2.9 %collective-permute-start.5 = (bf16[8,64,768]{2,1,0:T(8,128)(2,1)S(1)}, bf16[8,64,768]{2,1,0:T(8,128)(2,1)S(1)}, u32[]{:S(2)}, u32[]{:S(2)}) collective-permute-start(bf16[8,64,768]{2,1,0:T(8,128)(2,1)S(1)} %slice_bitcast_fusion), channel_id=1, source_target_pairs={{0,16},{16,32},{32,48},{48,64},{64,80},{80,96},{96,112},{112,128},... | collective-permute-start | bytes 2359304 | tf_op jit(solution)/shard_map/ppermute | solution.py:362
  101.3 0.0 collective-permute-done.2
  101.4 0.7 collective-permute-start.3
  102.0 3.2 %collective-permute-start.7 = (bf16[1408,768]{1,0:T(8,128)(2,1)}, bf16[1408,768]{1,0:T(8,128)(2,1)}, u32[]{:S(2)}, u32[]{:S(2)}) collective-permute-start(bf16[1408,768]{1,0:T(8,128)(2,1)} %copy-done.1), channel_id=1, source_target_pairs={{0,240},{16,224},{32,208},{48,192},{64,176},{80,160},{96,144},{112... | collective-permute-start | bytes 6488072 | tf_op jit(solution)/shard_map/ppermute | solution.py:365
  105.2 0.0 copy-done.2
  105.2 0.1 slice_bitcast_fusion.1.g_ref
  105.3 0.0 collective-permute-done.3.e_ref
  105.3 0.0 collective-permute-done.1.m_ref
  105.3 53.8 %collective-permute-done.w_ref = bf16[1536,768]{1,0:T(8,128)(2,1)S(1)} collective-permute-done((bf16[1536,768]{1,0:T(8,128)(2,1)}, bf16[1536,768]{1,0:T(8,128)(2,1)S(1)}, u32[]{:S(2)}, u32[]{:S(2)}) %collective-permute-start) | collective-permute-done | bytes 2359328 | tf_op jit(solution)/shard_map/ppermute | solution.py:356
  159.1 10.8 %backward_core.1 = bf16[8,3,64,768]{3,2,1,0:T(8,128)(2,1)S(1)} custom-call(bf16[1536,768]{1,0:T(8,128)(2,1)S(1)} %collective-permute-done.w_ref, bf16[1280,768]{1,0:T(8,128)(2,1)} %collective-permute-done.1.m_ref, bf16[256,768]{1,0:T(8,128)(2,1)S(1)} %collective-permute-done.3.e_ref, bf16[8,64,768]{2,1,0:T(8,128)(2,1)S(1)} %slice_bitcast_fusion.1.g_ref), custom_call_target="tpu_custom_call" | custom-call | flops 1 | bytes 1 | tf_op jit(solution)/shard_map/backward_core/pallas_call | solution.py:254
  169.9 0.0 copy-start
  169.9 1.4 copy-done
  171.3 0.0 collective-permute-done.5
  171.3 4.5 %all-to-all-start.2 = ((bf16[8,3,64,768]{3,2,1,0:T(8,128)(2,1)}), bf16[8,3,64,768]{3,2,1,0:T(8,128)(2,1)S(1)}, u32[]{:S(2)}, u32[]{:S(2)}) async-start(bf16[8,3,64,768]{3,2,1,0:T(8,128)(2,1)} %copy-done), calls=%async_computation.2 | async-start | bytes 4718592 | tf_op jit(solution)/shard_map/all_to_all | solution.py:331
  175.7 4.5 %collective-permute-start.6 = (bf16[128,768]{1,0:T(8,128)(2,1)S(1)}, bf16[128,768]{1,0:T(8,128)(2,1)S(1)}, u32[]{:S(2)}, u32[]{:S(2)}) collective-permute-start(bf16[128,768]{1,0:T(8,128)(2,1)S(1)} %get-tuple-element.57), channel_id=1, source_target_pairs={{0,240},{16,224},{32,208},{48,192},{64,176},{80,160},{96,144},{112... | collective-permute-start | bytes 589832 | tf_op jit(solution)/shard_map/ppermute | solution.py:366
  180.2 1.1 unpack_tokens.2.refs_0_
  181.4 24.4 %all-to-all-done.2.x_ref = bf16[8,3,64,768]{3,2,1,0:T(8,128)(2,1)S(1)} async-done(((bf16[8,3,64,768]{3,2,1,0:T(8,128)(2,1)}), bf16[8,3,64,768]{3,2,1,0:T(8,128)(2,1)S(1)}, u32[]{:S(2)}, u32[]{:S(2)}) %all-to-all-start.2) | async-done | bytes 2359328 | tf_op jit(solution)/shard_map/all_to_all | solution.py:331
  205.8 2.2 unpack_tokens.3
  207.9 11.9 %collective-permute-done.7.x_ref = bf16[1408,768]{1,0:T(8,128)(2,1)} collective-permute-done((bf16[1408,768]{1,0:T(8,128)(2,1)}, bf16[1408,768]{1,0:T(8,128)(2,1)}, u32[]{:S(2)}, u32[]{:S(2)}) %collective-permute-start.7) | collective-permute-done | bytes 2162720 | tf_op jit(solution)/shard_map/ppermute | solution.py:365
  219.9 2.5 %place.1._ = bf16[1,3,512,768]{3,2,1,0:T(8,128)(2,1)} custom-call(bf16[1408,768]{1,0:T(8,128)(2,1)} %collective-permute-done.7.x_ref, bf16[1,64,6144]{2,1,0:T(8,128)(2,1)} %unpack_tokens.2.refs_0_, bf16[1,3,64,6144]{3,2,1,0:T(8,128)(2,1)} %bitcast.8), custom_call_target="tpu_custom_call" | custom-call | flops 1 | bytes 1 | tf_op jit(solution)/shard_map/place/pallas_call | solution.py:292
  222.4 0.2 collective-permute-done.6.x_ref
  222.6 0.7 place_last.1
  (1 shorter events, 0.0 us)
Async XLA Ops:
  0.6 64.9 %collective-permute-start.4 = (bf16[1,64,6144]{2,1,0:T(8,128)(2,1)}, bf16[1,64,6144]{2,1,0:T(8,128)(2,1)S(1)}, u32[]{:S(2)}, u32[]{:S(2)}) collective-permute-start(bf16[1,64,6144]{2,1,0:T(8,128)(2,1)} %param.15), channel_id=1, source_target_pairs={{0,240},{16,0},{32,16},{48,32},{64,48},{80,64},{96,80},{112,96},{1... | collective-permute-start | bytes 2359304 | tf_op jit(solution)/shard_map/ppermute | solution.py:348
  5.1 153.9 %collective-permute-start = (bf16[1536,768]{1,0:T(8,128)(2,1)}, bf16[1536,768]{1,0:T(8,128)(2,1)S(1)}, u32[]{:S(2)}, u32[]{:S(2)}) collective-permute-start(bf16[1536,768]{1,0:T(8,128)(2,1)} %bitcast.10), channel_id=1, source_target_pairs={{0,240},{16,224},{48,192},{64,176},{96,144},{112,128},{128,112},{1... | collective-permute-start | bytes 7077896 | tf_op jit(solution)/shard_map/ppermute | solution.py:356
  10.6 94.7 %collective-permute-start.1 = (bf16[1280,768]{1,0:T(8,128)(2,1)}, bf16[1280,768]{1,0:T(8,128)(2,1)}, u32[]{:S(2)}, u32[]{:S(2)}) collective-permute-start(bf16[1280,768]{1,0:T(8,128)(2,1)} %slice.12), channel_id=1, source_target_pairs={{32,208},{80,160},{160,80},{33,209},{81,161},{161,81},{34,210},{82... | collective-permute-start | bytes 5898248 | tf_op jit(solution)/shard_map/ppermute | solution.py:357
  12.5 4.3 %copy-start.3 = (s32[16]{0:T(128)S(1)}, s32[16]{0:T(128)}, u32[]{:S(2)}) copy-start(s32[16]{0:T(128)} %slot_ref.1) | copy-start | bytes 196
  12.5 88.8 %collective-permute-start.2 = (bf16[256,768]{1,0:T(8,128)(2,1)}, bf16[256,768]{1,0:T(8,128)(2,1)}, u32[]{:S(2)}, u32[]{:S(2)}) collective-permute-start(bf16[256,768]{1,0:T(8,128)(2,1)} %get-tuple-element.49), channel_id=1, source_target_pairs={{80,64},{160,176},{32,48},{81,65},{161,177},{33,49},{82,66},{162,1... | collective-permute-start | bytes 1179656 | tf_op jit(solution)/shard_map/ppermute | solution.py:353
  18.3 34.6 %all-to-all-start = ((bf16[8,3,64,768]{3,2,1,0:T(8,128)(2,1)}), bf16[8,3,64,768]{3,2,1,0:T(8,128)(2,1)}, u32[]{:S(2)}, u32[]{:S(2)}) async-start(bf16[8,3,64,768]{3,2,1,0:T(8,128)(2,1)} %get-tuple-element.116), calls=%async_computation | async-start | bytes 4718592 | tf_op jit(solution)/shard_map/while/body/all_to_all | solution.py:331
  64.2 1.4 copy-start.1
  65.5 0.9 copy-start.4
  68.5 25.9 %all-to-all-start.1 = ((bf16[8,2,64,768]{3,2,1,0:T(8,128)(2,1)}), bf16[8,2,64,768]{3,2,1,0:T(8,128)(2,1)}, u32[]{:S(2)}, u32[]{:S(2)}) async-start(bf16[8,2,64,768]{3,2,1,0:T(8,128)(2,1)} %get-tuple-element.128), calls=%async_computation.1 | async-start | bytes 3145728 | tf_op jit(solution)/shard_map/while/body/all_to_all | solution.py:331
  97.1 8.2 %copy-start.2 = (bf16[8,2,64,768]{3,2,1,0:T(8,128)(2,1)S(1)}, bf16[8,2,64,768]{3,2,1,0:T(8,128)(2,1)}, u32[]{:S(2)}) copy-start(bf16[8,2,64,768]{3,2,1,0:T(8,128)(2,1)} %get-tuple-element.54) | copy-start | bytes 4718596
  98.4 72.9 %collective-permute-start.5 = (bf16[8,64,768]{2,1,0:T(8,128)(2,1)S(1)}, bf16[8,64,768]{2,1,0:T(8,128)(2,1)S(1)}, u32[]{:S(2)}, u32[]{:S(2)}) collective-permute-start(bf16[8,64,768]{2,1,0:T(8,128)(2,1)S(1)} %slice_bitcast_fusion), channel_id=1, source_target_pairs={{0,16},{16,32},{32,48},{48,64},{64,80},{80,96},{96,112},{112,128},... | collective-permute-start | bytes 2359304 | tf_op jit(solution)/shard_map/ppermute | solution.py:362
  101.4 3.9 %collective-permute-start.3 = (bf16[256,768]{1,0:T(8,128)(2,1)}, bf16[256,768]{1,0:T(8,128)(2,1)S(1)}, u32[]{:S(2)}, u32[]{:S(2)}) collective-permute-start(bf16[256,768]{1,0:T(8,128)(2,1)} %collective-permute-done.2), channel_id=1, source_target_pairs={{64,160},{176,80},{48,208},{65,161},{177,81},{49,209},{66,162},{17... | collective-permute-start | bytes 1179656 | tf_op jit(solution)/shard_map/ppermute | solution.py:354
  102.0 117.8 %collective-permute-start.7 = (bf16[1408,768]{1,0:T(8,128)(2,1)}, bf16[1408,768]{1,0:T(8,128)(2,1)}, u32[]{:S(2)}, u32[]{:S(2)}) collective-permute-start(bf16[1408,768]{1,0:T(8,128)(2,1)} %copy-done.1), channel_id=1, source_target_pairs={{0,240},{16,224},{32,208},{48,192},{64,176},{80,160},{96,144},{112... | collective-permute-start | bytes 6488072 | tf_op jit(solution)/shard_map/ppermute | solution.py:365
  169.9 1.4 copy-start
  171.3 34.5 %all-to-all-start.2 = ((bf16[8,3,64,768]{3,2,1,0:T(8,128)(2,1)}), bf16[8,3,64,768]{3,2,1,0:T(8,128)(2,1)S(1)}, u32[]{:S(2)}, u32[]{:S(2)}) async-start(bf16[8,3,64,768]{3,2,1,0:T(8,128)(2,1)} %copy-done), calls=%async_computation.2 | async-start | bytes 4718592 | tf_op jit(solution)/shard_map/all_to_all | solution.py:331
  175.7 46.8 %collective-permute-start.6 = (bf16[128,768]{1,0:T(8,128)(2,1)S(1)}, bf16[128,768]{1,0:T(8,128)(2,1)S(1)}, u32[]{:S(2)}, u32[]{:S(2)}) collective-permute-start(bf16[128,768]{1,0:T(8,128)(2,1)S(1)} %get-tuple-element.57), channel_id=1, source_target_pairs={{0,240},{16,224},{32,208},{48,192},{64,176},{80,160},{96,144},{112... | collective-permute-start | bytes 589832 | tf_op jit(solution)/shard_map/ppermute | solution.py:366

commit v5 on v4

--- a/solution.py
+++ b/solution.py
@@ -117,33 +117,53 @@
         copy.wait()
 
 
-def held_block(fetch_slot, stash_held):
+def held_block(fetch_slot, stash_held, in_two):
     _, _, n, length, feat = stash_held.shape
-
-    def kernel(slot_ref, stash_ref, out_ref, end_ref, buf_ref, in_sems, out_sems):
-        slot = slot_ref[lax.axis_size("pipe") - 1 - lax.axis_index("pipe")]
-        into = [pltpu.make_async_copy(stash_ref.at[0, slot, i], buf_ref.at[i], in_sems.at[i]) for i in range(n)]
-        out = [pltpu.make_async_copy(buf_ref.at[i], out_ref.at[i], out_sems.at[i]) for i in range(n)]
-        last = pltpu.make_async_copy(buf_ref.at[n - 1, pl.ds(length - AROUND, AROUND)], end_ref, out_sems.at[n])
-        for copy in into:
-            copy.start()
-        for first, second in zip(into, out):
-            first.wait()
-            second.start()
-        last.start()
-        for copy in (*out, last):
-            copy.wait()
+    rows = n * length
+
+    def kernel(slot_ref, stash_ref, whole_ref, main_ref, end_ref, buf_ref, in_sems, out_sems):
+        section = lax.axis_index("pipe")
+        slot = slot_ref[lax.axis_size("pipe") - 1 - section]
+        here = one_of(section, in_two)
+
+        def copy(first, size, dst, place, sem):
+            return pltpu.make_async_copy(buf_ref.at[pl.ds(first, size)], dst.at[pl.ds(place, size)], out_sems.at[sem])
+
+        into = [
+            pltpu.make_async_copy(stash_ref.at[0, slot, i], buf_ref.at[pl.ds(i * length, length)], in_sems.at[i])
+            for i in range(n)
+        ]
+        whole = [copy(i * length, length, whole_ref, i * length, i) for i in range(n)]
+        main = [copy(i * length, length, main_ref, i * length, i) for i in range(n - 1)]
+        main.append(copy((n - 1) * length, length - AROUND, main_ref, (n - 1) * length, n - 1))
+        last = copy(rows - AROUND, AROUND, end_ref, 0, n)
+        for c in into:
+            c.start()
+
+        @pl.when(here)
+        def _():
+            for first, second in zip(into, main):
+                first.wait()
+                second.start()
+            last.start()
+            for c in (*main, last):
+                c.wait()
+
+        @pl.when(jnp.logical_not(here))
+        def _():
+            for first, second in zip(into, whole):
+                first.wait()
+                second.start()
+            for c in whole:
+                c.wait()
 
     return pl.pallas_call(
         kernel,
         in_specs=[pl.BlockSpec(memory_space=pltpu.SMEM), HBM],
-        out_specs=[HBM, HBM],
-        out_shape=[
-            jax.ShapeDtypeStruct((n, length, feat), jnp.bfloat16),
-            jax.ShapeDtypeStruct((AROUND, feat), jnp.bfloat16),
-        ],
+        out_specs=[HBM, HBM, HBM],
+        out_shape=[jax.ShapeDtypeStruct((k, feat), jnp.bfloat16) for k in (rows, rows - AROUND, AROUND)],
         scratch_shapes=[
-            pltpu.VMEM((n, length, feat), jnp.bfloat16),
+            pltpu.VMEM((rows, feat), jnp.bfloat16),
             pltpu.SemaphoreType.DMA((n,)),
             pltpu.SemaphoreType.DMA((n + 1,)),
         ],
@@ -219,7 +239,7 @@
             jax.ShapeDtypeStruct((main, feat), jnp.bfloat16),
             jax.ShapeDtypeStruct((PIECE, feat), jnp.bfloat16),
         ],
-        compiler_params=pltpu.CompilerParams(vmem_limit_bytes=24 * 2**20),
+        compiler_params=pltpu.CompilerParams(vmem_limit_bytes=FULL),
         cost_estimate=SMALL,
         name="forward_core",
     )(x)
@@ -346,15 +366,14 @@
 
     once = jnp.minimum(jnp.max(fetch_slot) + 1, 1)
     upstream = lax.ppermute(cotangent, "pipe", [(s, (s - 1) % sections) for s in range(sections)])
-    held, end = held_block(fetch_slot, stash_held)
     half = sections // 2
     shared = [half - 3, half + 2, 2]
     beside = [(s, s ^ 1) for s in shared]
+    held, main, end = held_block(fetch_slot, stash_held, shared)
     end = lax.ppermute(end, "pipe", beside)
     end = lax.ppermute(end, "pipe", [(t, sections - 1 - s) for s, t in beside])
-    rows_held = held.reshape(-1, held.shape[2])
-    whole = lax.ppermute(rows_held, "pipe", [(s, t) for s, t in mirror if s not in shared])
-    main = lax.ppermute(rows_held[:-AROUND], "pipe", [(s, t) for s, t in mirror if s in shared])
+    whole = lax.ppermute(held, "pipe", [(s, t) for s, t in mirror if s not in shared])
+    main = lax.ppermute(main, "pipe", [(s, t) for s, t in mirror if s in shared])
 
     packed = pack_tokens((query_new, key_new, value_new), parts, after=(held,))
     output, block, last = forward_core(apart(packed, once))
@@ -369,7 +388,7 @@
     grads, output = lax.optimization_barrier((grads, output))
     received = unpack_tokens(output[:, None])
     gradients = unpack_tokens(exchange(grads))[None]
-    evicted = place(moved, (1, *held.shape), (received, gradients))
+    evicted = place(moved, (1, *stash_held.shape[2:]), (received, gradients))
     return received, gradients, place_last(last, evicted)
 
 

time: 227 us -> 227 us (level)
  local copies, waits for them, and re-layouts: 14 us -> 9.67 us
  waiting for transfers between devices: 142 us -> 146 us
    ppermute x2, waiting for transfers between devices: 53.8 us -> 58.7 us  [the longest x1 58.7 us: on_device(): lax.ppermute(held, 'pipe', [(s, t) for s, t in mirror if s not in shared])]
    slice x1 -> x0, local copies, waits for them, and re-layouts: 3 us -> none  [on_device(): rows_held[:-AROUND]]
  transfers between devices with their start and end apart: 11 -> 11, of which waited for: 6 -> 6; matrix products, arithmetic and copies ran while one was open for 5% -> 4% of each run, Pallas kernels for 15% -> 15%
where the time goes in v5:
time: 227 us; the launch traced here: 223 us
  waiting for transfers between devices  146 us (64%)
  Pallas kernels  33.6 us (15%)
  starting transfers between devices  31.1 us (14%)
  local copies, waits for them, and re-layouts  9.67 us (4%)
    all_to_all x3, waiting for transfers between devices, exchange(): return lax.all_to_all(x, 'tensor', split_axis=0, concat_axis=0, tiled=True)  76 us
    ppermute x1, waiting for transfers between devices, on_device(): lax.ppermute(held, 'pipe', [(s, t) for s, t in mirror if s not in shared])  58.7 us
    all_to_all x3, starting transfers between devices, exchange(): return lax.all_to_all(x, 'tensor', split_axis=0, concat_axis=0, tiled=True)  13.4 us
    ppermute x1, waiting for transfers between devices, on_device(): moved = lax.ppermute(block, 'pipe', mirror)  11.4 us
    pallas_call x1, Pallas kernels, backward_core(): pl.pallas_call(kernel, grid=(feat // HD,), in_specs=[pl.BlockSpec((x.shap...  10.8 us
    pallas_call x1, Pallas kernels, forward_core(): pl.pallas_call(_forward_kernel, grid=(feat // HD,), in_specs=[pl.BlockSpe...  8.26 us
    pallas_call x3, Pallas kernels, _move(): pl.pallas_call(kernel, in_specs=in_specs or [HBM] * len(inputs), out_spec...  6.1 us
    while x2, local copies, waits for them, and re-layouts  6.03 us
  transfers between devices with their start and end apart: 11, of which 6 were waited for; matrix products, arithmetic and copies ran while one was open for 4% of the time, Pallas kernels for 15%

profile of v5, /device:TPU:128, one launch (start us, length us, event | category | flops | bytes accessed | tf_op | source)
XLA Modules:
  0.0 222.8 jit_solution(6104530966727554521)
XLA Ops:
  0.6 1.1 collective-permute-start.4
  1.7 3.3 %held_block.1 = (bf16[1536,768]{1,0:T(8,128)(2,1)}, bf16[1280,768]{1,0:T(8,128)(2,1)}, bf16[256,768]{1,0:T(8,128)(2,1)}) custom-call(s32[16]{0:T(128)} %slot_ref.1, bf16[1,2,3,512,768]{4,3,2,1,0:T(8,128)(2,1)} %stash_ref.1), custom_call_target="tpu_custom_call" | custom-call | flops 1 | bytes 1 | tf_op jit(solution)/shard_map/held_block/pallas_call | solution.py:160
  5.0 2.4 %collective-permute-start = (bf16[1536,768]{1,0:T(8,128)(2,1)}, bf16[1536,768]{1,0:T(8,128)(2,1)S(1)}, u32[]{:S(2)}, u32[]{:S(2)}) collective-permute-start(bf16[1536,768]{1,0:T(8,128)(2,1)} %get-tuple-element.49.refs_3_), channel_id=1, source_target_pairs={{0,240},{16,224},{48,192},{64,176},{96,144},{112,128},{128,112},{1... | collective-permute-start | bytes 7077896 | tf_op jit(solution)/shard_map/ppermute | solution.py:375
  7.5 2.0 collective-permute-start.1
  9.4 0.0 copy-start.2
  9.4 0.8 collective-permute-start.2
  10.2 2.8 %pack_tokens.1 = bf16[8,3,64,768]{3,2,1,0:T(8,128)(2,1)} custom-call(bf16[1,64,6144]{2,1,0:T(8,128)(2,1)} %refs_0_.1, bf16[1,64,6144]{2,1,0:T(8,128)(2,1)} %refs_1_.1, bf16[1,64,6144]{2,1,0:T(8,128)(2,1)} %refs_2_.1, bf16[1536,768]{1,0:T(8,128)(2,1)} %get-tuple-element.49.refs_3_), custom_call_target="tpu_custom_call" | custom-call | flops 1 | bytes 1 | tf_op jit(solution)/shard_map/pack_tokens/pallas_call | solution.py:87
  13.1 0.0 copy-done.2
  13.1 0.7 reduce_max.9
  14.5 37.9 %while.20 = (s32[]{:T(128)}, bf16[8,3,64,768]{3,2,1,0:T(8,128)(2,1)}, s32[]{:T(128)}, s32[]{:T(128)}) while((s32[]{:T(128)}, bf16[8,3,64,768]{3,2,1,0:T(8,128)(2,1)}, s32[]{:T(128)}, s32[]{:T(128)}) %tuple.39), condition=%wide.region_2.0_spmd, body=%wide.region_1.0_spmd.sunk | while | flops 2 | bytes 11796565 | solution.py:358
  14.5 4.5 %all-to-all-start = ((bf16[8,3,64,768]{3,2,1,0:T(8,128)(2,1)}), bf16[8,3,64,768]{3,2,1,0:T(8,128)(2,1)}, u32[]{:S(2)}, u32[]{:S(2)}) async-start(bf16[8,3,64,768]{3,2,1,0:T(8,128)(2,1)} %get-tuple-element.118), calls=%async_computation | async-start | bytes 4718592 | tf_op jit(solution)/shard_map/while/body/all_to_all | solution.py:351
  19.0 30.1 %all-to-all-done = bf16[8,3,64,768]{3,2,1,0:T(8,128)(2,1)} async-done(((bf16[8,3,64,768]{3,2,1,0:T(8,128)(2,1)}), bf16[8,3,64,768]{3,2,1,0:T(8,128)(2,1)}, u32[]{:S(2)}, u32[]{:S(2)}) %all-to-all-start) | async-done | bytes 2359328 | tf_op jit(solution)/shard_map/while/body/all_to_all | solution.py:351
  49.1 3.3 %copy.22 = bf16[8,3,64,768]{3,2,1,0:T(8,128)(2,1)} copy(bf16[8,3,64,768]{3,2,1,0:T(8,128)(2,1)} %all-to-all-done) | data formatting | bytes 4718592 | tf_op jit(solution)/shard_map/while
  52.4 8.3 %forward_core.1 = (bf16[8,2,64,768]{3,2,1,0:T(8,128)(2,1)}, bf16[1408,768]{1,0:T(8,128)(2,1)}, bf16[128,768]{1,0:T(8,128)(2,1)}) custom-call(bf16[8,3,64,768]{3,2,1,0:T(8,128)(2,1)} %get-tuple-element.52.x_ref), custom_call_target="tpu_custom_call" | custom-call | flops 1 | bytes 1 | tf_op jit(solution)/shard_map/forward_core/pallas_call | solution.py:226
  60.7 0.0 collective-permute-done.4.up_ref
  60.7 0.0 copy-start.3
  60.7 0.9 copy-done.3
  61.5 2.0 pack_beside.1
  63.6 28.6 %while.21 = (s32[]{:T(128)}, bf16[8,2,64,768]{3,2,1,0:T(8,128)(2,1)}, s32[]{:T(128)}, s32[]{:T(128)}) while((s32[]{:T(128)}, bf16[8,2,64,768]{3,2,1,0:T(8,128)(2,1)}, s32[]{:T(128)}, s32[]{:T(128)}) %tuple.42), condition=%wide.region_4.0_spmd, body=%wide.region_3.0_spmd.sunk | while | flops 2 | bytes 7864405 | solution.py:358
  63.6 4.3 %all-to-all-start.1 = ((bf16[8,2,64,768]{3,2,1,0:T(8,128)(2,1)}), bf16[8,2,64,768]{3,2,1,0:T(8,128)(2,1)}, u32[]{:S(2)}, u32[]{:S(2)}) async-start(bf16[8,2,64,768]{3,2,1,0:T(8,128)(2,1)} %get-tuple-element.130), calls=%async_computation.1 | async-start | bytes 3145728 | tf_op jit(solution)/shard_map/while/body/all_to_all | solution.py:351
  67.9 21.6 %all-to-all-done.1 = bf16[8,2,64,768]{3,2,1,0:T(8,128)(2,1)} async-done(((bf16[8,2,64,768]{3,2,1,0:T(8,128)(2,1)}), bf16[8,2,64,768]{3,2,1,0:T(8,128)(2,1)}, u32[]{:S(2)}, u32[]{:S(2)}) %all-to-all-start.1) | async-done | bytes 1572896 | tf_op jit(solution)/shard_map/while/body/all_to_all | solution.py:351
  89.5 2.7 %copy.29 = bf16[8,2,64,768]{3,2,1,0:T(8,128)(2,1)} copy(bf16[8,2,64,768]{3,2,1,0:T(8,128)(2,1)} %all-to-all-done.1) | data formatting | bytes 3145728 | tf_op jit(solution)/shard_map/while
  92.2 0.0 copy-start.1
  92.2 1.3 slice_bitcast_fusion
  93.5 2.9 %collective-permute-start.5 = (bf16[8,64,768]{2,1,0:T(8,128)(2,1)S(1)}, bf16[8,64,768]{2,1,0:T(8,128)(2,1)S(1)}, u32[]{:S(2)}, u32[]{:S(2)}) collective-permute-start(bf16[8,64,768]{2,1,0:T(8,128)(2,1)S(1)} %slice_bitcast_fusion), channel_id=1, source_target_pairs={{0,16},{16,32},{32,48},{48,64},{64,80},{80,96},{96,112},{112,128},... | collective-permute-start | bytes 2359304 | tf_op jit(solution)/shard_map/ppermute | solution.py:381
  96.5 0.0 collective-permute-done.2
  96.5 0.7 collective-permute-start.3
  97.2 3.2 %collective-permute-start.7 = (bf16[1408,768]{1,0:T(8,128)(2,1)}, bf16[1408,768]{1,0:T(8,128)(2,1)}, u32[]{:S(2)}, u32[]{:S(2)}) collective-permute-start(bf16[1408,768]{1,0:T(8,128)(2,1)} %get-tuple-element.60), channel_id=1, source_target_pairs={{0,240},{16,224},{32,208},{48,192},{64,176},{80,160},{96,144},{112... | collective-permute-start | bytes 6488072 | tf_op jit(solution)/shard_map/ppermute | solution.py:384
  100.4 0.0 copy-done.1
  100.4 0.1 slice_bitcast_fusion.1.g_ref
  100.4 0.0 collective-permute-done.3.e_ref
  100.4 0.0 collective-permute-done.1.m_ref
  100.4 58.7 %collective-permute-done.w_ref = bf16[1536,768]{1,0:T(8,128)(2,1)S(1)} collective-permute-done((bf16[1536,768]{1,0:T(8,128)(2,1)}, bf16[1536,768]{1,0:T(8,128)(2,1)S(1)}, u32[]{:S(2)}, u32[]{:S(2)}) %collective-permute-start) | collective-permute-done | bytes 2359328 | tf_op jit(solution)/shard_map/ppermute | solution.py:375
  159.1 10.8 %backward_core.1 = bf16[8,3,64,768]{3,2,1,0:T(8,128)(2,1)S(1)} custom-call(bf16[1536,768]{1,0:T(8,128)(2,1)S(1)} %collective-permute-done.w_ref, bf16[1280,768]{1,0:T(8,128)(2,1)} %collective-permute-done.1.m_ref, bf16[256,768]{1,0:T(8,128)(2,1)S(1)} %collective-permute-done.3.e_ref, bf16[8,64,768]{2,1,0:T(8,128)(2,1)S(1)} %slice_bitcast_fusion.1.g_ref), custom_call_target="tpu_custom_call" | custom-call | flops 1 | bytes 1 | tf_op jit(solution)/shard_map/backward_core/pallas_call | solution.py:274
  169.9 0.0 copy-start
  169.9 1.4 copy-done
  171.3 0.0 copy-start.4
  171.3 0.0 collective-permute-done.5
  171.3 4.6 %all-to-all-start.2 = ((bf16[8,3,64,768]{3,2,1,0:T(8,128)(2,1)}), bf16[8,3,64,768]{3,2,1,0:T(8,128)(2,1)S(1)}, u32[]{:S(2)}, u32[]{:S(2)}) async-start(bf16[8,3,64,768]{3,2,1,0:T(8,128)(2,1)} %copy-done), calls=%async_computation.2 | async-start | bytes 4718592 | tf_op jit(solution)/shard_map/all_to_all | solution.py:351
  175.9 0.0 copy-done.4
  175.9 4.6 %collective-permute-start.6 = (bf16[128,768]{1,0:T(8,128)(2,1)S(1)}, bf16[128,768]{1,0:T(8,128)(2,1)S(1)}, u32[]{:S(2)}, u32[]{:S(2)}) collective-permute-start(bf16[128,768]{1,0:T(8,128)(2,1)S(1)} %copy-done.4), channel_id=1, source_target_pairs={{0,240},{16,224},{32,208},{48,192},{64,176},{80,160},{96,144},{112... | collective-permute-start | bytes 589832 | tf_op jit(solution)/shard_map/ppermute | solution.py:385
  180.5 1.1 unpack_tokens.2.refs_0_
  181.6 24.3 %all-to-all-done.2.x_ref = bf16[8,3,64,768]{3,2,1,0:T(8,128)(2,1)S(1)} async-done(((bf16[8,3,64,768]{3,2,1,0:T(8,128)(2,1)}), bf16[8,3,64,768]{3,2,1,0:T(8,128)(2,1)S(1)}, u32[]{:S(2)}, u32[]{:S(2)}) %all-to-all-start.2) | async-done | bytes 2359328 | tf_op jit(solution)/shard_map/all_to_all | solution.py:351
  205.9 2.2 unpack_tokens.3
  208.1 11.4 %collective-permute-done.7.x_ref = bf16[1408,768]{1,0:T(8,128)(2,1)} collective-permute-done((bf16[1408,768]{1,0:T(8,128)(2,1)}, bf16[1408,768]{1,0:T(8,128)(2,1)}, u32[]{:S(2)}, u32[]{:S(2)}) %collective-permute-start.7) | collective-permute-done | bytes 2162720 | tf_op jit(solution)/shard_map/ppermute | solution.py:384
  219.4 2.5 %place.1._ = bf16[1,3,512,768]{3,2,1,0:T(8,128)(2,1)} custom-call(bf16[1408,768]{1,0:T(8,128)(2,1)} %collective-permute-done.7.x_ref, bf16[1,64,6144]{2,1,0:T(8,128)(2,1)} %unpack_tokens.2.refs_0_, bf16[1,3,64,6144]{3,2,1,0:T(8,128)(2,1)} %bitcast.7), custom_call_target="tpu_custom_call" | custom-call | flops 1 | bytes 1 | tf_op jit(solution)/shard_map/place/pallas_call | solution.py:312
  222.0 0.1 collective-permute-done.6.x_ref
  222.1 0.7 place_last.1
Async XLA Ops:
  0.6 60.0 %collective-permute-start.4 = (bf16[1,64,6144]{2,1,0:T(8,128)(2,1)}, bf16[1,64,6144]{2,1,0:T(8,128)(2,1)S(1)}, u32[]{:S(2)}, u32[]{:S(2)}) collective-permute-start(bf16[1,64,6144]{2,1,0:T(8,128)(2,1)} %param.15), channel_id=1, source_target_pairs={{0,240},{16,0},{32,16},{48,32},{64,48},{80,64},{96,80},{112,96},{1... | collective-permute-start | bytes 2359304 | tf_op jit(solution)/shard_map/ppermute | solution.py:368
  5.0 154.1 %collective-permute-start = (bf16[1536,768]{1,0:T(8,128)(2,1)}, bf16[1536,768]{1,0:T(8,128)(2,1)S(1)}, u32[]{:S(2)}, u32[]{:S(2)}) collective-permute-start(bf16[1536,768]{1,0:T(8,128)(2,1)} %get-tuple-element.49.refs_3_), channel_id=1, source_target_pairs={{0,240},{16,224},{48,192},{64,176},{96,144},{112,128},{128,112},{1... | collective-permute-start | bytes 7077896 | tf_op jit(solution)/shard_map/ppermute | solution.py:375
  7.5 93.0 %collective-permute-start.1 = (bf16[1280,768]{1,0:T(8,128)(2,1)}, bf16[1280,768]{1,0:T(8,128)(2,1)}, u32[]{:S(2)}, u32[]{:S(2)}) collective-permute-start(bf16[1280,768]{1,0:T(8,128)(2,1)} %get-tuple-element.50), channel_id=1, source_target_pairs={{32,208},{80,160},{160,80},{33,209},{81,161},{161,81},{34,210},{82... | collective-permute-start | bytes 5898248 | tf_op jit(solution)/shard_map/ppermute | solution.py:376
  9.4 3.6 %copy-start.2 = (s32[16]{0:T(128)S(1)}, s32[16]{0:T(128)}, u32[]{:S(2)}) copy-start(s32[16]{0:T(128)} %slot_ref.1) | copy-start | bytes 196
  9.4 87.0 %collective-permute-start.2 = (bf16[256,768]{1,0:T(8,128)(2,1)}, bf16[256,768]{1,0:T(8,128)(2,1)S(1)}, u32[]{:S(2)}, u32[]{:S(2)}) collective-permute-start(bf16[256,768]{1,0:T(8,128)(2,1)} %get-tuple-element.51), channel_id=1, source_target_pairs={{80,64},{160,176},{32,48},{81,65},{161,177},{33,49},{82,66},{162,1... | collective-permute-start | bytes 1179656 | tf_op jit(solution)/shard_map/ppermute | solution.py:373
  14.5 34.6 %all-to-all-start = ((bf16[8,3,64,768]{3,2,1,0:T(8,128)(2,1)}), bf16[8,3,64,768]{3,2,1,0:T(8,128)(2,1)}, u32[]{:S(2)}, u32[]{:S(2)}) async-start(bf16[8,3,64,768]{3,2,1,0:T(8,128)(2,1)} %get-tuple-element.118), calls=%async_computation | async-start | bytes 4718592 | tf_op jit(solution)/shard_map/while/body/all_to_all | solution.py:351
  60.7 0.9 copy-start.3
  63.6 25.9 %all-to-all-start.1 = ((bf16[8,2,64,768]{3,2,1,0:T(8,128)(2,1)}), bf16[8,2,64,768]{3,2,1,0:T(8,128)(2,1)}, u32[]{:S(2)}, u32[]{:S(2)}) async-start(bf16[8,2,64,768]{3,2,1,0:T(8,128)(2,1)} %get-tuple-element.130), calls=%async_computation.1 | async-start | bytes 3145728 | tf_op jit(solution)/shard_map/while/body/all_to_all | solution.py:351
  92.2 8.2 %copy-start.1 = (bf16[8,2,64,768]{3,2,1,0:T(8,128)(2,1)S(1)}, bf16[8,2,64,768]{3,2,1,0:T(8,128)(2,1)}, u32[]{:S(2)}) copy-start(bf16[8,2,64,768]{3,2,1,0:T(8,128)(2,1)} %get-tuple-element.56) | copy-start | bytes 4718596
  93.5 77.8 %collective-permute-start.5 = (bf16[8,64,768]{2,1,0:T(8,128)(2,1)S(1)}, bf16[8,64,768]{2,1,0:T(8,128)(2,1)S(1)}, u32[]{:S(2)}, u32[]{:S(2)}) collective-permute-start(bf16[8,64,768]{2,1,0:T(8,128)(2,1)S(1)} %slice_bitcast_fusion), channel_id=1, source_target_pairs={{0,16},{16,32},{32,48},{48,64},{64,80},{80,96},{96,112},{112,128},... | collective-permute-start | bytes 2359304 | tf_op jit(solution)/shard_map/ppermute | solution.py:381
  96.5 3.9 %collective-permute-start.3 = (bf16[256,768]{1,0:T(8,128)(2,1)S(1)}, bf16[256,768]{1,0:T(8,128)(2,1)S(1)}, u32[]{:S(2)}, u32[]{:S(2)}) collective-permute-start(bf16[256,768]{1,0:T(8,128)(2,1)S(1)} %collective-permute-done.2), channel_id=1, source_target_pairs={{64,160},{176,80},{48,208},{65,161},{177,81},{49,209},{66,162},{17... | collective-permute-start | bytes 1179656 | tf_op jit(solution)/shard_map/ppermute | solution.py:374
  97.2 122.3 %collective-permute-start.7 = (bf16[1408,768]{1,0:T(8,128)(2,1)}, bf16[1408,768]{1,0:T(8,128)(2,1)}, u32[]{:S(2)}, u32[]{:S(2)}) collective-permute-start(bf16[1408,768]{1,0:T(8,128)(2,1)} %get-tuple-element.60), channel_id=1, source_target_pairs={{0,240},{16,224},{32,208},{48,192},{64,176},{80,160},{96,144},{112... | collective-permute-start | bytes 6488072 | tf_op jit(solution)/shard_map/ppermute | solution.py:384
  169.9 1.4 copy-start
  171.3 4.6 %copy-start.4 = (bf16[128,768]{1,0:T(8,128)(2,1)S(1)}, bf16[128,768]{1,0:T(8,128)(2,1)}, u32[]{:S(2)}) copy-start(bf16[128,768]{1,0:T(8,128)(2,1)} %get-tuple-element.59) | copy-start | bytes 589828
  171.3 34.6 %all-to-all-start.2 = ((bf16[8,3,64,768]{3,2,1,0:T(8,128)(2,1)}), bf16[8,3,64,768]{3,2,1,0:T(8,128)(2,1)S(1)}, u32[]{:S(2)}, u32[]{:S(2)}) async-start(bf16[8,3,64,768]{3,2,1,0:T(8,128)(2,1)} %copy-done), calls=%async_computation.2 | async-start | bytes 4718592 | tf_op jit(solution)/shard_map/all_to_all | solution.py:351
  175.9 46.2 %collective-permute-start.6 = (bf16[128,768]{1,0:T(8,128)(2,1)S(1)}, bf16[128,768]{1,0:T(8,128)(2,1)S(1)}, u32[]{:S(2)}, u32[]{:S(2)}) collective-permute-start(bf16[128,768]{1,0:T(8,128)(2,1)S(1)} %copy-done.4), channel_id=1, source_target_pairs={{0,240},{16,224},{32,208},{48,192},{64,176},{80,160},{96,144},{112... | collective-permute-start | bytes 589832 | tf_op jit(solution)/shard_map/ppermute | solution.py:385

commit v6 on v5

--- a/solution.py
+++ b/solution.py
@@ -364,7 +364,7 @@
     parts = lax.axis_size("tensor")
     mirror = [(s, sections - 1 - s) for s in range(sections)]
 
-    once = jnp.minimum(jnp.max(fetch_slot) + 1, 1)
+    once = jnp.minimum(fetch_slot[0] + 1, 1)
     upstream = lax.ppermute(cotangent, "pipe", [(s, (s - 1) % sections) for s in range(sections)])
     half = sections // 2
     shared = [half - 3, half + 2, 2]

time: 227 us -> 227 us (level)
  transfers between devices with their start and end apart: 11 -> 11, of which waited for: 6 -> 6; matrix products, arithmetic and copies ran while one was open for 4% -> 3% of each run, Pallas kernels for 15% -> 15%
where the time goes in v6:
time: 227 us; the launch traced here: 223 us
  waiting for transfers between devices  148 us (65%)
  Pallas kernels  33.6 us (15%)
  starting transfers between devices  31.1 us (14%)
  local copies, waits for them, and re-layouts  9.7 us (4%)
    all_to_all x3, waiting for transfers between devices, exchange(): return lax.all_to_all(x, 'tensor', split_axis=0, concat_axis=0, tiled=True)  76 us
    ppermute x1, waiting for transfers between devices, on_device(): lax.ppermute(held, 'pipe', [(s, t) for s, t in mirror if s not in shared])  60 us
    all_to_all x3, starting transfers between devices, exchange(): return lax.all_to_all(x, 'tensor', split_axis=0, concat_axis=0, tiled=True)  13.4 us
    ppermute x1, waiting for transfers between devices, on_device(): moved = lax.ppermute(block, 'pipe', mirror)  11.4 us
    pallas_call x1, Pallas kernels, backward_core(): pl.pallas_call(kernel, grid=(feat // HD,), in_specs=[pl.BlockSpec((x.shap...  10.8 us
    pallas_call x1, Pallas kernels, forward_core(): pl.pallas_call(_forward_kernel, grid=(feat // HD,), in_specs=[pl.BlockSpe...  8.23 us
    pallas_call x3, Pallas kernels, _move(): pl.pallas_call(kernel, in_specs=in_specs or [HBM] * len(inputs), out_spec...  6.1 us
    while x2, local copies, waits for them, and re-layouts  6.06 us
  transfers between devices with their start and end apart: 11, of which 6 were waited for; matrix products, arithmetic and copies ran while one was open for 3% of the time, Pallas kernels for 15%

profile of v6, /device:TPU:128, one launch (start us, length us, event | category | flops | bytes accessed | tf_op | source)
XLA Modules:
  0.0 222.8 jit_solution(14929534425446222878)
XLA Ops:
  0.6 1.1 collective-permute-start.4
  1.7 3.3 %held_block.1 = (bf16[1536,768]{1,0:T(8,128)(2,1)}, bf16[1280,768]{1,0:T(8,128)(2,1)}, bf16[256,768]{1,0:T(8,128)(2,1)}) custom-call(s32[16]{0:T(128)} %slot_ref.1, bf16[1,2,3,512,768]{4,3,2,1,0:T(8,128)(2,1)} %stash_ref.1), custom_call_target="tpu_custom_call" | custom-call | flops 1 | bytes 1 | tf_op jit(solution)/shard_map/held_block/pallas_call | solution.py:160
  5.0 2.4 %collective-permute-start = (bf16[1536,768]{1,0:T(8,128)(2,1)}, bf16[1536,768]{1,0:T(8,128)(2,1)S(1)}, u32[]{:S(2)}, u32[]{:S(2)}) collective-permute-start(bf16[1536,768]{1,0:T(8,128)(2,1)} %get-tuple-element.49.refs_3_), channel_id=1, source_target_pairs={{0,240},{16,224},{48,192},{64,176},{96,144},{112,128},{128,112},{1... | collective-permute-start | bytes 7077896 | tf_op jit(solution)/shard_map/ppermute | solution.py:375
  7.5 2.0 collective-permute-start.1
  9.4 0.0 copy-start.2
  9.4 0.8 collective-permute-start.2
  10.3 2.8 %pack_tokens.1 = bf16[8,3,64,768]{3,2,1,0:T(8,128)(2,1)} custom-call(bf16[1,64,6144]{2,1,0:T(8,128)(2,1)} %refs_0_.1, bf16[1,64,6144]{2,1,0:T(8,128)(2,1)} %refs_1_.1, bf16[1,64,6144]{2,1,0:T(8,128)(2,1)} %refs_2_.1, bf16[1536,768]{1,0:T(8,128)(2,1)} %get-tuple-element.49.refs_3_), custom_call_target="tpu_custom_call" | custom-call | flops 1 | bytes 1 | tf_op jit(solution)/shard_map/pack_tokens/pallas_call | solution.py:87
  13.1 0.0 copy-done.2
  13.1 37.9 %while.20 = (s32[]{:T(128)}, bf16[8,3,64,768]{3,2,1,0:T(8,128)(2,1)}, s32[]{:T(128)}, s32[]{:T(128)}) while((s32[]{:T(128)}, bf16[8,3,64,768]{3,2,1,0:T(8,128)(2,1)}, s32[]{:T(128)}, s32[]{:T(128)}) %tuple.39), condition=%wide.region_1.0_spmd, body=%wide.region_0.0_spmd.sunk | while | flops 2 | bytes 11796565 | solution.py:358
  13.1 4.5 %all-to-all-start = ((bf16[8,3,64,768]{3,2,1,0:T(8,128)(2,1)}), bf16[8,3,64,768]{3,2,1,0:T(8,128)(2,1)}, u32[]{:S(2)}, u32[]{:S(2)}) async-start(bf16[8,3,64,768]{3,2,1,0:T(8,128)(2,1)} %get-tuple-element.118), calls=%async_computation | async-start | bytes 4718592 | tf_op jit(solution)/shard_map/while/body/all_to_all | solution.py:351
  17.6 30.1 %all-to-all-done = bf16[8,3,64,768]{3,2,1,0:T(8,128)(2,1)} async-done(((bf16[8,3,64,768]{3,2,1,0:T(8,128)(2,1)}), bf16[8,3,64,768]{3,2,1,0:T(8,128)(2,1)}, u32[]{:S(2)}, u32[]{:S(2)}) %all-to-all-start) | async-done | bytes 2359328 | tf_op jit(solution)/shard_map/while/body/all_to_all | solution.py:351
  47.7 3.3 %copy.22 = bf16[8,3,64,768]{3,2,1,0:T(8,128)(2,1)} copy(bf16[8,3,64,768]{3,2,1,0:T(8,128)(2,1)} %all-to-all-done) | data formatting | bytes 4718592 | tf_op jit(solution)/shard_map/while
  51.0 8.2 %forward_core.1 = (bf16[8,2,64,768]{3,2,1,0:T(8,128)(2,1)}, bf16[1408,768]{1,0:T(8,128)(2,1)}, bf16[128,768]{1,0:T(8,128)(2,1)}) custom-call(bf16[8,3,64,768]{3,2,1,0:T(8,128)(2,1)} %get-tuple-element.52.x_ref), custom_call_target="tpu_custom_call" | custom-call | flops 1 | bytes 1 | tf_op jit(solution)/shard_map/forward_core/pallas_call | solution.py:226
  59.3 0.0 collective-permute-done.4.up_ref
  59.3 0.0 copy-start.3
  59.3 0.9 copy-done.3
  60.1 2.0 pack_beside.1
  62.1 28.7 %while.21 = (s32[]{:T(128)}, bf16[8,2,64,768]{3,2,1,0:T(8,128)(2,1)}, s32[]{:T(128)}, s32[]{:T(128)}) while((s32[]{:T(128)}, bf16[8,2,64,768]{3,2,1,0:T(8,128)(2,1)}, s32[]{:T(128)}, s32[]{:T(128)}) %tuple.42), condition=%wide.region_3.0_spmd, body=%wide.region_2.0_spmd.sunk | while | flops 2 | bytes 7864405 | solution.py:358
  62.2 4.3 %all-to-all-start.1 = ((bf16[8,2,64,768]{3,2,1,0:T(8,128)(2,1)}), bf16[8,2,64,768]{3,2,1,0:T(8,128)(2,1)}, u32[]{:S(2)}, u32[]{:S(2)}) async-start(bf16[8,2,64,768]{3,2,1,0:T(8,128)(2,1)} %get-tuple-element.130), calls=%async_computation.1 | async-start | bytes 3145728 | tf_op jit(solution)/shard_map/while/body/all_to_all | solution.py:351
  66.5 21.6 %all-to-all-done.1 = bf16[8,2,64,768]{3,2,1,0:T(8,128)(2,1)} async-done(((bf16[8,2,64,768]{3,2,1,0:T(8,128)(2,1)}), bf16[8,2,64,768]{3,2,1,0:T(8,128)(2,1)}, u32[]{:S(2)}, u32[]{:S(2)}) %all-to-all-start.1) | async-done | bytes 1572896 | tf_op jit(solution)/shard_map/while/body/all_to_all | solution.py:351
  88.1 2.8 %copy.29 = bf16[8,2,64,768]{3,2,1,0:T(8,128)(2,1)} copy(bf16[8,2,64,768]{3,2,1,0:T(8,128)(2,1)} %all-to-all-done.1) | data formatting | bytes 3145728 | tf_op jit(solution)/shard_map/while
  90.8 0.0 copy-start.1
  90.8 1.3 slice_bitcast_fusion
  92.1 2.9 %collective-permute-start.5 = (bf16[8,64,768]{2,1,0:T(8,128)(2,1)S(1)}, bf16[8,64,768]{2,1,0:T(8,128)(2,1)S(1)}, u32[]{:S(2)}, u32[]{:S(2)}) collective-permute-start(bf16[8,64,768]{2,1,0:T(8,128)(2,1)S(1)} %slice_bitcast_fusion), channel_id=1, source_target_pairs={{0,16},{16,32},{32,48},{48,64},{64,80},{80,96},{96,112},{112,128},... | collective-permute-start | bytes 2359304 | tf_op jit(solution)/shard_map/ppermute | solution.py:381
  95.1 0.0 collective-permute-done.2
  95.1 0.7 collective-permute-start.3
  95.8 3.2 %collective-permute-start.7 = (bf16[1408,768]{1,0:T(8,128)(2,1)}, bf16[1408,768]{1,0:T(8,128)(2,1)}, u32[]{:S(2)}, u32[]{:S(2)}) collective-permute-start(bf16[1408,768]{1,0:T(8,128)(2,1)} %get-tuple-element.60), channel_id=1, source_target_pairs={{0,240},{16,224},{32,208},{48,192},{64,176},{80,160},{96,144},{112... | collective-permute-start | bytes 6488072 | tf_op jit(solution)/shard_map/ppermute | solution.py:384
  99.0 0.0 copy-done.1
  99.0 0.1 slice_bitcast_fusion.1.g_ref
  99.0 0.0 collective-permute-done.3.e_ref
  99.0 0.0 collective-permute-done.1.m_ref
  99.1 60.0 %collective-permute-done.w_ref = bf16[1536,768]{1,0:T(8,128)(2,1)S(1)} collective-permute-done((bf16[1536,768]{1,0:T(8,128)(2,1)}, bf16[1536,768]{1,0:T(8,128)(2,1)S(1)}, u32[]{:S(2)}, u32[]{:S(2)}) %collective-permute-start) | collective-permute-done | bytes 2359328 | tf_op jit(solution)/shard_map/ppermute | solution.py:375
  159.1 10.8 %backward_core.1 = bf16[8,3,64,768]{3,2,1,0:T(8,128)(2,1)S(1)} custom-call(bf16[1536,768]{1,0:T(8,128)(2,1)S(1)} %collective-permute-done.w_ref, bf16[1280,768]{1,0:T(8,128)(2,1)} %collective-permute-done.1.m_ref, bf16[256,768]{1,0:T(8,128)(2,1)S(1)} %collective-permute-done.3.e_ref, bf16[8,64,768]{2,1,0:T(8,128)(2,1)S(1)} %slice_bitcast_fusion.1.g_ref), custom_call_target="tpu_custom_call" | custom-call | flops 1 | bytes 1 | tf_op jit(solution)/shard_map/backward_core/pallas_call | solution.py:274
  169.9 0.0 copy-start
  169.9 1.4 copy-done
  171.3 0.0 copy-start.4
  171.3 0.0 collective-permute-done.5
  171.3 4.6 %all-to-all-start.2 = ((bf16[8,3,64,768]{3,2,1,0:T(8,128)(2,1)}), bf16[8,3,64,768]{3,2,1,0:T(8,128)(2,1)S(1)}, u32[]{:S(2)}, u32[]{:S(2)}) async-start(bf16[8,3,64,768]{3,2,1,0:T(8,128)(2,1)} %copy-done), calls=%async_computation.2 | async-start | bytes 4718592 | tf_op jit(solution)/shard_map/all_to_all | solution.py:351
  175.9 0.0 copy-done.4
  175.9 4.6 %collective-permute-start.6 = (bf16[128,768]{1,0:T(8,128)(2,1)S(1)}, bf16[128,768]{1,0:T(8,128)(2,1)S(1)}, u32[]{:S(2)}, u32[]{:S(2)}) collective-permute-start(bf16[128,768]{1,0:T(8,128)(2,1)S(1)} %copy-done.4), channel_id=1, source_target_pairs={{0,240},{16,224},{32,208},{48,192},{64,176},{80,160},{96,144},{112... | collective-permute-start | bytes 589832 | tf_op jit(solution)/shard_map/ppermute | solution.py:385
  180.5 1.1 unpack_tokens.2.refs_0_
  181.6 24.3 %all-to-all-done.2.x_ref = bf16[8,3,64,768]{3,2,1,0:T(8,128)(2,1)S(1)} async-done(((bf16[8,3,64,768]{3,2,1,0:T(8,128)(2,1)}), bf16[8,3,64,768]{3,2,1,0:T(8,128)(2,1)S(1)}, u32[]{:S(2)}, u32[]{:S(2)}) %all-to-all-start.2) | async-done | bytes 2359328 | tf_op jit(solution)/shard_map/all_to_all | solution.py:351
  205.9 2.2 unpack_tokens.3
  208.1 11.4 %collective-permute-done.7.x_ref = bf16[1408,768]{1,0:T(8,128)(2,1)} collective-permute-done((bf16[1408,768]{1,0:T(8,128)(2,1)}, bf16[1408,768]{1,0:T(8,128)(2,1)}, u32[]{:S(2)}, u32[]{:S(2)}) %collective-permute-start.7) | collective-permute-done | bytes 2162720 | tf_op jit(solution)/shard_map/ppermute | solution.py:384
  219.4 2.5 %place.1._ = bf16[1,3,512,768]{3,2,1,0:T(8,128)(2,1)} custom-call(bf16[1408,768]{1,0:T(8,128)(2,1)} %collective-permute-done.7.x_ref, bf16[1,64,6144]{2,1,0:T(8,128)(2,1)} %unpack_tokens.2.refs_0_, bf16[1,3,64,6144]{3,2,1,0:T(8,128)(2,1)} %bitcast.9), custom_call_target="tpu_custom_call" | custom-call | flops 1 | bytes 1 | tf_op jit(solution)/shard_map/place/pallas_call | solution.py:312
  222.0 0.1 collective-permute-done.6.x_ref
  222.1 0.7 place_last.1
Async XLA Ops:
  0.6 58.6 %collective-permute-start.4 = (bf16[1,64,6144]{2,1,0:T(8,128)(2,1)}, bf16[1,64,6144]{2,1,0:T(8,128)(2,1)S(1)}, u32[]{:S(2)}, u32[]{:S(2)}) collective-permute-start(bf16[1,64,6144]{2,1,0:T(8,128)(2,1)} %param.15), channel_id=1, source_target_pairs={{0,240},{16,0},{32,16},{48,32},{64,48},{80,64},{96,80},{112,96},{1... | collective-permute-start | bytes 2359304 | tf_op jit(solution)/shard_map/ppermute | solution.py:368
  5.0 154.1 %collective-permute-start = (bf16[1536,768]{1,0:T(8,128)(2,1)}, bf16[1536,768]{1,0:T(8,128)(2,1)S(1)}, u32[]{:S(2)}, u32[]{:S(2)}) collective-permute-start(bf16[1536,768]{1,0:T(8,128)(2,1)} %get-tuple-element.49.refs_3_), channel_id=1, source_target_pairs={{0,240},{16,224},{48,192},{64,176},{96,144},{112,128},{128,112},{1... | collective-permute-start | bytes 7077896 | tf_op jit(solution)/shard_map/ppermute | solution.py:375
  7.5 91.6 %collective-permute-start.1 = (bf16[1280,768]{1,0:T(8,128)(2,1)}, bf16[1280,768]{1,0:T(8,128)(2,1)}, u32[]{:S(2)}, u32[]{:S(2)}) collective-permute-start(bf16[1280,768]{1,0:T(8,128)(2,1)} %get-tuple-element.50), channel_id=1, source_target_pairs={{32,208},{80,160},{160,80},{33,209},{81,161},{161,81},{34,210},{82... | collective-permute-start | bytes 5898248 | tf_op jit(solution)/shard_map/ppermute | solution.py:376
  9.4 3.6 %copy-start.2 = (s32[16]{0:T(128)S(1)}, s32[16]{0:T(128)}, u32[]{:S(2)}) copy-start(s32[16]{0:T(128)} %slot_ref.1) | copy-start | bytes 196
  9.4 85.6 %collective-permute-start.2 = (bf16[256,768]{1,0:T(8,128)(2,1)}, bf16[256,768]{1,0:T(8,128)(2,1)S(1)}, u32[]{:S(2)}, u32[]{:S(2)}) collective-permute-start(bf16[256,768]{1,0:T(8,128)(2,1)} %get-tuple-element.51), channel_id=1, source_target_pairs={{80,64},{160,176},{32,48},{81,65},{161,177},{33,49},{82,66},{162,1... | collective-permute-start | bytes 1179656 | tf_op jit(solution)/shard_map/ppermute | solution.py:373
  13.1 34.6 %all-to-all-start = ((bf16[8,3,64,768]{3,2,1,0:T(8,128)(2,1)}), bf16[8,3,64,768]{3,2,1,0:T(8,128)(2,1)}, u32[]{:S(2)}, u32[]{:S(2)}) async-start(bf16[8,3,64,768]{3,2,1,0:T(8,128)(2,1)} %get-tuple-element.118), calls=%async_computation | async-start | bytes 4718592 | tf_op jit(solution)/shard_map/while/body/all_to_all | solution.py:351
  59.3 0.9 copy-start.3
  62.2 25.9 %all-to-all-start.1 = ((bf16[8,2,64,768]{3,2,1,0:T(8,128)(2,1)}), bf16[8,2,64,768]{3,2,1,0:T(8,128)(2,1)}, u32[]{:S(2)}, u32[]{:S(2)}) async-start(bf16[8,2,64,768]{3,2,1,0:T(8,128)(2,1)} %get-tuple-element.130), calls=%async_computation.1 | async-start | bytes 3145728 | tf_op jit(solution)/shard_map/while/body/all_to_all | solution.py:351
  90.8 8.2 %copy-start.1 = (bf16[8,2,64,768]{3,2,1,0:T(8,128)(2,1)S(1)}, bf16[8,2,64,768]{3,2,1,0:T(8,128)(2,1)}, u32[]{:S(2)}) copy-start(bf16[8,2,64,768]{3,2,1,0:T(8,128)(2,1)} %get-tuple-element.56) | copy-start | bytes 4718596
  92.1 79.1 %collective-permute-start.5 = (bf16[8,64,768]{2,1,0:T(8,128)(2,1)S(1)}, bf16[8,64,768]{2,1,0:T(8,128)(2,1)S(1)}, u32[]{:S(2)}, u32[]{:S(2)}) collective-permute-start(bf16[8,64,768]{2,1,0:T(8,128)(2,1)S(1)} %slice_bitcast_fusion), channel_id=1, source_target_pairs={{0,16},{16,32},{32,48},{48,64},{64,80},{80,96},{96,112},{112,128},... | collective-permute-start | bytes 2359304 | tf_op jit(solution)/shard_map/ppermute | solution.py:381
  95.1 3.9 %collective-permute-start.3 = (bf16[256,768]{1,0:T(8,128)(2,1)S(1)}, bf16[256,768]{1,0:T(8,128)(2,1)S(1)}, u32[]{:S(2)}, u32[]{:S(2)}) collective-permute-start(bf16[256,768]{1,0:T(8,128)(2,1)S(1)} %collective-permute-done.2), channel_id=1, source_target_pairs={{64,160},{176,80},{48,208},{65,161},{177,81},{49,209},{66,162},{17... | collective-permute-start | bytes 1179656 | tf_op jit(solution)/shard_map/ppermute | solution.py:374
  95.8 123.7 %collective-permute-start.7 = (bf16[1408,768]{1,0:T(8,128)(2,1)}, bf16[1408,768]{1,0:T(8,128)(2,1)}, u32[]{:S(2)}, u32[]{:S(2)}) collective-permute-start(bf16[1408,768]{1,0:T(8,128)(2,1)} %get-tuple-element.60), channel_id=1, source_target_pairs={{0,240},{16,224},{32,208},{48,192},{64,176},{80,160},{96,144},{112... | collective-permute-start | bytes 6488072 | tf_op jit(solution)/shard_map/ppermute | solution.py:384
  169.9 1.4 copy-start
  171.3 4.6 %copy-start.4 = (bf16[128,768]{1,0:T(8,128)(2,1)S(1)}, bf16[128,768]{1,0:T(8,128)(2,1)}, u32[]{:S(2)}) copy-start(bf16[128,768]{1,0:T(8,128)(2,1)} %get-tuple-element.59) | copy-start | bytes 589828
  171.3 34.6 %all-to-all-start.2 = ((bf16[8,3,64,768]{3,2,1,0:T(8,128)(2,1)}), bf16[8,3,64,768]{3,2,1,0:T(8,128)(2,1)S(1)}, u32[]{:S(2)}, u32[]{:S(2)}) async-start(bf16[8,3,64,768]{3,2,1,0:T(8,128)(2,1)} %copy-done), calls=%async_computation.2 | async-start | bytes 4718592 | tf_op jit(solution)/shard_map/all_to_all | solution.py:351
  175.9 46.2 %collective-permute-start.6 = (bf16[128,768]{1,0:T(8,128)(2,1)S(1)}, bf16[128,768]{1,0:T(8,128)(2,1)S(1)}, u32[]{:S(2)}, u32[]{:S(2)}) collective-permute-start(bf16[128,768]{1,0:T(8,128)(2,1)S(1)} %copy-done.4), channel_id=1, source_target_pairs={{0,240},{16,224},{32,208},{48,192},{64,176},{80,160},{96,144},{112... | collective-permute-start | bytes 589832 | tf_op jit(solution)/shard_map/ppermute | solution.py:385

commit v7 on v6

--- a/solution.py
+++ b/solution.py
@@ -279,7 +279,7 @@
         out_specs=pl.BlockSpec((parts, 3, rows, HD), lambda h: (0, 0, 0, h)),
         out_shape=jax.ShapeDtypeStruct((parts, 3, rows, feat), jnp.bfloat16),
         scratch_shapes=[pltpu.VMEM((3 * length, HD), jnp.bfloat16)] + [pltpu.VMEM((length, HD), jnp.float32)] * 2,
-        compiler_params=pltpu.CompilerParams(vmem_limit_bytes=24 * 2**20),
+        compiler_params=pltpu.CompilerParams(vmem_limit_bytes=FULL),
         cost_estimate=SMALL,
         name="backward_core",
     )(whole, main, end, upstream)

time: 227 us -> 227 us (level)
  local copies, waits for them, and re-layouts: 9.7 us -> 6.69 us
  waiting for transfers between devices: 148 us -> 151 us
    while x2, local copies, waits for them, and re-layouts: 6.06 us -> 2.55 us
    ppermute x1, waiting for transfers between devices: 60 us -> 62.5 us  [on_device(): lax.ppermute(held, 'pipe', [(s, t) for s, t in mirror if s not in shared])]
where the time goes in v7:
time: 227 us; the launch traced here: 223 us
  waiting for transfers between devices  151 us (67%)
  Pallas kernels  33.9 us (15%)
  starting transfers between devices  30.5 us (13%)
  local copies, waits for them, and re-layouts  6.69 us (3%)
    all_to_all x3, waiting for transfers between devices, exchange(): return lax.all_to_all(x, 'tensor', split_axis=0, concat_axis=0, tiled=True)  75.7 us
    ppermute x1, waiting for transfers between devices, on_device(): lax.ppermute(held, 'pipe', [(s, t) for s, t in mirror if s not in shared])  62.5 us
    all_to_all x3, starting transfers between devices, exchange(): return lax.all_to_all(x, 'tensor', split_axis=0, concat_axis=0, tiled=True)  12.7 us
    ppermute x1, waiting for transfers between devices, on_device(): moved = lax.ppermute(block, 'pipe', mirror)  12.5 us
    pallas_call x1, Pallas kernels, backward_core(): pl.pallas_call(kernel, grid=(feat // HD,), in_specs=[pl.BlockSpec((x.shap...  11 us
    pallas_call x1, Pallas kernels, forward_core(): pl.pallas_call(_forward_kernel, grid=(feat // HD,), in_specs=[pl.BlockSpe...  8.27 us
    pallas_call x3, Pallas kernels, _move(): pl.pallas_call(kernel, in_specs=in_specs or [HBM] * len(inputs), out_spec...  6.1 us
    ppermute x1, starting transfers between devices, on_device(): last = lax.ppermute(last, 'pipe', mirror)  4.64 us
  transfers between devices with their start and end apart: 11, of which 6 were waited for; matrix products, arithmetic and copies ran while one was open for 3% of the time, Pallas kernels for 15%

profile of v7, /device:TPU:128, one launch (start us, length us, event | category | flops | bytes accessed | tf_op | source)
XLA Modules:
  0.0 222.8 jit_solution(16436909344923888949)
XLA Ops:
  0.6 1.1 collective-permute-start.4
  1.7 3.3 %held_block.1 = (bf16[1536,768]{1,0:T(8,128)(2,1)}, bf16[1280,768]{1,0:T(8,128)(2,1)}, bf16[256,768]{1,0:T(8,128)(2,1)}) custom-call(s32[16]{0:T(128)} %slot_ref.1, bf16[1,2,3,512,768]{4,3,2,1,0:T(8,128)(2,1)} %stash_ref.1), custom_call_target="tpu_custom_call" | custom-call | flops 1 | bytes 1 | tf_op jit(solution)/shard_map/held_block/pallas_call | solution.py:160
  5.0 2.4 %collective-permute-start = (bf16[1536,768]{1,0:T(8,128)(2,1)}, bf16[1536,768]{1,0:T(8,128)(2,1)}, u32[]{:S(2)}, u32[]{:S(2)}) collective-permute-start(bf16[1536,768]{1,0:T(8,128)(2,1)} %get-tuple-element.49.refs_3_), channel_id=1, source_target_pairs={{0,240},{16,224},{48,192},{64,176},{96,144},{112,128},{128,112},{1... | collective-permute-start | bytes 7077896 | tf_op jit(solution)/shard_map/ppermute | solution.py:375
  7.5 2.0 collective-permute-start.1
  9.5 0.0 copy-start.1
  9.5 0.8 collective-permute-start.2
  10.3 2.8 %pack_tokens.1 = bf16[8,3,64,768]{3,2,1,0:T(8,128)(2,1)} custom-call(bf16[1,64,6144]{2,1,0:T(8,128)(2,1)} %refs_0_.1, bf16[1,64,6144]{2,1,0:T(8,128)(2,1)} %refs_1_.1, bf16[1,64,6144]{2,1,0:T(8,128)(2,1)} %refs_2_.1, bf16[1536,768]{1,0:T(8,128)(2,1)} %get-tuple-element.49.refs_3_), custom_call_target="tpu_custom_call" | custom-call | flops 1 | bytes 1 | tf_op jit(solution)/shard_map/pack_tokens/pallas_call | solution.py:87
  13.1 0.0 copy-done.1
  13.1 35.9 %while.20 = (s32[]{:T(128)}, bf16[8,3,64,768]{3,2,1,0:T(8,128)(2,1)}, s32[]{:T(128)}, s32[]{:T(128)}) while((s32[]{:T(128)}, bf16[8,3,64,768]{3,2,1,0:T(8,128)(2,1)}, s32[]{:T(128)}, s32[]{:T(128)}) %tuple.39), condition=%wide.region_1.0_spmd, body=%wide.region_0.0_spmd.sunk | while | flops 2 | bytes 11796565 | solution.py:358
  13.1 4.5 %all-to-all-start = ((bf16[8,3,64,768]{3,2,1,0:T(8,128)(2,1)}), bf16[8,3,64,768]{3,2,1,0:T(8,128)(2,1)S(1)}, u32[]{:S(2)}, u32[]{:S(2)}) async-start(bf16[8,3,64,768]{3,2,1,0:T(8,128)(2,1)} %get-tuple-element.118), calls=%async_computation | async-start | bytes 4718592 | tf_op jit(solution)/shard_map/while/body/all_to_all | solution.py:351
  17.6 30.0 %all-to-all-done = bf16[8,3,64,768]{3,2,1,0:T(8,128)(2,1)S(1)} async-done(((bf16[8,3,64,768]{3,2,1,0:T(8,128)(2,1)}), bf16[8,3,64,768]{3,2,1,0:T(8,128)(2,1)S(1)}, u32[]{:S(2)}, u32[]{:S(2)}) %all-to-all-start) | async-done | bytes 2359328 | tf_op jit(solution)/shard_map/while/body/all_to_all | solution.py:351
  47.6 1.4 copy.22
  49.0 8.3 %forward_core.1 = (bf16[8,2,64,768]{3,2,1,0:T(8,128)(2,1)}, bf16[1408,768]{1,0:T(8,128)(2,1)}, bf16[128,768]{1,0:T(8,128)(2,1)}) custom-call(bf16[8,3,64,768]{3,2,1,0:T(8,128)(2,1)} %get-tuple-element.52.x_ref), custom_call_target="tpu_custom_call" | custom-call | flops 1 | bytes 1 | tf_op jit(solution)/shard_map/forward_core/pallas_call | solution.py:226
  57.3 0.0 collective-permute-done.4.up_ref
  57.3 0.0 copy-start.2
  57.3 0.9 copy-done.2
  58.2 2.0 pack_beside.1
  60.2 26.3 %while.21 = (s32[]{:T(128)}, bf16[8,2,64,768]{3,2,1,0:T(8,128)(2,1)}, s32[]{:T(128)}, s32[]{:T(128)}) while((s32[]{:T(128)}, bf16[8,2,64,768]{3,2,1,0:T(8,128)(2,1)}, s32[]{:T(128)}, s32[]{:T(128)}) %tuple.42), condition=%wide.region_3.0_spmd, body=%wide.region_2.0_spmd.sunk | while | flops 2 | bytes 7864405 | solution.py:358
  60.2 3.6 %all-to-all-start.1 = ((bf16[8,2,64,768]{3,2,1,0:T(8,128)(2,1)}), bf16[8,2,64,768]{3,2,1,0:T(8,128)(2,1)S(1)}, u32[]{:S(2)}, u32[]{:S(2)}) async-start(bf16[8,2,64,768]{3,2,1,0:T(8,128)(2,1)} %get-tuple-element.130), calls=%async_computation.1 | async-start | bytes 3145728 | tf_op jit(solution)/shard_map/while/body/all_to_all | solution.py:351
  63.8 21.5 %all-to-all-done.1 = bf16[8,2,64,768]{3,2,1,0:T(8,128)(2,1)S(1)} async-done(((bf16[8,2,64,768]{3,2,1,0:T(8,128)(2,1)}), bf16[8,2,64,768]{3,2,1,0:T(8,128)(2,1)S(1)}, u32[]{:S(2)}, u32[]{:S(2)}) %all-to-all-start.1) | async-done | bytes 1572896 | tf_op jit(solution)/shard_map/while/body/all_to_all | solution.py:351
  85.3 1.1 copy.29
  86.5 1.2 slice_bitcast_fusion
  87.7 2.9 %collective-permute-start.5 = (bf16[8,64,768]{2,1,0:T(8,128)(2,1)S(1)}, bf16[8,64,768]{2,1,0:T(8,128)(2,1)S(1)}, u32[]{:S(2)}, u32[]{:S(2)}) collective-permute-start(bf16[8,64,768]{2,1,0:T(8,128)(2,1)S(1)} %slice_bitcast_fusion), channel_id=1, source_target_pairs={{0,16},{16,32},{32,48},{48,64},{64,80},{80,96},{96,112},{112,128},... | collective-permute-start | bytes 2359304 | tf_op jit(solution)/shard_map/ppermute | solution.py:381
  90.6 0.0 collective-permute-done.2
  90.6 0.7 collective-permute-start.3
  91.3 3.2 %collective-permute-start.7 = (bf16[1408,768]{1,0:T(8,128)(2,1)}, bf16[1408,768]{1,0:T(8,128)(2,1)}, u32[]{:S(2)}, u32[]{:S(2)}) collective-permute-start(bf16[1408,768]{1,0:T(8,128)(2,1)} %get-tuple-element.60), channel_id=1, source_target_pairs={{0,240},{16,224},{32,208},{48,192},{64,176},{80,160},{96,144},{112... | collective-permute-start | bytes 6488072 | tf_op jit(solution)/shard_map/ppermute | solution.py:384
  94.5 2.1 slice_bitcast_fusion.1.g_ref
  96.6 0.0 collective-permute-done.3.e_ref
  96.6 0.0 copy-start
  96.6 0.0 collective-permute-done.1.m_ref
  96.6 62.5 %collective-permute-done.w_ref = bf16[1536,768]{1,0:T(8,128)(2,1)} collective-permute-done((bf16[1536,768]{1,0:T(8,128)(2,1)}, bf16[1536,768]{1,0:T(8,128)(2,1)}, u32[]{:S(2)}, u32[]{:S(2)}) %collective-permute-start) | collective-permute-done | bytes 2359328 | tf_op jit(solution)/shard_map/ppermute | solution.py:375
  159.1 0.0 copy-done
  159.1 11.0 %backward_core.1 = bf16[8,3,64,768]{3,2,1,0:T(8,128)(2,1)} custom-call(bf16[1536,768]{1,0:T(8,128)(2,1)} %collective-permute-done.w_ref, bf16[1280,768]{1,0:T(8,128)(2,1)} %collective-permute-done.1.m_ref, bf16[256,768]{1,0:T(8,128)(2,1)} %copy-done, bf16[8,64,768]{2,1,0:T(8,128)(2,1)} %slice_bitcast_fusion.1.g_ref), custom_call_target="tpu_custom_call" | custom-call | flops 1 | bytes 1 | tf_op jit(solution)/shard_map/backward_core/pallas_call | solution.py:274
  170.1 0.0 copy-start.3
  170.1 0.0 collective-permute-done.5
  170.1 4.7 %all-to-all-start.2 = ((bf16[8,3,64,768]{3,2,1,0:T(8,128)(2,1)}), bf16[8,3,64,768]{3,2,1,0:T(8,128)(2,1)S(1)}, u32[]{:S(2)}, u32[]{:S(2)}) async-start(bf16[8,3,64,768]{3,2,1,0:T(8,128)(2,1)} %backward_core.1), calls=%async_computation.2 | async-start | bytes 4718592 | tf_op jit(solution)/shard_map/all_to_all | solution.py:351
  174.7 0.0 copy-done.3
  174.7 4.6 %collective-permute-start.6 = (bf16[128,768]{1,0:T(8,128)(2,1)S(1)}, bf16[128,768]{1,0:T(8,128)(2,1)S(1)}, u32[]{:S(2)}, u32[]{:S(2)}) collective-permute-start(bf16[128,768]{1,0:T(8,128)(2,1)S(1)} %copy-done.3), channel_id=1, source_target_pairs={{0,240},{16,224},{32,208},{48,192},{64,176},{80,160},{96,144},{112... | collective-permute-start | bytes 589832 | tf_op jit(solution)/shard_map/ppermute | solution.py:385
  179.4 1.1 unpack_tokens.2.refs_0_
  180.5 24.2 %all-to-all-done.2.x_ref = bf16[8,3,64,768]{3,2,1,0:T(8,128)(2,1)S(1)} async-done(((bf16[8,3,64,768]{3,2,1,0:T(8,128)(2,1)}), bf16[8,3,64,768]{3,2,1,0:T(8,128)(2,1)S(1)}, u32[]{:S(2)}, u32[]{:S(2)}) %all-to-all-start.2) | async-done | bytes 2359328 | tf_op jit(solution)/shard_map/all_to_all | solution.py:351
  204.7 2.2 unpack_tokens.3
  206.9 12.5 %collective-permute-done.7.x_ref = bf16[1408,768]{1,0:T(8,128)(2,1)} collective-permute-done((bf16[1408,768]{1,0:T(8,128)(2,1)}, bf16[1408,768]{1,0:T(8,128)(2,1)}, u32[]{:S(2)}, u32[]{:S(2)}) %collective-permute-start.7) | collective-permute-done | bytes 2162720 | tf_op jit(solution)/shard_map/ppermute | solution.py:384
  219.4 2.5 %place.1._ = bf16[1,3,512,768]{3,2,1,0:T(8,128)(2,1)} custom-call(bf16[1408,768]{1,0:T(8,128)(2,1)} %collective-permute-done.7.x_ref, bf16[1,64,6144]{2,1,0:T(8,128)(2,1)} %unpack_tokens.2.refs_0_, bf16[1,3,64,6144]{3,2,1,0:T(8,128)(2,1)} %bitcast.9), custom_call_target="tpu_custom_call" | custom-call | flops 1 | bytes 1 | tf_op jit(solution)/shard_map/place/pallas_call | solution.py:312
  222.0 0.1 collective-permute-done.6.x_ref
  222.1 0.7 place_last.1
Async XLA Ops:
  0.6 56.7 %collective-permute-start.4 = (bf16[1,64,6144]{2,1,0:T(8,128)(2,1)}, bf16[1,64,6144]{2,1,0:T(8,128)(2,1)S(1)}, u32[]{:S(2)}, u32[]{:S(2)}) collective-permute-start(bf16[1,64,6144]{2,1,0:T(8,128)(2,1)} %param.15), channel_id=1, source_target_pairs={{0,240},{16,0},{32,16},{48,32},{64,48},{80,64},{96,80},{112,96},{1... | collective-permute-start | bytes 2359304 | tf_op jit(solution)/shard_map/ppermute | solution.py:368
  5.0 154.1 %collective-permute-start = (bf16[1536,768]{1,0:T(8,128)(2,1)}, bf16[1536,768]{1,0:T(8,128)(2,1)}, u32[]{:S(2)}, u32[]{:S(2)}) collective-permute-start(bf16[1536,768]{1,0:T(8,128)(2,1)} %get-tuple-element.49.refs_3_), channel_id=1, source_target_pairs={{0,240},{16,224},{48,192},{64,176},{96,144},{112,128},{128,112},{1... | collective-permute-start | bytes 7077896 | tf_op jit(solution)/shard_map/ppermute | solution.py:375
  7.5 89.1 %collective-permute-start.1 = (bf16[1280,768]{1,0:T(8,128)(2,1)}, bf16[1280,768]{1,0:T(8,128)(2,1)}, u32[]{:S(2)}, u32[]{:S(2)}) collective-permute-start(bf16[1280,768]{1,0:T(8,128)(2,1)} %get-tuple-element.50), channel_id=1, source_target_pairs={{32,208},{80,160},{160,80},{33,209},{81,161},{161,81},{34,210},{82... | collective-permute-start | bytes 5898248 | tf_op jit(solution)/shard_map/ppermute | solution.py:376
  9.5 3.6 %copy-start.1 = (s32[16]{0:T(128)S(1)}, s32[16]{0:T(128)}, u32[]{:S(2)}) copy-start(s32[16]{0:T(128)} %slot_ref.1) | copy-start | bytes 196
  9.5 81.2 %collective-permute-start.2 = (bf16[256,768]{1,0:T(8,128)(2,1)}, bf16[256,768]{1,0:T(8,128)(2,1)S(1)}, u32[]{:S(2)}, u32[]{:S(2)}) collective-permute-start(bf16[256,768]{1,0:T(8,128)(2,1)} %get-tuple-element.51), channel_id=1, source_target_pairs={{80,64},{160,176},{32,48},{81,65},{161,177},{33,49},{82,66},{162,1... | collective-permute-start | bytes 1179656 | tf_op jit(solution)/shard_map/ppermute | solution.py:373
  13.1 34.5 %all-to-all-start = ((bf16[8,3,64,768]{3,2,1,0:T(8,128)(2,1)}), bf16[8,3,64,768]{3,2,1,0:T(8,128)(2,1)S(1)}, u32[]{:S(2)}, u32[]{:S(2)}) async-start(bf16[8,3,64,768]{3,2,1,0:T(8,128)(2,1)} %get-tuple-element.118), calls=%async_computation | async-start | bytes 4718592 | tf_op jit(solution)/shard_map/while/body/all_to_all | solution.py:351
  57.3 0.9 copy-start.2
  60.2 25.1 %all-to-all-start.1 = ((bf16[8,2,64,768]{3,2,1,0:T(8,128)(2,1)}), bf16[8,2,64,768]{3,2,1,0:T(8,128)(2,1)S(1)}, u32[]{:S(2)}, u32[]{:S(2)}) async-start(bf16[8,2,64,768]{3,2,1,0:T(8,128)(2,1)} %get-tuple-element.130), calls=%async_computation.1 | async-start | bytes 3145728 | tf_op jit(solution)/shard_map/while/body/all_to_all | solution.py:351
  87.7 82.4 %collective-permute-start.5 = (bf16[8,64,768]{2,1,0:T(8,128)(2,1)S(1)}, bf16[8,64,768]{2,1,0:T(8,128)(2,1)S(1)}, u32[]{:S(2)}, u32[]{:S(2)}) collective-permute-start(bf16[8,64,768]{2,1,0:T(8,128)(2,1)S(1)} %slice_bitcast_fusion), channel_id=1, source_target_pairs={{0,16},{16,32},{32,48},{48,64},{64,80},{80,96},{96,112},{112,128},... | collective-permute-start | bytes 2359304 | tf_op jit(solution)/shard_map/ppermute | solution.py:381
  90.6 5.9 %collective-permute-start.3 = (bf16[256,768]{1,0:T(8,128)(2,1)S(1)}, bf16[256,768]{1,0:T(8,128)(2,1)S(1)}, u32[]{:S(2)}, u32[]{:S(2)}) collective-permute-start(bf16[256,768]{1,0:T(8,128)(2,1)S(1)} %collective-permute-done.2), channel_id=1, source_target_pairs={{64,160},{176,80},{48,208},{65,161},{177,81},{49,209},{66,162},{17... | collective-permute-start | bytes 1179656 | tf_op jit(solution)/shard_map/ppermute | solution.py:374
  91.3 128.1 %collective-permute-start.7 = (bf16[1408,768]{1,0:T(8,128)(2,1)}, bf16[1408,768]{1,0:T(8,128)(2,1)}, u32[]{:S(2)}, u32[]{:S(2)}) collective-permute-start(bf16[1408,768]{1,0:T(8,128)(2,1)} %get-tuple-element.60), channel_id=1, source_target_pairs={{0,240},{16,224},{32,208},{48,192},{64,176},{80,160},{96,144},{112... | collective-permute-start | bytes 6488072 | tf_op jit(solution)/shard_map/ppermute | solution.py:384
  96.6 62.5 %copy-start = (bf16[256,768]{1,0:T(8,128)(2,1)}, bf16[256,768]{1,0:T(8,128)(2,1)S(1)}, u32[]{:S(2)}) copy-start(bf16[256,768]{1,0:T(8,128)(2,1)S(1)} %collective-permute-done.3.e_ref) | copy-start | bytes 1179652
  170.1 4.7 %copy-start.3 = (bf16[128,768]{1,0:T(8,128)(2,1)S(1)}, bf16[128,768]{1,0:T(8,128)(2,1)}, u32[]{:S(2)}) copy-start(bf16[128,768]{1,0:T(8,128)(2,1)} %get-tuple-element.59) | copy-start | bytes 589828
  170.1 34.7 %all-to-all-start.2 = ((bf16[8,3,64,768]{3,2,1,0:T(8,128)(2,1)}), bf16[8,3,64,768]{3,2,1,0:T(8,128)(2,1)S(1)}, u32[]{:S(2)}, u32[]{:S(2)}) async-start(bf16[8,3,64,768]{3,2,1,0:T(8,128)(2,1)} %backward_core.1), calls=%async_computation.2 | async-start | bytes 4718592 | tf_op jit(solution)/shard_map/all_to_all | solution.py:351
  174.7 47.4 %collective-permute-start.6 = (bf16[128,768]{1,0:T(8,128)(2,1)S(1)}, bf16[128,768]{1,0:T(8,128)(2,1)S(1)}, u32[]{:S(2)}, u32[]{:S(2)}) collective-permute-start(bf16[128,768]{1,0:T(8,128)(2,1)S(1)} %copy-done.3), channel_id=1, source_target_pairs={{0,240},{16,224},{32,208},{48,192},{64,176},{80,160},{96,144},{112... | collective-permute-start | bytes 589832 | tf_op jit(solution)/shard_map/ppermute | solution.py:385
